TPU v7x, 32 devices: a whole 2x2x4 slice. The times are simulated.
32 devices in a mesh: groups: 2 (over x), frame: 16 (over z, y, core).
Axes of the slice: x: 2, y: 2, z: 4, core: 2. Of those that a mesh axis runs over, the one named last changes fastest.
Arguments:
- video_qkv: bfloat16 [3, 32, 128, 1536], P(None, ('groups', 'frame')), parts along dimension 1, may hold values from -8 to 8
- text_qkv: bfloat16 [3, 512, 1536], P(None, ('groups', 'frame')), parts along dimension 1, may hold values from -8 to 8
- head_kind: int32 [24], P('groups'), parts along dimension 0, may hold values from 0 to 1, as said below
- text_len: int32 [2], P('groups'), parts along dimension 0, may hold values from 64 to 256
Outputs:
- video_out: bfloat16 [32, 128, 1536], P(('groups', 'frame')), parts along dimension 0
- text_out: bfloat16 [512, 1536], P(('groups', 'frame')), parts along dimension 0
There are 2 independent parts, one for each index of `groups`. A program takes and returns all parts, laid end to end along the dimension named above; each array names one. Nothing has to cross between parts.
Inputs may be any that keep to these rules, and one draw needn't show every extreme that they name: `head_kind`: exactly 6 of the 12 entries are 1.
All inputs are finite; a program needn't handle non-finite values.
Results may differ from a plain program's by a relative error of at most 0.009.
Values may be sent and summed in bfloat16 or wider, within the bound.
No kernel may reach another device: no remote copies, remote signals or barrier semaphores. Data moves between devices by JAX's collectives and lax.ppermute only.
A program may use at most 448 MiB of HBM per device.

v0:
```python
import jax
import jax.numpy as jnp
from jax import lax
from jax.sharding import PartitionSpec as P

masked_score = -1e30


def body(video_qkv, text_qkv, head_kind, text_len):
    head_count = head_kind.shape[0]
    head_width = video_qkv.shape[-1]
    head_dim = head_width // head_count
    positions = video_qkv.shape[2]
    shard_text = text_qkv.shape[1]
    score_scale = head_dim ** (-0.5)
    device_rank = lax.axis_index("frame")
    local_video = video_qkv.reshape(3, 1, positions, head_count, head_dim)
    gathered = lax.all_gather(text_qkv, "frame", axis=1, tiled=True)
    text_total = gathered.shape[1]
    all_text = gathered.reshape(3, text_total, head_count, head_dim)
    text_valid = jnp.arange(text_total) < text_len[0]
    spatial_heads = jnp.nonzero(head_kind == 0, size=head_count - head_count // 2)[0].astype(
        jnp.int32
    )
    temporal_heads = jnp.nonzero(head_kind == 1, size=head_count // 2)[0].astype(jnp.int32)
    own_frame = jnp.take(local_video[:, 0], spatial_heads, axis=2)
    text_spatial = jnp.take(all_text[1:], spatial_heads, axis=2)
    joint_keys = jnp.concatenate([own_frame[1], text_spatial[0]], axis=0)
    joint_values = jnp.concatenate([own_frame[2], text_spatial[1]], axis=0)
    joint_valid = jnp.concatenate([jnp.ones((positions,), bool), text_valid])
    spatial_scores = (
        jnp.einsum("phd,khd->hpk", own_frame[0], joint_keys, preferred_element_type=jnp.float32)
        * score_scale
    )
    spatial_scores = jnp.where(joint_valid, spatial_scores, masked_score)
    row_max = spatial_scores.max(-1, keepdims=True)
    spatial_exp = jnp.exp(spatial_scores - row_max)
    totals = spatial_exp.sum(-1)
    summed = jnp.einsum(
        "hpk,khd->phd",
        spatial_exp.astype(jnp.bfloat16),
        joint_values,
        preferred_element_type=jnp.float32,
    )
    spatial_result = (summed / totals.T[..., None]).astype(jnp.bfloat16)
    selected = jnp.take(local_video, temporal_heads, axis=3)
    block = lax.all_to_all(selected, "frame", split_axis=2, concat_axis=1, tiled=True)
    scores = (
        jnp.einsum("fphd,gphd->phfg", block[0], block[1], preferred_element_type=jnp.float32)
        * score_scale
    )
    block_max = scores.max(-1, keepdims=True)
    exps = jnp.exp(scores - block_max)
    block_totals = exps.sum(-1)
    block_sum = jnp.einsum(
        "phfg,gphd->fphd", exps.astype(jnp.bfloat16), block[2], preferred_element_type=jnp.float32
    )
    result = (block_sum / jnp.transpose(block_totals, (2, 0, 1))[..., None]).astype(jnp.bfloat16)
    temporal_result = lax.all_to_all(result, "frame", split_axis=0, concat_axis=1, tiled=True)[0]
    joined = jnp.concatenate([spatial_result, temporal_result], axis=1)
    order = jnp.concatenate([spatial_heads, temporal_heads])
    inverse = jnp.argsort(order)
    video_out = jnp.take(joined, inverse, axis=1).reshape(1, positions, head_width)
    text_queries = all_text[0]
    own_text = text_qkv.reshape(3, shard_text, head_count, head_dim)
    own_valid = device_rank * shard_text + jnp.arange(shard_text) < text_len[0]
    local_keys = jnp.concatenate([local_video[1, 0], own_text[1]], axis=0)
    local_values = jnp.concatenate([local_video[2, 0], own_text[2]], axis=0)
    local_valid = jnp.concatenate([jnp.ones((positions,), bool), own_valid])
    query_scores = (
        jnp.einsum("thd,khd->thk", text_queries, local_keys, preferred_element_type=jnp.float32)
        * score_scale
    )
    query_scores = jnp.where(local_valid, query_scores, masked_score)
    local_max = query_scores.max(-1)
    global_max = lax.pmax(local_max, "frame")
    query_exp = jnp.exp(query_scores - global_max[..., None])
    query_totals = query_exp.sum(-1)
    query_sums = jnp.einsum(
        "thk,khd->thd",
        query_exp.astype(jnp.bfloat16),
        local_values,
        preferred_element_type=jnp.float32,
    )
    query_totals, query_sums = (query_totals, query_sums)
    query_sums, query_totals = (
        lax.psum_scatter(query_sums, "frame", scatter_dimension=0, tiled=True),
        lax.psum_scatter(query_totals, "frame", scatter_dimension=0, tiled=True),
    )
    text_out = (
        (query_sums / query_totals[..., None]).astype(jnp.bfloat16).reshape(shard_text, head_width)
    )
    return (video_out, text_out)


def solution(mesh):
    in_specs = (
        P(None, ("groups", "frame"), None, None),
        P(None, ("groups", "frame"), None),
        P("groups"),
        P("groups"),
    )
    out_specs = (P(("groups", "frame"), None, None), P(("groups", "frame"), None))
    return jax.shard_map(body, mesh=mesh, in_specs=in_specs, out_specs=out_specs, check_vma=False)
```

profile of v0, /device:TPU:0, one launch (start us, length us, event | category | flops | bytes accessed | tf_op | source)
XLA Modules:
  0.0 248.0 jit_solution(8122713932160356328)
XLA Ops:
  7.2 0.7 all-gather.2.cloned.1.call-update
  7.9 0.7 fusion.43
  8.9 0.6 scatter_custom_fusion
  9.6 0.6 scatter_custom_fusion.1
  10.6 1.7 copy.94
  12.3 0.7 copy.95
  13.0 0.6 fusion.44
  13.7 1.3 fusion.41
  15.0 0.7 gather_fusion.2
  15.7 1.8 compare_and_fusion
  17.7 1.4 copy.102
  19.1 7.4 %all-to-all-start = ((bf16[3,1,128,6,128]{4,0,3,1,2:T(4,128)(2,1)}), bf16[3,1,128,6,128]{4,0,3,1,2:T(4,128)(2,1)S(1)}, u32[]{:S(2)}, u32[]{:S(2)}) async-start(bf16[3,1,128,6,128]{4,0,3,1,2:T(4,128)(2,1)} %copy.102), calls=%async_computation | async-start | bytes 1572864 | tf_op jit(solution)/shard_map/all_to_all | solution.py:47
  27.2 0.6 copy.116
  27.9 0.6 copy.119
  28.6 0.8 fusion.57
  29.4 1.2 copy.133
  30.6 0.9 copy.115
  32.0 0.7 gather_fusion
  32.8 1.2 sort.17
  34.1 0.9 fusion.23
  35.1 11.1 %all-to-all-done = bf16[3,1,128,6,128]{4,0,3,1,2:T(4,128)(2,1)S(1)} async-done(((bf16[3,1,128,6,128]{4,0,3,1,2:T(4,128)(2,1)}), bf16[3,1,128,6,128]{4,0,3,1,2:T(4,128)(2,1)S(1)}, u32[]{:S(2)}, u32[]{:S(2)}) %all-to-all-start) | async-done | bytes 589856 | tf_op jit(solution)/shard_map/all_to_all | solution.py:47
  46.1 0.8 fusion.58
  47.0 0.7 copy.160
  48.1 0.7 copy-done.2
  48.9 11.8 %all-gather.2.cloned.1.call-done = bf16[3,256,1536]{2,1,0:T(8,128)(2,1)} async-done(((bf16[3,16,1536]{2,1,0:T(8,128)(2,1)}), bf16[3,256,1536]{2,1,0:T(8,128)(2,1)}) %all-gather.2.cloned.1.call-update) | async-done | bytes 2359312 | tf_op jit(solution)/shard_map/all_gather | solution.py:18
  60.7 1.1 slice-done
  62.6 59.1 %pmax.7 = f32[256,12]{0,1:T(8,128)S(1)} all-reduce(f32[256,12]{0,1:T(8,128)S(1)} %get-tuple-element.31), channel_id=1, replica_groups=mesh['groups'=2,'frame'=16] {'frame'}, use_global_device_ids=true, to_apply=%region_14.15 | all-reduce | flops 3072 | bytes 24576 | tf_op jit(solution)/shard_map/pmax | solution.py:76
  122.2 0.8 copy.127
  123.0 1.7 convolution_bitcast_fusion
  124.7 1.9 copy.122
  126.7 1.0 copy-done.3
  128.0 0.8 copy.110
  128.7 3.5 %all-to-all-start.1 = ((bf16[16,8,6,128]{3,1,2,0:T(8,128)(2,1)}), bf16[16,8,6,128]{3,1,2,0:T(8,128)(2,1)S(1)}, u32[]{:S(2)}, u32[]{:S(2)}) async-start(bf16[16,8,6,128]{3,1,2,0:T(8,128)(2,1)} %copy.110), calls=%async_computation.1 | async-start | bytes 393216 | tf_op jit(solution)/shard_map/all_to_all | solution.py:59
  132.8 0.7 slice_bitcast_fusion.5
  133.5 7.7 %all-to-all-done.1 = bf16[16,8,6,128]{3,1,2,0:T(8,128)(2,1)S(1)} async-done(((bf16[16,8,6,128]{3,1,2,0:T(8,128)(2,1)}), bf16[16,8,6,128]{3,1,2,0:T(8,128)(2,1)S(1)}, u32[]{:S(2)}, u32[]{:S(2)}) %all-to-all-start.1) | async-done | bytes 196640 | tf_op jit(solution)/shard_map/all_to_all | solution.py:59
  141.4 1.4 slice-done.1
  142.8 0.7 copy.129
  143.5 0.9 copy.98
  144.4 0.7 gather_fusion.1
  145.4 0.7 copy-done.7
  146.1 1.4 fusion.61
  147.9 0.5 fusion.6
  148.5 0.6 gather_fusion.3
  149.3 0.8 broadcast_select_fusion
  150.1 25.4 %reduce-scatter.7.cloned.1.call-done = f32[16,12]{1,0:T(8,128)} async-done(((f32[256,12]{1,0:T(8,128)}), f32[16,12]{1,0:T(8,128)}) %reduce-scatter.7.cloned.1.call-update) | async-done | bytes 784 | tf_op jit(solution)/shard_map/reduce_scatter | solution.py:88
  175.4 64.4 %reduce-scatter.5.cloned.1.call-done = f32[16,12,128]{2,1,0:T(8,128)} async-done(((f32[256,12,128]{2,1,0:T(8,128)}), f32[16,12,128]{2,1,0:T(8,128)}) %reduce-scatter.5.cloned.1.call-update) | async-done | bytes 98320 | tf_op jit(solution)/shard_map/reduce_scatter | solution.py:87
  239.8 1.0 divide_convert_fusion
  240.8 0.6 copy.162
  (70 shorter events, 5.3 us)
Async XLA Ops:
  7.2 53.6 %all-gather.2.cloned.1.call-start = ((), (), s32[]{:S(2)}) async-start(), calls=%async_computation.4 | async-start | bytes 2506752 | tf_op jit(solution)/shard_map/all_gather | solution.py:18
  12.3 0.8 copy-start.11
  17.6 9.5 %copy-start.4 = (bf16[3,16,1536]{2,1,0:T(8,128)(2,1)S(1)}, bf16[3,16,1536]{2,1,0:T(8,128)(2,1)}, u32[]{:S(2)}) copy-start(bf16[3,16,1536]{2,1,0:T(8,128)(2,1)} %param.5) | copy-start | bytes 442372
  17.6 10.9 %copy-start = (bf16[3,1,128,1536]{3,2,1,0:T(8,128)(2,1)S(1)}, bf16[3,1,128,1536]{3,2,1,0:T(8,128)(2,1)}, u32[]{:S(2)}) copy-start(bf16[3,1,128,1536]{3,2,1,0:T(8,128)(2,1)} %param.4) | copy-start | bytes 3538948
  19.1 27.1 %all-to-all-start = ((bf16[3,1,128,6,128]{4,0,3,1,2:T(4,128)(2,1)}), bf16[3,1,128,6,128]{4,0,3,1,2:T(4,128)(2,1)S(1)}, u32[]{:S(2)}, u32[]{:S(2)}) async-start(bf16[3,1,128,6,128]{4,0,3,1,2:T(4,128)(2,1)} %copy.102), calls=%async_computation | async-start | bytes 1572864 | tf_op jit(solution)/shard_map/all_to_all | solution.py:47
  26.4 149.0 %reduce-scatter.7.cloned.1.call-start = ((), (), s32[]{:S(2)}) async-start(), calls=%async_computation.6 | async-start | bytes 139264 | tf_op jit(solution)/shard_map/reduce_scatter | solution.py:88
  31.5 1.2 copy-start.9
  31.5 1.2 copy-start.10
  48.0 0.7 copy-start.2
  48.9 13.2 %copy-start.8 = (bf16[16,12,128]{2,0,1:T(8,128)(2,1)S(1)}, bf16[16,12,128]{2,0,1:T(8,128)(2,1)}, u32[]{:S(2)}) copy-start(bf16[16,12,128]{2,0,1:T(8,128)(2,1)} %copy.119) | copy-start | bytes 147460
  60.7 1.1 slice-start
  62.6 60.4 %copy-start.5 = (bf16[16,12,128]{2,0,1:T(8,128)(2,1)S(1)}, bf16[16,12,128]{2,0,1:T(8,128)(2,1)}, u32[]{:S(2)}) copy-start(bf16[16,12,128]{2,0,1:T(8,128)(2,1)} %copy.116) | copy-start | bytes 147460
  122.9 116.9 %reduce-scatter.5.cloned.1.call-start = ((), (), s32[]{:S(2)}) async-start(), calls=%async_computation.5 | async-start | bytes 2228224 | tf_op jit(solution)/shard_map/reduce_scatter | solution.py:87
  126.6 1.0 copy-start.3
  126.6 1.0 copy-start.6
  126.6 6.1 %copy-start.1 = (bf16[3,128,6,128]{3,1,2,0:T(8,128)(2,1)S(1)}, bf16[3,128,6,128]{3,1,2,0:T(8,128)(2,1)}, u32[]{:S(2)}) copy-start(bf16[3,128,6,128]{3,1,2,0:T(8,128)(2,1)} %fusion.23) | copy-start | bytes 1769476
  128.7 12.5 %all-to-all-start.1 = ((bf16[16,8,6,128]{3,1,2,0:T(8,128)(2,1)}), bf16[16,8,6,128]{3,1,2,0:T(8,128)(2,1)S(1)}, u32[]{:S(2)}, u32[]{:S(2)}) async-start(bf16[16,8,6,128]{3,1,2,0:T(8,128)(2,1)} %copy.110), calls=%async_computation.1 | async-start | bytes 393216 | tf_op jit(solution)/shard_map/all_to_all | solution.py:59
  141.4 1.4 slice-start.1
  145.1 0.9 copy-start.7
  145.2 0.9 copy-start.12
Sparse Core Ops, SparseCore 0:
  10.3 50.3 all-gather.1
  123.1 52.3 reduce-scatter.6
  179.2 60.5 reduce-scatter.4
where the time goes:
time: 249 us; the launch traced here: 248 us
  waiting for transfers between devices  121 us (49%)
  blocking collectives  59.1 us (24%)
  local copies, waits for them, and re-layouts  25.6 us (10%)
  between operations  14.8 us (6%)
  other arithmetic  11.8 us (5%)
  starting transfers between devices  11 us (4%)
  matrix products  4.6 us (2%)
    reduce_scatter x1, waiting for transfers between devices, body(): lax.psum_scatter(query_sums, 'frame', scatter_dimension=0, tiled=True)  64.4 us
    pmax x1, blocking collectives, body(): global_max = lax.pmax(local_max, 'frame')  59.1 us
    reduce_scatter x1, waiting for transfers between devices, body(): lax.psum_scatter(query_totals, 'frame', scatter_dimension=0, tiled=True)  25.4 us
    all_gather x1, waiting for transfers between devices, body(): gathered = lax.all_gather(text_qkv, 'frame', axis=1, tiled=True)  11.8 us
    all_to_all x1, waiting for transfers between devices, body(): lax.all_to_all(selected, 'frame', split_axis=2, concat_axis=1, tiled=True)  11.1 us
    unnamed x36, local copies, waits for them, and re-layouts  8.76 us
    all_to_all x1, waiting for transfers between devices, body(): lax.all_to_all(result, 'frame', split_axis=0, concat_axis=1, tiled=True)[0]  7.7 us
    all_to_all x1, starting transfers between devices, body(): lax.all_to_all(selected, 'frame', split_axis=2, concat_axis=1, tiled=True)  7.39 us
  transfers between devices with their start and end apart: 5, of which 5 were waited for; matrix products, arithmetic and copies ran while one was open for 13% of the time, Pallas kernels for 0%

commit v1 on v0

v1 whole, which is shorter than its diff:
```python
import functools

import jax
import jax.numpy as jnp
from jax import lax
from jax.experimental import pallas as pl
from jax.experimental.pallas import tpu as pltpu
from jax.sharding import PartitionSpec as P

masked_score = -1e30
lanes = 128


def contract_last(a, b):
    return lax.dot_general(a, b, (((1,), (1,)), ((), ())), preferred_element_type=jnp.float32)


def head_lanes(head):
    if isinstance(head, int):
        return pl.ds(head * lanes, lanes)
    return pl.ds(pl.multiple_of(head * lanes, lanes), lanes)


def list_heads(kind_ref, list_ref, head_count):
    ones = jnp.int32(0)
    for head in range(head_count):
        kind = kind_ref[head]
        slot = jnp.where(kind == 1, head_count + ones, head - ones)
        list_ref[slot] = jnp.int32(head)
        ones = ones + kind


def pack_kernel(head_count, kind_ref, video_ref, text_ref, temporal_ref, keys_ref, list_ref):
    list_heads(kind_ref, list_ref, head_count)
    half = head_count // 2
    for slot in range(half):
        head = list_ref[head_count + slot]
        for part in range(3):
            temporal_ref[:, pl.ds((part * half + slot) * lanes, lanes)] = video_ref[
                part, :, head_lanes(head)
            ]
    for slot in range(half):
        head = list_ref[slot]
        for part in range(2):
            keys_ref[:, pl.ds((part * half + slot) * lanes, lanes)] = text_ref[
                part + 1, :, head_lanes(head)
            ]


def temporal_kernel(half, stride, scale, block_ref, out_ref):
    rows = block_ref.shape[0]
    row = lax.broadcasted_iota(jnp.int32, (rows, rows), 0)
    column = lax.broadcasted_iota(jnp.int32, (rows, rows), 1)
    same = lax.rem(row, stride) == lax.rem(column, stride)
    for slot in range(half):
        query, key, value = (
            block_ref[:, pl.ds((part * half + slot) * lanes, lanes)] for part in range(3)
        )
        scores = jnp.where(same, contract_last(query, key) * scale, masked_score)
        exps = jnp.exp(scores - scores.max(-1, keepdims=True))
        total = exps.sum(-1, keepdims=True)
        summed = jnp.dot(exps.astype(jnp.bfloat16), value, preferred_element_type=jnp.float32)
        out_ref[:, pl.ds(slot * lanes, lanes)] = (summed / total).astype(jnp.bfloat16)


def spatial_kernel(
    head_count, shard, relative, scale, kind_ref, length_ref, video_ref, near_ref, far_ref, out_ref, list_ref
):
    list_heads(kind_ref, list_ref, head_count)
    half = head_count // 2
    positions = video_ref.shape[1]
    near = near_ref.shape[0]
    text_total = near + far_ref.shape[0]
    index = lax.broadcasted_iota(jnp.int32, (positions, text_total), 1)
    if relative:
        block = index // shard
        differs = (block & 3) * 4 + ((block >> 2) & 1) * 2 + ((block >> 3) & 1)
        index = (lax.axis_index("frame") ^ differs) * shard + lax.rem(index, shard)
    valid = index < length_ref[0]
    for slot in range(half):
        head = list_ref[slot]
        query, key, value = (video_ref[part, :, head_lanes(head)] for part in range(3))
        text_key, text_value = (
            jnp.concatenate(
                [
                    ref[:, pl.ds((part * half + slot) * lanes, lanes)]
                    for ref in (near_ref, far_ref)
                ],
                axis=0,
            )
            for part in range(2)
        )
        own_scores = contract_last(query, key) * scale
        text_scores = jnp.where(valid, contract_last(query, text_key) * scale, masked_score)
        row_max = jnp.maximum(
            own_scores.max(-1, keepdims=True), text_scores.max(-1, keepdims=True)
        )
        own_exp = jnp.exp(own_scores - row_max)
        text_exp = jnp.exp(text_scores - row_max)
        total = own_exp.sum(-1, keepdims=True) + text_exp.sum(-1, keepdims=True)
        summed = jnp.dot(own_exp.astype(jnp.bfloat16), value, preferred_element_type=jnp.float32)
        summed = summed + jnp.dot(
            text_exp.astype(jnp.bfloat16), text_value, preferred_element_type=jnp.float32
        )
        out_ref[:, pl.ds(slot * lanes, lanes)] = (summed / total).astype(jnp.bfloat16)


def text_kernel(
    head_count, shard, scale, length_ref, video_ref, other_ref, text_ref, other_text_ref, *refs
):
    query_refs, out_ref = refs[:-1], refs[-1]
    rows = out_ref.shape[0]
    me = lax.axis_index("frame")
    index = lax.broadcasted_iota(jnp.int32, (rows, shard), 1)
    valid = [index + owner * shard < length_ref[0] for owner in (me, me ^ 1)]
    lane = lax.broadcasted_iota(jnp.int32, (rows, lanes), 1)
    stats = jnp.zeros((rows, lanes), jnp.float32)
    for head in range(head_count):
        span = head_lanes(head)
        query = jnp.concatenate([ref[:, span] for ref in query_refs], axis=0)
        keys = [ref[1, :, span] for ref in (video_ref, other_ref, text_ref, other_text_ref)]
        values = [ref[2, :, span] for ref in (video_ref, other_ref, text_ref, other_text_ref)]
        scores = [contract_last(query, key) * scale for key in keys]
        scores = scores[:2] + [
            jnp.where(ok, score, masked_score) for ok, score in zip(valid, scores[2:])
        ]
        row_max = functools.reduce(
            jnp.maximum, [score.max(-1, keepdims=True) for score in scores]
        )
        point = row_max.astype(jnp.bfloat16).astype(jnp.float32)
        exps = [jnp.exp(score - point) for score in scores]
        total = sum(e.sum(-1, keepdims=True) for e in exps)
        summed = sum(
            jnp.dot(e.astype(jnp.bfloat16), value, preferred_element_type=jnp.float32)
            for e, value in zip(exps, values)
        )
        out_ref[:, span] = summed.astype(jnp.bfloat16)
        high = total.astype(jnp.bfloat16).astype(jnp.float32)
        for place, column in enumerate((point, high, total - high)):
            stats = jnp.where(lane == 3 * head + place, column, stats)
    out_ref[:, head_lanes(head_count)] = stats.astype(jnp.bfloat16)


def merge(head_count, blocks):
    stats = [block(head_count).astype(jnp.float32) for block in blocks]
    merged = []
    for head in range(head_count):
        points = [s[:, 3 * head : 3 * head + 1] for s in stats]
        totals = [s[:, 3 * head + 1 : 3 * head + 2] + s[:, 3 * head + 2 : 3 * head + 3] for s in stats]
        point = functools.reduce(jnp.maximum, points)
        factors = [jnp.exp(p - point) for p in points]
        total = sum(f * t for f, t in zip(factors, totals))
        summed = sum(f * block(head).astype(jnp.float32) for f, block in zip(factors, blocks))
        merged.append((point, total, summed))
    return merged


def reader(ref):
    return lambda head: ref[:, head_lanes(head)]


def merge_kernel(head_count, *refs):
    out_ref = refs[-1]
    lane = lax.broadcasted_iota(jnp.int32, (out_ref.shape[0], lanes), 1)
    stats = jnp.zeros(lane.shape, jnp.float32)
    for head, (point, total, summed) in enumerate(
        merge(head_count, [reader(ref) for ref in refs[:-1]])
    ):
        out_ref[:, head_lanes(head)] = summed.astype(jnp.bfloat16)
        high = total.astype(jnp.bfloat16).astype(jnp.float32)
        for place, column in enumerate((point, high, total - high)):
            stats = jnp.where(lane == 3 * head + place, column, stats)
    out_ref[:, head_lanes(head_count)] = stats.astype(jnp.bfloat16)


def finish_kernel(head_count, *refs):
    out_ref = refs[-1]
    for head, (_, total, summed) in enumerate(
        merge(head_count, [reader(ref) for ref in refs[:-1]])
    ):
        out_ref[:, head_lanes(head)] = (summed / total).astype(jnp.bfloat16)


def join_kernel(head_count, kind_ref, spatial_ref, temporal_ref, out_ref, list_ref):
    list_heads(kind_ref, list_ref, head_count)
    half = head_count // 2
    for kind, ref in enumerate((spatial_ref, temporal_ref)):
        for slot in range(half):
            out_ref[:, head_lanes(list_ref[kind * head_count + slot])] = ref[
                :, pl.ds(slot * lanes, lanes)
            ]


def call(kernel, name, out, scalars, arrays, list_size=0, flops=0):
    shapes = out if isinstance(out, list) else [out]
    outs = tuple(jax.ShapeDtypeStruct(shape, jnp.bfloat16) for shape in shapes)
    moved = sum(a.size * 2 for a in arrays) + sum(o.size * 2 for o in outs)
    result = pl.pallas_call(
        kernel,
        out_shape=outs,
        in_specs=[pl.BlockSpec(memory_space=pltpu.SMEM)] * len(scalars)
        + [pl.BlockSpec(memory_space=pltpu.VMEM)] * len(arrays),
        out_specs=tuple(pl.BlockSpec(memory_space=pltpu.VMEM) for _ in outs),
        scratch_shapes=[pltpu.SMEM((list_size,), jnp.int32)] if list_size else [],
        compiler_params=pltpu.CompilerParams(vmem_limit_bytes=24 * 2**20),
        cost_estimate=pl.CostEstimate(flops=flops, bytes_accessed=moved, transcendentals=0),
        name=name,
    )(*scalars, *arrays)
    return result if isinstance(out, list) else result[0]


def body(devices, video_qkv, text_qkv, head_kind, text_len):
    head_count = head_kind.shape[0]
    half = head_count // 2
    width = video_qkv.shape[-1]
    positions = video_qkv.shape[2]
    shard = text_qkv.shape[1]
    scale = (width // head_count) ** -0.5
    video = video_qkv.reshape(3, positions, width)
    relative = devices == 16

    def swap(array, bits):
        return lax.ppermute(array, "frame", [(i, i ^ bits) for i in range(devices)])

    temporal_block, spatial_keys = call(
        functools.partial(pack_kernel, head_count),
        "pack",
        [(positions, 3 * half * lanes), (shard, 2 * half * lanes)],
        [head_kind],
        [video, text_qkv],
        list_size=2 * head_count,
    )
    block = lax.all_to_all(temporal_block, "frame", split_axis=0, concat_axis=0, tiled=True)

    other_video = swap(video, 1)
    other_text = swap(text_qkv, 1)

    def attend(queries):
        rows = sum(q.shape[0] for q in queries)
        return call(
            functools.partial(text_kernel, head_count, shard, scale),
            "text",
            (rows, width + lanes),
            [text_len],
            [video, other_video, text_qkv, other_text, *queries],
            flops=8 * rows * width * (positions + shard),
        )

    queries = text_qkv[0]
    if relative:
        column = [queries] + [swap(queries, 4 * step) for step in (1, 2, 3)]
        across = swap(jnp.concatenate(column, axis=0), 2)
        sent = swap(attend([across]), 2)
        kept = attend(column)
        joined = call(
            functools.partial(merge_kernel, head_count), "merge", kept.shape, [], [kept, sent]
        )
        pieces = [joined[:shard]] + [
            swap(joined[step * shard : (step + 1) * shard], 4 * step) for step in (1, 2, 3)
        ]
        text_out = call(
            functools.partial(finish_kernel, head_count), "finish", (shard, width), [], pieces
        )
        keys_column = jnp.concatenate(
            [spatial_keys] + [swap(spatial_keys, 4 * step) for step in (1, 2, 3)], axis=0
        )
        near_keys = jnp.concatenate([keys_column, swap(keys_column, 2)], axis=0)
        far_keys = swap(near_keys, 1)
    else:
        side = [[2 * chip + core for chip in range(devices // 2)] for core in range(2)]
        gathered = lax.all_gather(queries, "frame", axis=0, tiled=True, axis_index_groups=side)
        partial_sums = lax.all_to_all(
            attend([gathered]), "frame", 0, 0, tiled=True, axis_index_groups=side
        ).reshape(devices // 2, shard, width + lanes)
        blocks = [
            lambda head, i=i: partial_sums[i, :, head * lanes : (head + 1) * lanes]
            for i in range(devices // 2)
        ]
        text_out = jnp.concatenate(
            [summed / total for _, total, summed in merge(head_count, blocks)], axis=1
        ).astype(jnp.bfloat16)
        all_keys = lax.all_gather(spatial_keys, "frame", axis=0, tiled=True)
        near_keys, far_keys = jnp.split(all_keys, 2, axis=0)

    spatial = call(
        functools.partial(spatial_kernel, head_count, shard, relative, scale),
        "spatial",
        (positions, half * lanes),
        [head_kind, text_len],
        [video, near_keys, far_keys],
        list_size=2 * head_count,
        flops=4 * positions * half * lanes * (positions + devices * shard),
    )
    result = call(
        functools.partial(temporal_kernel, half, positions // devices, scale),
        "temporal",
        (positions, half * lanes),
        [],
        [block],
        flops=4 * positions * half * lanes * positions,
    )
    temporal = lax.all_to_all(result, "frame", split_axis=0, concat_axis=0, tiled=True)
    video_out = call(
        functools.partial(join_kernel, head_count),
        "join",
        (positions, width),
        [head_kind],
        [spatial, temporal],
        list_size=2 * head_count,
    )
    return video_out.reshape(1, positions, width), text_out


def solution(mesh):
    in_specs = (
        P(None, ("groups", "frame"), None, None),
        P(None, ("groups", "frame"), None),
        P("groups"),
        P("groups"),
    )
    out_specs = (P(("groups", "frame"), None, None), P(("groups", "frame"), None))
    return jax.shard_map(
        functools.partial(body, mesh.shape["frame"]),
        mesh=mesh,
        in_specs=in_specs,
        out_specs=out_specs,
        check_vma=False,
    )
```

time: 249 us -> 72.3 us (0.29)
  waiting for transfers between devices: 121 us -> 15.9 us
  blocking collectives: 59.1 us -> 0 us
  starting transfers between devices: 11 us -> 28.9 us
  local copies, waits for them, and re-layouts: 25.6 us -> 9.25 us
  Pallas kernels: 0 us -> 16.2 us
  between operations: 14.8 us -> 1.45 us
  other arithmetic: 11.8 us -> 0.03 us
  matrix products: 4.6 us -> 0 us
    reduce_scatter x2 -> x0, waiting for transfers between devices: 89.7 us -> none  [the longest x1 64.4 us: body(): lax.psum_scatter(query_sums, 'frame', scatter_dimension=0, tiled=True)]
    pmax x1 -> x0, blocking collectives: 59.1 us -> none  [body(): global_max = lax.pmax(local_max, 'frame')]
    ppermute x0 -> x15, starting transfers between devices: none -> 18.8 us  [swap(): return lax.ppermute(array, 'frame', [(i, i ^ bits) for i in range(devices)])]
    all_to_all x2, waiting for transfers between devices: 18.8 us -> 0.01 us  [the longest x1 0.01 us: body(): lax.all_to_all(temporal_block, 'frame', split_axis=0, concat_axis=0, tile...]
    pallas_call x0 -> x8, Pallas kernels: none -> 16.2 us  [call(): pl.pallas_call(kernel, out_shape=outs, in_specs=[pl.BlockSpec(memory_spac...]
    ppermute x0 -> x15, waiting for transfers between devices: none -> 15.8 us  [swap(): return lax.ppermute(array, 'frame', [(i, i ^ bits) for i in range(devices)])]
    all_gather x1 -> x0, waiting for transfers between devices: 11.8 us -> none  [body(): gathered = lax.all_gather(text_qkv, 'frame', axis=1, tiled=True)]
    slice x8 -> x1, local copies, waits for them, and re-layouts: 5.08 us -> 0.02 us  [body(): joined[step * shard:(step + 1) * shard]]
  transfers between devices with their start and end apart: 5 -> 17, of which waited for: 5 -> 4; matrix products, arithmetic and copies ran while one was open for 13% -> 5% of each run, Pallas kernels for 0% -> 21%
where the time goes in v1:
time: 72.3 us; the launch traced here: 71.7 us
  starting transfers between devices  28.9 us (40%)
  Pallas kernels  16.2 us (22%)
  waiting for transfers between devices  15.9 us (22%)
  local copies, waits for them, and re-layouts  9.25 us (13%)
  between operations  1.45 us (2%)
    ppermute x15, starting transfers between devices, swap(): return lax.ppermute(array, 'frame', [(i, i ^ bits) for i in range(devices)])  18.8 us
    pallas_call x8, Pallas kernels, call(): pl.pallas_call(kernel, out_shape=outs, in_specs=[pl.BlockSpec(memory_spac...  16.2 us
    ppermute x15, waiting for transfers between devices, swap(): return lax.ppermute(array, 'frame', [(i, i ^ bits) for i in range(devices)])  15.8 us
    unnamed x26, local copies, waits for them, and re-layouts  7.74 us
    all_to_all x1, starting transfers between devices, body(): lax.all_to_all(temporal_block, 'frame', split_axis=0, concat_axis=0, tile...  6.29 us
    all_to_all x1, starting transfers between devices, body(): lax.all_to_all(result, 'frame', split_axis=0, concat_axis=0, tiled=True)  3.76 us
  transfers between devices with their start and end apart: 17, of which 4 were waited for; matrix products, arithmetic and copies ran while one was open for 5% of the time, Pallas kernels for 21%

profile of v1, /device:TPU:0, one launch (start us, length us, event | category | flops | bytes accessed | tf_op | source)
XLA Modules:
  0.0 71.7 jit_solution(4781435949179435862)
XLA Ops:
  0.6 0.8 %slice_bitcast_fusion.refs_0_ = bf16[16,1536]{1,0:T(8,128)(2,1)S(1)} fusion(bf16[3,16,1536]{2,1,0:T(8,128)(2,1)} %text_ref.5), kind=kLoop, calls=%fused_computation.2 | loop fusion | bytes 98304 | tf_op jit(solution)/shard_map/squeeze | solution.py:249
  1.4 3.0 %collective-permute-start.7 = (bf16[16,1536]{1,0:T(8,128)(2,1)S(1)}, bf16[16,1536]{1,0:T(8,128)(2,1)S(1)}, u32[]{:S(2)}, u32[]{:S(2)}) collective-permute-start(bf16[16,1536]{1,0:T(8,128)(2,1)S(1)} %slice_bitcast_fusion.refs_0_), channel_id=1, source_target_pairs={{0,4},{1,5},{2,6},{3,7},{4,0},{5,1},{6,2},{7,3},{8,12},{9,13},{10,... | collective-permute-start | bytes 147464 | tf_op jit(solution)/shard_map/ppermute | solution.py:223
  4.5 2.6 %collective-permute-start.8 = (bf16[16,1536]{1,0:T(8,128)(2,1)S(1)}, bf16[16,1536]{1,0:T(8,128)(2,1)S(1)}, u32[]{:S(2)}, u32[]{:S(2)}) collective-permute-start(bf16[16,1536]{1,0:T(8,128)(2,1)S(1)} %slice_bitcast_fusion.refs_0_), channel_id=1, source_target_pairs={{0,8},{1,9},{2,10},{3,11},{4,12},{5,13},{6,14},{7,15},{8,0},{9,1},... | collective-permute-start | bytes 147464 | tf_op jit(solution)/shard_map/ppermute | solution.py:223
  7.0 0.0 collective-permute-start.9
  7.1 0.0 collective-permute-start.6
  7.1 0.5 collective-permute-start.5
  7.6 1.3 %copy-done = bf16[3,1,128,1536]{3,2,1,0:T(8,128)(2,1)S(1)} copy-done((bf16[3,1,128,1536]{3,2,1,0:T(8,128)(2,1)S(1)}, bf16[3,1,128,1536]{3,2,1,0:T(8,128)(2,1)}, u32[]{:S(2)}) %copy-start) | copy-done | bytes 1179672
  8.8 0.9 %copy-done.2 = bf16[3,16,1536]{2,1,0:T(8,128)(2,1)S(1)} copy-done((bf16[3,16,1536]{2,1,0:T(8,128)(2,1)S(1)}, bf16[3,16,1536]{2,1,0:T(8,128)(2,1)}, u32[]{:S(2)}) %copy-start.2) | copy-done | bytes 147480
  9.7 0.7 copy-done.9
  10.4 0.7 pack.1
  11.1 0.8 %copy-done.4 = bf16[128,2304]{1,0:T(8,128)(2,1)} copy-done((bf16[128,2304]{1,0:T(8,128)(2,1)}, bf16[128,2304]{1,0:T(8,128)(2,1)S(1)}, u32[]{:S(2)}) %copy-start.4) | copy-done | bytes 589848
  11.9 6.3 %all-to-all-start = ((bf16[16,8,2304]{2,1,0:T(8,128)(2,1)}), bf16[16,8,2304]{2,1,0:T(8,128)(2,1)S(1)}, u32[]{:S(2)}, u32[]{:S(2)}) async-start(bf16[16,8,2304]{2,1,0:T(8,128)(2,1)} %bitcast.15), calls=%async_computation | async-start | bytes 1179648 | tf_op jit(solution)/shard_map/all_to_all | solution.py:233
  18.2 0.6 constant_dynamic-update-slice_fusion.4
  19.5 0.0 collective-permute-done.7.refs_1_
  19.5 2.0 %collective-permute-start = (bf16[16,1536]{1,0:T(8,128)(2,1)S(1)}, bf16[16,1536]{1,0:T(8,128)(2,1)S(1)}, u32[]{:S(2)}, u32[]{:S(2)}) collective-permute-start(bf16[16,1536]{1,0:T(8,128)(2,1)S(1)} %get-tuple-element.4), channel_id=1, source_target_pairs={{0,4},{1,5},{2,6},{3,7},{4,0},{5,1},{6,2},{7,3},{8,12},{9,13},{10,... | collective-permute-start | bytes 147464 | tf_op jit(solution)/shard_map/ppermute | solution.py:223
  21.5 0.0 collective-permute-done.8.refs_2_
  21.5 2.4 %collective-permute-start.1 = (bf16[16,1536]{1,0:T(8,128)(2,1)S(1)}, bf16[16,1536]{1,0:T(8,128)(2,1)S(1)}, u32[]{:S(2)}, u32[]{:S(2)}) collective-permute-start(bf16[16,1536]{1,0:T(8,128)(2,1)S(1)} %get-tuple-element.4), channel_id=1, source_target_pairs={{0,8},{1,9},{2,10},{3,11},{4,12},{5,13},{6,14},{7,15},{8,0},{9,1},... | collective-permute-start | bytes 147464 | tf_op jit(solution)/shard_map/ppermute | solution.py:223
  23.9 0.0 collective-permute-done.9.refs_3_
  23.9 0.1 collective-permute-start.2
  24.0 6.3 %collective-permute-done = bf16[16,1536]{1,0:T(8,128)(2,1)S(1)} collective-permute-done((bf16[16,1536]{1,0:T(8,128)(2,1)S(1)}, bf16[16,1536]{1,0:T(8,128)(2,1)S(1)}, u32[]{:S(2)}, u32[]{:S(2)}) %collective-permute-start) | collective-permute-done | bytes 49184 | tf_op jit(solution)/shard_map/ppermute | solution.py:223
  30.3 1.6 %collective-permute-start.10 = (bf16[64,1536]{1,0:T(8,128)(2,1)S(1)}, bf16[64,1536]{1,0:T(8,128)(2,1)S(1)}, u32[]{:S(2)}, u32[]{:S(2)}) collective-permute-start(bf16[64,1536]{1,0:T(8,128)(2,1)S(1)} %pad_maximum_fusion.1), channel_id=1, source_target_pairs={{0,2},{1,3},{2,0},{3,1},{4,6},{5,7},{6,4},{7,5},{8,10},{9,11},{10,... | collective-permute-start | bytes 589832 | tf_op jit(solution)/shard_map/ppermute | solution.py:223
  31.9 6.6 %collective-permute-done.1 = bf16[16,1536]{1,0:T(8,128)(2,1)S(1)} collective-permute-done((bf16[16,1536]{1,0:T(8,128)(2,1)S(1)}, bf16[16,1536]{1,0:T(8,128)(2,1)S(1)}, u32[]{:S(2)}, u32[]{:S(2)}) %collective-permute-start.1) | collective-permute-done | bytes 49184 | tf_op jit(solution)/shard_map/ppermute | solution.py:223
  38.6 1.5 %collective-permute-start.3 = (bf16[64,1536]{1,0:T(8,128)(2,1)S(1)}, bf16[64,1536]{1,0:T(8,128)(2,1)S(1)}, u32[]{:S(2)}, u32[]{:S(2)}) collective-permute-start(bf16[64,1536]{1,0:T(8,128)(2,1)S(1)} %pad_maximum_fusion), channel_id=1, source_target_pairs={{0,2},{1,3},{2,0},{3,1},{4,6},{5,7},{6,4},{7,5},{8,10},{9,11},{10,... | collective-permute-start | bytes 589832 | tf_op jit(solution)/shard_map/ppermute | solution.py:223
  40.1 0.6 constant_dynamic-update-slice_fusion.3
  40.7 0.6 constant_dynamic-update-slice_fusion.2
  41.4 0.6 constant_dynamic-update-slice_fusion.1
  42.0 0.0 collective-permute-done.10.refs_0_
  42.0 3.3 %text.3 = bf16[64,1664]{1,0:T(8,128)(2,1)S(1)} custom-call(s32[1]{0:T(128)S(6)} %copy.10.length_ref, bf16[3,128,1536]{2,1,0:T(8,128)(2,1)S(1)} %bitcast.10, bf16[3,128,1536]{2,1,0:T(8,128)(2,1)S(1)} %collective-permute-done.5.other_ref, bf16[3,16,1536]{2,1,0:T(8,128)(2,1)S(1)} %copy-done.3, bf16[3,16,1536]{2,1,0:T(8,128)(2,1)S(1)} %collective-permute-done.6.other_text_ref, ...), custom_call_target="tpu_custom_call" | custom-call | flops 113246208 | bytes 3063808 | tf_op jit(solution)/shard_map/text/pallas_call | solution.py:198
  45.4 0.6 collective-permute-start.11
  46.0 0.0 collective-permute-done.3
  46.0 0.7 constant_dynamic-update-slice_fusion.near_ref
  46.7 2.2 %temporal.1 = bf16[128,768]{1,0:T(8,128)(2,1)} custom-call(bf16[128,2304]{1,0:T(8,128)(2,1)S(1)} %bitcast.13), custom_call_target="tpu_custom_call" | custom-call | flops 50331648 | bytes 786432 | tf_op jit(solution)/shard_map/temporal/pallas_call | solution.py:198
  48.9 3.8 %all-to-all-start.1 = ((bf16[16,8,768]{2,1,0:T(8,128)(2,1)}), bf16[16,8,768]{2,1,0:T(8,128)(2,1)S(1)}, u32[]{:S(2)}, u32[]{:S(2)}) async-start(bf16[16,8,768]{2,1,0:T(8,128)(2,1)} %bitcast.3), calls=%async_computation.1 | async-start | bytes 393216 | tf_op jit(solution)/shard_map/all_to_all | solution.py:302
  52.7 0.0 copy-start.6
  52.7 0.8 %copy-done.6 = bf16[16,1536]{1,0:T(8,128)(2,1)S(1)} copy-done((bf16[16,1536]{1,0:T(8,128)(2,1)S(1)}, bf16[16,1536]{1,0:T(8,128)(2,1)}, u32[]{:S(2)}) %copy-start.6) | copy-done | bytes 49176
  53.5 0.8 %copy-done.8 = bf16[16,1536]{1,0:T(8,128)(2,1)S(1)} copy-done((bf16[16,1536]{1,0:T(8,128)(2,1)S(1)}, bf16[16,1536]{1,0:T(8,128)(2,1)}, u32[]{:S(2)}) %copy-start.8) | copy-done | bytes 49176
  54.3 3.3 %text.2.refs_0_ = bf16[64,1664]{1,0:T(8,128)(2,1)S(1)} custom-call(s32[1]{0:T(128)S(6)} %copy.10.length_ref, bf16[3,128,1536]{2,1,0:T(8,128)(2,1)S(1)} %bitcast.11, bf16[3,128,1536]{2,1,0:T(8,128)(2,1)S(1)} %collective-permute-done.5.other_ref, bf16[3,16,1536]{2,1,0:T(8,128)(2,1)S(1)} %copy-done.3, ...), custom_call_target="tpu_custom_call" | custom-call | flops 113246208 | bytes 3063808 | tf_op jit(solution)/shard_map/text/pallas_call | solution.py:198
  57.6 0.0 collective-permute-done.11.refs_1_
  57.6 1.5 %merge.1 = bf16[64,1664]{1,0:T(8,128)(2,1)S(1)} custom-call(bf16[64,1664]{1,0:T(8,128)(2,1)S(1)} %text.2.refs_0_, bf16[64,1664]{1,0:T(8,128)(2,1)} %collective-permute-done.11.refs_1_), custom_call_target="tpu_custom_call" | custom-call | bytes 638976 | tf_op jit(solution)/shard_map/merge/pallas_call | solution.py:198
  59.1 2.0 %collective-permute-start.12 = (bf16[16,1664]{1,0:T(8,128)(2,1)S(1)}, bf16[16,1664]{1,0:T(8,128)(2,1)S(1)}, u32[]{:S(2)}, u32[]{:S(2)}) collective-permute-start(bf16[16,1664]{1,0:T(8,128)(2,1)S(1)} %get-tuple-element.8), channel_id=1, source_target_pairs={{0,4},{1,5},{2,6},{3,7},{4,0},{5,1},{6,2},{7,3},{8,12},{9,13},{10,... | collective-permute-start | bytes 159752 | tf_op jit(solution)/shard_map/ppermute | solution.py:223
  61.1 2.4 %collective-permute-start.13 = (bf16[16,1664]{1,0:T(8,128)(2,1)S(1)}, bf16[16,1664]{1,0:T(8,128)(2,1)S(1)}, u32[]{:S(2)}, u32[]{:S(2)}) collective-permute-start(bf16[16,1664]{1,0:T(8,128)(2,1)S(1)} %get-tuple-element.7), channel_id=1, source_target_pairs={{0,8},{1,9},{2,10},{3,11},{4,12},{5,13},{6,14},{7,15},{8,0},{9,1},... | collective-permute-start | bytes 159752 | tf_op jit(solution)/shard_map/ppermute | solution.py:223
  63.5 0.1 collective-permute-start.14
  63.5 0.0 collective-permute-done.4.far_ref
  63.6 2.9 %spatial.1.spatial_ref = bf16[128,768]{1,0:T(8,128)(2,1)S(1)} custom-call(s32[12]{0:T(128)S(1)} %copy-done.10, s32[1]{0:T(128)S(6)} %copy.10.length_ref, bf16[3,128,1536]{2,1,0:T(8,128)(2,1)S(1)} %bitcast.12, bf16[128,1536]{1,0:T(8,128)(2,1)} %constant_dynamic-update-slice_fusion.near_ref, bf16[128,1536]{1,0:T(8,128)(2,1)} %collective-permute-done.4.far_ref), custom_call_target="tpu_custom_call" | custom-call | flops 150994944 | bytes 2162688 | tf_op jit(solution)/shard_map/spatial/pallas_call | solution.py:198
  66.5 0.8 %collective-permute-done.13.refs_2_ = bf16[16,1664]{1,0:T(8,128)(2,1)S(1)} collective-permute-done((bf16[16,1664]{1,0:T(8,128)(2,1)S(1)}, bf16[16,1664]{1,0:T(8,128)(2,1)S(1)}, u32[]{:S(2)}, u32[]{:S(2)}) %collective-permute-start.13) | collective-permute-done | bytes 53280 | tf_op jit(solution)/shard_map/ppermute | solution.py:223
  67.3 2.1 %collective-permute-done.14.refs_3_ = bf16[16,1664]{1,0:T(8,128)(2,1)S(1)} collective-permute-done((bf16[16,1664]{1,0:T(8,128)(2,1)S(1)}, bf16[16,1664]{1,0:T(8,128)(2,1)S(1)}, u32[]{:S(2)}, u32[]{:S(2)}) %collective-permute-start.14) | collective-permute-done | bytes 53280 | tf_op jit(solution)/shard_map/ppermute | solution.py:223
  69.4 0.9 %finish.1 = bf16[16,1536]{1,0:T(8,128)(2,1)} custom-call(bf16[16,1664]{1,0:T(8,128)(2,1)S(1)} %get-tuple-element.9.refs_0_, bf16[16,1664]{1,0:T(8,128)(2,1)S(1)} %collective-permute-done.12.refs_1_, bf16[16,1664]{1,0:T(8,128)(2,1)S(1)} %collective-permute-done.13.refs_2_, bf16[16,1664]{1,0:T(8,128)(2,1)S(1)} %collective-permute-done.14.refs_3_), custom_call_target="tpu_custom_call" | custom-call | bytes 262144 | tf_op jit(solution)/shard_map/finish/pallas_call | solution.py:198
  70.3 1.4 %join.1 = bf16[128,1536]{1,0:T(8,128)(2,1)} custom-call(s32[12]{0:T(128)S(1)} %copy-done.10, bf16[128,768]{1,0:T(8,128)(2,1)S(1)} %spatial.1.spatial_ref, bf16[128,768]{1,0:T(8,128)(2,1)S(1)} %bitcast.14), custom_call_target="tpu_custom_call" | custom-call | bytes 786432 | tf_op jit(solution)/shard_map/join/pallas_call | solution.py:198
  (25 shorter events, 0.1 us)
Async XLA Ops:
  1.4 18.1 %collective-permute-start.7 = (bf16[16,1536]{1,0:T(8,128)(2,1)S(1)}, bf16[16,1536]{1,0:T(8,128)(2,1)S(1)}, u32[]{:S(2)}, u32[]{:S(2)}) collective-permute-start(bf16[16,1536]{1,0:T(8,128)(2,1)S(1)} %slice_bitcast_fusion.refs_0_), channel_id=1, source_target_pairs={{0,4},{1,5},{2,6},{3,7},{4,0},{5,1},{6,2},{7,3},{8,12},{9,13},{10,... | collective-permute-start | bytes 147464 | tf_op jit(solution)/shard_map/ppermute | solution.py:223
  4.5 17.0 %collective-permute-start.8 = (bf16[16,1536]{1,0:T(8,128)(2,1)S(1)}, bf16[16,1536]{1,0:T(8,128)(2,1)S(1)}, u32[]{:S(2)}, u32[]{:S(2)}) collective-permute-start(bf16[16,1536]{1,0:T(8,128)(2,1)S(1)} %slice_bitcast_fusion.refs_0_), channel_id=1, source_target_pairs={{0,8},{1,9},{2,10},{3,11},{4,12},{5,13},{6,14},{7,15},{8,0},{9,1},... | collective-permute-start | bytes 147464 | tf_op jit(solution)/shard_map/ppermute | solution.py:223
  7.0 16.8 %collective-permute-start.9 = (bf16[16,1536]{1,0:T(8,128)(2,1)S(1)}, bf16[16,1536]{1,0:T(8,128)(2,1)S(1)}, u32[]{:S(2)}, u32[]{:S(2)}) collective-permute-start(bf16[16,1536]{1,0:T(8,128)(2,1)S(1)} %slice_bitcast_fusion.refs_0_), channel_id=1, source_target_pairs={{0,12},{1,13},{2,14},{3,15},{4,8},{5,9},{6,10},{7,11},{8,4},{9,5},... | collective-permute-start | bytes 147464 | tf_op jit(solution)/shard_map/ppermute | solution.py:223
  7.1 34.9 %collective-permute-start.6 = (bf16[3,16,1536]{2,1,0:T(8,128)(2,1)}, bf16[3,16,1536]{2,1,0:T(8,128)(2,1)S(1)}, u32[]{:S(2)}, u32[]{:S(2)}) collective-permute-start(bf16[3,16,1536]{2,1,0:T(8,128)(2,1)} %text_ref.5), channel_id=1, source_target_pairs={{0,1},{1,0},{2,3},{3,2},{4,5},{5,4},{6,7},{7,6},{8,9},{9,8},{10,11... | collective-permute-start | bytes 442376 | tf_op jit(solution)/shard_map/ppermute | solution.py:223
  7.1 35.0 %collective-permute-start.5 = (bf16[3,128,1536]{2,1,0:T(8,128)(2,1)}, bf16[3,128,1536]{2,1,0:T(8,128)(2,1)S(1)}, u32[]{:S(2)}, u32[]{:S(2)}) collective-permute-start(bf16[3,128,1536]{2,1,0:T(8,128)(2,1)} %bitcast.8), channel_id=1, source_target_pairs={{0,1},{1,0},{2,3},{3,2},{4,5},{5,4},{6,7},{7,6},{8,9},{9,8},{10,11... | collective-permute-start | bytes 3538952 | tf_op jit(solution)/shard_map/ppermute | solution.py:223
  7.6 1.3 %copy-start = (bf16[3,1,128,1536]{3,2,1,0:T(8,128)(2,1)S(1)}, bf16[3,1,128,1536]{3,2,1,0:T(8,128)(2,1)}, u32[]{:S(2)}) copy-start(bf16[3,1,128,1536]{3,2,1,0:T(8,128)(2,1)} %param.4) | copy-start | bytes 3538948
  8.8 0.9 %copy-start.2 = (bf16[3,16,1536]{2,1,0:T(8,128)(2,1)S(1)}, bf16[3,16,1536]{2,1,0:T(8,128)(2,1)}, u32[]{:S(2)}) copy-start(bf16[3,16,1536]{2,1,0:T(8,128)(2,1)} %text_ref.5) | copy-start | bytes 442372
  9.7 0.7 copy-start.9
  11.1 0.8 %copy-start.4 = (bf16[128,2304]{1,0:T(8,128)(2,1)}, bf16[128,2304]{1,0:T(8,128)(2,1)S(1)}, u32[]{:S(2)}) copy-start(bf16[128,2304]{1,0:T(8,128)(2,1)S(1)} %get-tuple-element.5) | copy-start | bytes 1769476
  11.9 30.1 %copy-start.1 = (bf16[3,1,128,1536]{3,2,1,0:T(8,128)(2,1)S(1)}, bf16[3,1,128,1536]{3,2,1,0:T(8,128)(2,1)}, u32[]{:S(2)}) copy-start(bf16[3,1,128,1536]{3,2,1,0:T(8,128)(2,1)} %param.4) | copy-start | bytes 3538948
  11.9 30.1 %copy-start.3 = (bf16[3,16,1536]{2,1,0:T(8,128)(2,1)S(1)}, bf16[3,16,1536]{2,1,0:T(8,128)(2,1)}, u32[]{:S(2)}) copy-start(bf16[3,16,1536]{2,1,0:T(8,128)(2,1)} %text_ref.5) | copy-start | bytes 442372
  11.9 34.8 %all-to-all-start = ((bf16[16,8,2304]{2,1,0:T(8,128)(2,1)}), bf16[16,8,2304]{2,1,0:T(8,128)(2,1)S(1)}, u32[]{:S(2)}, u32[]{:S(2)}) async-start(bf16[16,8,2304]{2,1,0:T(8,128)(2,1)} %bitcast.15), calls=%async_computation | async-start | bytes 1179648 | tf_op jit(solution)/shard_map/all_to_all | solution.py:233
  19.5 10.8 %collective-permute-start = (bf16[16,1536]{1,0:T(8,128)(2,1)S(1)}, bf16[16,1536]{1,0:T(8,128)(2,1)S(1)}, u32[]{:S(2)}, u32[]{:S(2)}) collective-permute-start(bf16[16,1536]{1,0:T(8,128)(2,1)S(1)} %get-tuple-element.4), channel_id=1, source_target_pairs={{0,4},{1,5},{2,6},{3,7},{4,0},{5,1},{6,2},{7,3},{8,12},{9,13},{10,... | collective-permute-start | bytes 147464 | tf_op jit(solution)/shard_map/ppermute | solution.py:223
  21.5 20.5 %copy-start.5 = (bf16[16,1536]{1,0:T(8,128)(2,1)}, bf16[16,1536]{1,0:T(8,128)(2,1)S(1)}, u32[]{:S(2)}) copy-start(bf16[16,1536]{1,0:T(8,128)(2,1)S(1)} %collective-permute-done.8.refs_2_) | copy-start | bytes 147460
  21.5 17.1 %collective-permute-start.1 = (bf16[16,1536]{1,0:T(8,128)(2,1)S(1)}, bf16[16,1536]{1,0:T(8,128)(2,1)S(1)}, u32[]{:S(2)}, u32[]{:S(2)}) collective-permute-start(bf16[16,1536]{1,0:T(8,128)(2,1)S(1)} %get-tuple-element.4), channel_id=1, source_target_pairs={{0,8},{1,9},{2,10},{3,11},{4,12},{5,13},{6,14},{7,15},{8,0},{9,1},... | collective-permute-start | bytes 147464 | tf_op jit(solution)/shard_map/ppermute | solution.py:223
  23.9 18.1 %copy-start.7 = (bf16[16,1536]{1,0:T(8,128)(2,1)}, bf16[16,1536]{1,0:T(8,128)(2,1)S(1)}, u32[]{:S(2)}) copy-start(bf16[16,1536]{1,0:T(8,128)(2,1)S(1)} %collective-permute-done.9.refs_3_) | copy-start | bytes 147460
  23.9 14.7 %collective-permute-start.2 = (bf16[16,1536]{1,0:T(8,128)(2,1)S(1)}, bf16[16,1536]{1,0:T(8,128)(2,1)S(1)}, u32[]{:S(2)}, u32[]{:S(2)}) collective-permute-start(bf16[16,1536]{1,0:T(8,128)(2,1)S(1)} %get-tuple-element.4), channel_id=1, source_target_pairs={{0,12},{1,13},{2,14},{3,15},{4,8},{5,9},{6,10},{7,11},{8,4},{9,5},... | collective-permute-start | bytes 147464 | tf_op jit(solution)/shard_map/ppermute | solution.py:223
  30.3 11.7 %collective-permute-start.10 = (bf16[64,1536]{1,0:T(8,128)(2,1)S(1)}, bf16[64,1536]{1,0:T(8,128)(2,1)S(1)}, u32[]{:S(2)}, u32[]{:S(2)}) collective-permute-start(bf16[64,1536]{1,0:T(8,128)(2,1)S(1)} %pad_maximum_fusion.1), channel_id=1, source_target_pairs={{0,2},{1,3},{2,0},{3,1},{4,6},{5,7},{6,4},{7,5},{8,10},{9,11},{10,... | collective-permute-start | bytes 589832 | tf_op jit(solution)/shard_map/ppermute | solution.py:223
  38.6 7.4 %collective-permute-start.3 = (bf16[64,1536]{1,0:T(8,128)(2,1)S(1)}, bf16[64,1536]{1,0:T(8,128)(2,1)S(1)}, u32[]{:S(2)}, u32[]{:S(2)}) collective-permute-start(bf16[64,1536]{1,0:T(8,128)(2,1)S(1)} %pad_maximum_fusion), channel_id=1, source_target_pairs={{0,2},{1,3},{2,0},{3,1},{4,6},{5,7},{6,4},{7,5},{8,10},{9,11},{10,... | collective-permute-start | bytes 589832 | tf_op jit(solution)/shard_map/ppermute | solution.py:223
  45.4 12.2 %collective-permute-start.11 = (bf16[64,1664]{1,0:T(8,128)(2,1)S(1)}, bf16[64,1664]{1,0:T(8,128)(2,1)}, u32[]{:S(2)}, u32[]{:S(2)}) collective-permute-start(bf16[64,1664]{1,0:T(8,128)(2,1)S(1)} %text.3), channel_id=1, source_target_pairs={{0,2},{1,3},{2,0},{3,1},{4,6},{5,7},{6,4},{7,5},{8,10},{9,11},{10,... | collective-permute-start | bytes 638984 | tf_op jit(solution)/shard_map/ppermute | solution.py:223
  46.7 16.9 %collective-permute-start.4 = (bf16[128,1536]{1,0:T(8,128)(2,1)}, bf16[128,1536]{1,0:T(8,128)(2,1)}, u32[]{:S(2)}, u32[]{:S(2)}) collective-permute-start(bf16[128,1536]{1,0:T(8,128)(2,1)} %constant_dynamic-update-slice_fusion.near_ref), channel_id=1, source_target_pairs={{0,1},{1,0},{2,3},{3,2},{4,5},{5,4},{6,7},{7,6},{8,9},{9,8},{10,11... | collective-permute-start | bytes 1179656 | tf_op jit(solution)/shard_map/ppermute | solution.py:223
  48.9 21.4 %all-to-all-start.1 = ((bf16[16,8,768]{2,1,0:T(8,128)(2,1)}), bf16[16,8,768]{2,1,0:T(8,128)(2,1)S(1)}, u32[]{:S(2)}, u32[]{:S(2)}) async-start(bf16[16,8,768]{2,1,0:T(8,128)(2,1)} %bitcast.3), calls=%async_computation.1 | async-start | bytes 393216 | tf_op jit(solution)/shard_map/all_to_all | solution.py:302
  52.7 0.8 %copy-start.6 = (bf16[16,1536]{1,0:T(8,128)(2,1)S(1)}, bf16[16,1536]{1,0:T(8,128)(2,1)}, u32[]{:S(2)}) copy-start(bf16[16,1536]{1,0:T(8,128)(2,1)} %copy-done.5) | copy-start | bytes 147460
  53.5 0.8 %copy-start.8 = (bf16[16,1536]{1,0:T(8,128)(2,1)S(1)}, bf16[16,1536]{1,0:T(8,128)(2,1)}, u32[]{:S(2)}) copy-start(bf16[16,1536]{1,0:T(8,128)(2,1)} %copy-done.7) | copy-start | bytes 147460
  54.3 9.3 %copy-start.10 = (s32[12]{0:T(128)S(1)}, s32[12]{0:T(128)}, u32[]{:S(2)}) copy-start(s32[12]{0:T(128)} %kind_ref.5) | copy-start | bytes 148
  59.1 7.4 %collective-permute-start.12 = (bf16[16,1664]{1,0:T(8,128)(2,1)S(1)}, bf16[16,1664]{1,0:T(8,128)(2,1)S(1)}, u32[]{:S(2)}, u32[]{:S(2)}) collective-permute-start(bf16[16,1664]{1,0:T(8,128)(2,1)S(1)} %get-tuple-element.8), channel_id=1, source_target_pairs={{0,4},{1,5},{2,6},{3,7},{4,0},{5,1},{6,2},{7,3},{8,12},{9,13},{10,... | collective-permute-start | bytes 159752 | tf_op jit(solution)/shard_map/ppermute | solution.py:223
  61.1 6.2 %collective-permute-start.13 = (bf16[16,1664]{1,0:T(8,128)(2,1)S(1)}, bf16[16,1664]{1,0:T(8,128)(2,1)S(1)}, u32[]{:S(2)}, u32[]{:S(2)}) collective-permute-start(bf16[16,1664]{1,0:T(8,128)(2,1)S(1)} %get-tuple-element.7), channel_id=1, source_target_pairs={{0,8},{1,9},{2,10},{3,11},{4,12},{5,13},{6,14},{7,15},{8,0},{9,1},... | collective-permute-start | bytes 159752 | tf_op jit(solution)/shard_map/ppermute | solution.py:223
  63.5 5.9 %collective-permute-start.14 = (bf16[16,1664]{1,0:T(8,128)(2,1)S(1)}, bf16[16,1664]{1,0:T(8,128)(2,1)S(1)}, u32[]{:S(2)}, u32[]{:S(2)}) collective-permute-start(bf16[16,1664]{1,0:T(8,128)(2,1)S(1)} %get-tuple-element.6), channel_id=1, source_target_pairs={{0,12},{1,13},{2,14},{3,15},{4,8},{5,9},{6,10},{7,11},{8,4},{9,5},... | collective-permute-start | bytes 159752 | tf_op jit(solution)/shard_map/ppermute | solution.py:223

commit v2 on v1

v2 whole, which is shorter than its diff:
```python
import functools

import jax
import jax.numpy as jnp
from jax import lax
from jax.experimental import pallas as pl
from jax.experimental.pallas import tpu as pltpu
from jax.sharding import PartitionSpec as P

masked_score = -1e30
lanes = 128


def contract_last(a, b):
    return lax.dot_general(a, b, (((1,), (1,)), ((), ())), preferred_element_type=jnp.float32)


def head_lanes(head):
    if isinstance(head, int):
        return pl.ds(head * lanes, lanes)
    return pl.ds(pl.multiple_of(head * lanes, lanes), lanes)


def list_heads(kind_ref, list_ref, head_count):
    ones = jnp.int32(0)
    for head in range(head_count):
        kind = kind_ref[head]
        slot = jnp.where(kind == 1, head_count + ones, head - ones)
        list_ref[slot] = jnp.int32(head)
        ones = ones + kind


def pack_kernel(
    head_count, kind_ref, text_ref, video_ref, packed_ref, temporal_ref, list_ref, text_here, video_here, sems
):
    copies = [pltpu.make_async_copy(text_ref, text_here, sems.at[3])]
    for part in range(3):
        copies.append(
            pltpu.make_async_copy(video_ref.at[part], video_here.at[part], sems.at[part])
        )
    for copy in copies:
        copy.start()
    list_heads(kind_ref, list_ref, head_count)
    half = head_count // 2
    copies[0].wait()
    packed_ref[:, : head_count * lanes] = text_here[0]
    for slot in range(half):
        for part in range(2):
            packed_ref[:, head_lanes(head_count + part * half + slot)] = text_here[
                part + 1, :, head_lanes(list_ref[slot])
            ]
    for part in range(3):
        copies[part + 1].wait()
        for slot in range(half):
            temporal_ref[:, head_lanes(part * half + slot)] = video_here[
                part, :, head_lanes(list_ref[head_count + slot])
            ]


def temporal_kernel(half, stride, scale, block_ref, out_ref, score_ref, weight_ref):
    rows = block_ref.shape[0]
    row = lax.broadcasted_iota(jnp.int32, (rows, rows), 0)
    column = lax.broadcasted_iota(jnp.int32, (rows, rows), 1)
    same = lax.rem(row, stride) == lax.rem(column, stride)
    for slot in range(half):
        score_ref[slot] = contract_last(
            block_ref[:, head_lanes(slot)], block_ref[:, head_lanes(half + slot)]
        )
    totals = []
    for slot in range(half):
        scores = jnp.where(same, score_ref[slot] * scale, masked_score)
        exps = jnp.exp(scores - scores.max(-1, keepdims=True))
        totals.append(exps.sum(-1, keepdims=True))
        weight_ref[slot] = exps.astype(jnp.bfloat16)
    for slot in range(half):
        summed = jnp.dot(
            weight_ref[slot],
            block_ref[:, head_lanes(2 * half + slot)],
            preferred_element_type=jnp.float32,
        )
        out_ref[:, head_lanes(slot)] = (summed / totals[slot]).astype(jnp.bfloat16)


def spatial_kernel(
    head_count,
    shard,
    relative,
    scale,
    kind_ref,
    length_ref,
    video_ref,
    near_ref,
    far_ref,
    out_ref,
    list_ref,
    score_ref,
    weight_ref,
):
    list_heads(kind_ref, list_ref, head_count)
    half = head_count // 2
    positions = video_ref.shape[1]
    text_total = near_ref.shape[0] + far_ref.shape[0]
    index = lax.broadcasted_iota(jnp.int32, (8, text_total), 1)
    if relative:
        block = index // shard
        differs = (block & 3) * 4 + ((block >> 2) & 1) * 2 + ((block >> 3) & 1)
        index = (lax.axis_index("frame") ^ differs) * shard + lax.rem(index, shard)
    bias = jnp.where(index < length_ref[0], 0.0, masked_score)[:1]
    bias = jnp.concatenate([jnp.zeros((1, positions), jnp.float32), bias], axis=1)

    def gathered(part, slot):
        return jnp.concatenate(
            [
                video_ref[part + 1, :, head_lanes(list_ref[slot])],
                near_ref[:, head_lanes(part * half + slot)],
                far_ref[:, head_lanes(part * half + slot)],
            ],
            axis=0,
        )

    for slot in range(half):
        score_ref[slot] = contract_last(
            video_ref[0, :, head_lanes(list_ref[slot])], gathered(0, slot)
        )
    totals = []
    for slot in range(half):
        scores = score_ref[slot] * scale + bias
        exps = jnp.exp(scores - scores.max(-1, keepdims=True))
        totals.append(exps.sum(-1, keepdims=True))
        weight_ref[slot] = exps.astype(jnp.bfloat16)
    for slot in range(half):
        summed = jnp.dot(
            weight_ref[slot], gathered(1, slot), preferred_element_type=jnp.float32
        )
        out_ref[:, head_lanes(slot)] = (summed / totals[slot]).astype(jnp.bfloat16)


def text_kernel(head_count, shard, scale, length_ref, *refs):
    query_refs, key_refs = refs[:-7], refs[-7:-3]
    out_ref, score_ref, weight_ref = refs[-3:]
    rows = out_ref.shape[0]
    positions, text_rows = key_refs[0].shape[1], key_refs[2].shape[1]
    place = lax.broadcasted_iota(jnp.int32, (8, 2 * (positions + text_rows)), 1) - 2 * positions
    block = jnp.where(place >= text_rows, 1, 0)
    within = place - block * text_rows
    token = (lax.axis_index("frame") ^ block) * shard + within
    unused = (place >= 0) & ((within >= shard) | (token >= length_ref[0]))
    bias = jnp.where(unused, masked_score, 0.0)[:1]
    lane = lax.broadcasted_iota(jnp.int32, (rows, lanes), 1)
    stats = jnp.zeros((rows, lanes), jnp.float32)

    def gathered(part, head):
        return jnp.concatenate([ref[part, :, head_lanes(head)] for ref in key_refs], axis=0)

    for head in range(head_count):
        query = jnp.concatenate([ref[:, head_lanes(head)] for ref in query_refs], axis=0)
        score_ref[head] = contract_last(query, gathered(1, head))
    for head in range(head_count):
        scores = score_ref[head] * scale + bias
        point = scores.max(-1, keepdims=True).astype(jnp.bfloat16).astype(jnp.float32)
        exps = jnp.exp(scores - point)
        total = exps.sum(-1, keepdims=True)
        weight_ref[head] = exps.astype(jnp.bfloat16)
        high = total.astype(jnp.bfloat16).astype(jnp.float32)
        for place, column in enumerate((point, high, total - high)):
            stats = jnp.where(lane == 3 * head + place, column, stats)
    for head in range(head_count):
        summed = jnp.dot(
            weight_ref[head], gathered(2, head), preferred_element_type=jnp.float32
        )
        out_ref[:, head_lanes(head)] = summed.astype(jnp.bfloat16)
    out_ref[:, head_lanes(head_count)] = stats.astype(jnp.bfloat16)


def merge(head_count, blocks):
    stats = [block(head_count).astype(jnp.float32) for block in blocks]
    merged = []
    for head in range(head_count):
        points = [s[:, 3 * head : 3 * head + 1] for s in stats]
        totals = [s[:, 3 * head + 1 : 3 * head + 2] + s[:, 3 * head + 2 : 3 * head + 3] for s in stats]
        point = functools.reduce(jnp.maximum, points)
        factors = [jnp.exp(p - point) for p in points]
        total = sum(f * t for f, t in zip(factors, totals))
        summed = sum(f * block(head).astype(jnp.float32) for f, block in zip(factors, blocks))
        merged.append((point, total, summed))
    return merged


def reader(ref):
    return lambda head: ref[:, head_lanes(head)]


def merge_kernel(head_count, *refs):
    out_ref = refs[-1]
    lane = lax.broadcasted_iota(jnp.int32, (out_ref.shape[0], lanes), 1)
    stats = jnp.zeros(lane.shape, jnp.float32)
    for head, (point, total, summed) in enumerate(
        merge(head_count, [reader(ref) for ref in refs[:-1]])
    ):
        out_ref[:, head_lanes(head)] = summed.astype(jnp.bfloat16)
        high = total.astype(jnp.bfloat16).astype(jnp.float32)
        for place, column in enumerate((point, high, total - high)):
            stats = jnp.where(lane == 3 * head + place, column, stats)
    out_ref[:, head_lanes(head_count)] = stats.astype(jnp.bfloat16)


def finish_kernel(head_count, *refs):
    out_ref = refs[-1]
    for head, (_, total, summed) in enumerate(
        merge(head_count, [reader(ref) for ref in refs[:-1]])
    ):
        out_ref[:, head_lanes(head)] = (summed / total).astype(jnp.bfloat16)


def join_kernel(head_count, kind_ref, spatial_ref, temporal_ref, out_ref, list_ref):
    list_heads(kind_ref, list_ref, head_count)
    half = head_count // 2
    for kind, ref in enumerate((spatial_ref, temporal_ref)):
        for slot in range(half):
            out_ref[:, head_lanes(list_ref[kind * head_count + slot])] = ref[
                :, pl.ds(slot * lanes, lanes)
            ]


def after(array, *others):
    return lax.optimization_barrier((array, *others))[0]


def after(array, *others):
    return lax.optimization_barrier((array, *others))[0]


def call(kernel, name, out, scalars, arrays, scratch=(), flops=0, space=pltpu.VMEM):
    outs = [jax.ShapeDtypeStruct(shape, jnp.bfloat16) for shape in out]
    moved = sum(a.size * 2 for a in arrays) + sum(o.size * 2 for o in outs)
    return pl.pallas_call(
        kernel,
        out_shape=outs,
        in_specs=[pl.BlockSpec(memory_space=pltpu.SMEM)] * len(scalars)
        + [pl.BlockSpec(memory_space=space)] * len(arrays),
        out_specs=[pl.BlockSpec(memory_space=pltpu.VMEM)] * len(outs),
        scratch_shapes=scratch,
        compiler_params=pltpu.CompilerParams(vmem_limit_bytes=32 * 2**20),
        cost_estimate=pl.CostEstimate(flops=flops, bytes_accessed=moved, transcendentals=0),
        name=name,
    )(*scalars, *arrays)


def score_scratch(heads, rows, keys):
    return [pltpu.VMEM((heads, rows, keys), jnp.float32), pltpu.VMEM((heads, rows, keys), jnp.bfloat16)]


def body(devices, video_qkv, text_qkv, head_kind, text_len):
    head_count = head_kind.shape[0]
    half = head_count // 2
    width = video_qkv.shape[-1]
    positions = video_qkv.shape[2]
    shard = text_qkv.shape[1]
    scale = (width // head_count) ** -0.5
    video = video_qkv.reshape(3, positions, width)
    relative = devices == 16
    head_list = [pltpu.SMEM((2 * head_count,), jnp.int32)]

    def swap(array, bits):
        return lax.ppermute(array, "frame", [(i, i ^ bits) for i in range(devices)])

    packed_text, packed_video = call(
        functools.partial(pack_kernel, head_count),
        "pack",
        [(shard, 2 * width), (positions, 3 * half * lanes)],
        [head_kind],
        [text_qkv, video],
        head_list
        + [pltpu.VMEM(a.shape, a.dtype) for a in (text_qkv, video)]
        + [pltpu.SemaphoreType.DMA((4,))],
        space=pl.ANY,
    )
    block = lax.all_to_all(packed_video, "frame", split_axis=0, concat_axis=0, tiled=True)

    text_rows = -(-shard // 16) * 16
    text = jnp.pad(text_qkv, ((0, 0), (0, text_rows - shard), (0, 0)))
    keys = [video, swap(video, 1), text, swap(text, 1)]

    def attend(queries):
        rows = sum(q.shape[0] for q in queries)
        key_count = 2 * (positions + text_rows)
        return call(
            functools.partial(text_kernel, head_count, shard, scale),
            "text",
            [(rows, width + lanes)],
            [text_len],
            [*queries, *keys],
            score_scratch(head_count, rows, key_count),
            flops=4 * rows * width * key_count,
        )[0]

    if relative:
        column = [packed_text] + [swap(packed_text, 4 * step) for step in (1, 2, 3)]
        across = swap(jnp.concatenate([c[:, :width] for c in column], axis=0), 2)
        kept = attend(column)
        across = after(across, kept)
        partial_sums = attend([across])
        sent = swap(partial_sums, 2)
        block = after(block, partial_sums)
        (joined,) = call(
            functools.partial(merge_kernel, head_count), "merge", [kept.shape], [], [kept, sent]
        )
        pieces = [joined[:shard]] + [
            swap(joined[step * shard : (step + 1) * shard], 4 * step) for step in (1, 2, 3)
        ]
        keys_column = jnp.concatenate([c[:, width:] for c in column], axis=0)
        keys_column = after(keys_column, partial_sums)
        near_keys = jnp.concatenate([keys_column, swap(keys_column, 2)], axis=0)
        far_keys = swap(near_keys, 1)
    else:
        side = [[2 * chip + core for chip in range(devices // 2)] for core in range(2)]
        gathered = lax.all_gather(
            packed_text[:, :width], "frame", axis=0, tiled=True, axis_index_groups=side
        )
        partial_sums = lax.all_to_all(
            attend([gathered]), "frame", 0, 0, tiled=True, axis_index_groups=side
        ).reshape(devices // 2, shard, width + lanes)
        blocks = [
            lambda head, i=i: partial_sums[i, :, head * lanes : (head + 1) * lanes]
            for i in range(devices // 2)
        ]
        text_out = jnp.concatenate(
            [summed / total for _, total, summed in merge(head_count, blocks)], axis=1
        ).astype(jnp.bfloat16)
        all_keys = lax.all_gather(packed_text[:, width:], "frame", axis=0, tiled=True)
        near_keys, far_keys = jnp.split(all_keys, 2, axis=0)

    key_count = positions + devices * shard
    (spatial,) = call(
        functools.partial(spatial_kernel, head_count, shard, relative, scale),
        "spatial",
        [(positions, half * lanes)],
        [head_kind, text_len],
        [video, near_keys, far_keys],
        head_list + score_scratch(half, positions, key_count),
        flops=4 * positions * half * lanes * key_count,
    )
    if relative:
        pieces[0] = after(pieces[0], spatial)
        (text_out,) = call(
            functools.partial(finish_kernel, head_count), "finish", [(shard, width)], [], pieces
        )
    (result,) = call(
        functools.partial(temporal_kernel, half, positions // devices, scale),
        "temporal",
        [(positions, half * lanes)],
        [],
        [block],
        score_scratch(half, positions, positions),
        flops=4 * positions * half * lanes * positions,
    )
    temporal = lax.all_to_all(result, "frame", split_axis=0, concat_axis=0, tiled=True)
    (video_out,) = call(
        functools.partial(join_kernel, head_count),
        "join",
        [(positions, width)],
        [head_kind],
        [spatial, temporal],
        head_list,
    )
    return video_out.reshape(1, positions, width), text_out


def solution(mesh):
    in_specs = (
        P(None, ("groups", "frame"), None, None),
        P(None, ("groups", "frame"), None),
        P("groups"),
        P("groups"),
    )
    out_specs = (P(("groups", "frame"), None, None), P(("groups", "frame"), None))
    return jax.shard_map(
        functools.partial(body, mesh.shape["frame"]),
        mesh=mesh,
        in_specs=in_specs,
        out_specs=out_specs,
        check_vma=False,
    )
```

time: 72.3 us -> 53.5 us (0.74)
  local copies, waits for them, and re-layouts: 9.25 us -> 0.74 us
  waiting for transfers between devices: 15.9 us -> 11.5 us
  Pallas kernels: 16.2 us -> 13 us
  starting transfers between devices: 28.9 us -> 26.4 us
    unnamed x26 -> x5, local copies, waits for them, and re-layouts: 7.74 us -> 0.67 us
    ppermute x15 -> x12, waiting for transfers between devices: 15.8 us -> 11.5 us  [swap(): return lax.ppermute(array, 'frame', [(i, i ^ bits) for i in range(devices)])]
    ppermute x15 -> x12, starting transfers between devices: 18.8 us -> 14.7 us  [swap(): return lax.ppermute(array, 'frame', [(i, i ^ bits) for i in range(devices)])]
    pallas_call x8, Pallas kernels: 16.2 us -> 13 us  [call(): pl.pallas_call(kernel, out_shape=outs, in_specs=[pl.BlockSpec(memory_spac...]
    all_to_all x1, starting transfers between devices: 3.76 us -> 5.57 us  [body(): lax.all_to_all(result, 'frame', split_axis=0, concat_axis=0, tiled=True)]
    squeeze x1 -> x0, local copies, waits for them, and re-layouts: 0.8 us -> none  [body(): queries = text_qkv[0]]
  transfers between devices with their start and end apart: 17 -> 14, of which waited for: 4 -> 5; matrix products, arithmetic and copies ran while one was open for 5% -> 0% of each run, Pallas kernels for 21% -> 18%
where the time goes in v2:
time: 53.5 us; the launch traced here: 53.1 us
  starting transfers between devices  26.4 us (49%)
  Pallas kernels  13 us (24%)
  waiting for transfers between devices  11.5 us (21%)
  between operations  1.46 us (3%)
  local copies, waits for them, and re-layouts  0.74 us (1%)
    ppermute x12, starting transfers between devices, swap(): return lax.ppermute(array, 'frame', [(i, i ^ bits) for i in range(devices)])  14.7 us
    pallas_call x8, Pallas kernels, call(): pl.pallas_call(kernel, out_shape=outs, in_specs=[pl.BlockSpec(memory_spac...  13 us
    ppermute x12, waiting for transfers between devices, swap(): return lax.ppermute(array, 'frame', [(i, i ^ bits) for i in range(devices)])  11.5 us
    all_to_all x1, starting transfers between devices, body(): lax.all_to_all(packed_video, 'frame', split_axis=0, concat_axis=0, tiled=...  6.16 us
    all_to_all x1, starting transfers between devices, body(): lax.all_to_all(result, 'frame', split_axis=0, concat_axis=0, tiled=True)  5.57 us
  transfers between devices with their start and end apart: 14, of which 5 were waited for; matrix products, arithmetic and copies ran while one was open for 0% of the time, Pallas kernels for 18%

profile of v2, /device:TPU:0, one launch (start us, length us, event | category | flops | bytes accessed | tf_op | source)
XLA Modules:
  0.0 53.1 jit_solution(619437063282897748)
XLA Ops:
  0.6 0.0 copy-start
  0.6 0.6 %copy-done = s32[12]{0:T(128)S(1)} copy-done((s32[12]{0:T(128)S(1)}, s32[12]{0:T(128)}, u32[]{:S(2)}) %copy-start) | copy-done | bytes 72
  1.3 2.8 %pack.1 = (bf16[16,3072]{1,0:T(8,128)(2,1)S(1)}, bf16[128,2304]{1,0:T(8,128)(2,1)}) custom-call(s32[12]{0:T(128)S(1)} %copy-done, bf16[3,16,1536]{2,1,0:T(8,128)(2,1)} %refs_3_.1, bf16[3,128,1536]{2,1,0:T(8,128)(2,1)} %bitcast.video_ref.refs_4_.refs_1_), custom_call_target="tpu_custom_call" | custom-call | bytes 2015232 | tf_op jit(solution)/shard_map/pack/pallas_call | solution.py:236
  4.0 3.1 %collective-permute-start = (bf16[16,3072]{1,0:T(8,128)(2,1)S(1)}, bf16[16,3072]{1,0:T(8,128)(2,1)S(1)}, u32[]{:S(2)}, u32[]{:S(2)}) collective-permute-start(bf16[16,3072]{1,0:T(8,128)(2,1)S(1)} %get-tuple-element.8.refs_0_), channel_id=1, source_target_pairs={{0,4},{1,5},{2,6},{3,7},{4,0},{5,1},{6,2},{7,3},{8,12},{9,13},{10,... | collective-permute-start | bytes 294920 | tf_op jit(solution)/shard_map/ppermute | solution.py:265
  7.1 2.6 %collective-permute-start.1 = (bf16[16,3072]{1,0:T(8,128)(2,1)S(1)}, bf16[16,3072]{1,0:T(8,128)(2,1)S(1)}, u32[]{:S(2)}, u32[]{:S(2)}) collective-permute-start(bf16[16,3072]{1,0:T(8,128)(2,1)S(1)} %get-tuple-element.8.refs_0_), channel_id=1, source_target_pairs={{0,8},{1,9},{2,10},{3,11},{4,12},{5,13},{6,14},{7,15},{8,0},{9,1},... | collective-permute-start | bytes 294920 | tf_op jit(solution)/shard_map/ppermute | solution.py:265
  9.7 0.0 collective-permute-start.2
  9.7 0.0 collective-permute-start.4
  9.7 0.5 collective-permute-start.5
  10.2 6.2 %all-to-all-start = ((bf16[16,8,2304]{2,1,0:T(8,128)(2,1)}), bf16[16,8,2304]{2,1,0:T(8,128)(2,1)S(1)}, u32[]{:S(2)}, u32[]{:S(2)}) async-start(bf16[16,8,2304]{2,1,0:T(8,128)(2,1)} %bitcast.1), calls=%async_computation | async-start | bytes 1179648 | tf_op jit(solution)/shard_map/all_to_all | solution.py:278
  17.1 0.0 collective-permute-done.refs_1_
  17.1 0.5 collective-permute-done.1.refs_2_
  17.6 0.0 collective-permute-done.2.refs_3_
  17.6 1.6 %collective-permute-start.3 = (bf16[64,1536]{1,0:T(8,128)(2,1)S(1)}, bf16[64,1536]{1,0:T(8,128)(2,1)S(1)}, u32[]{:S(2)}, u32[]{:S(2)}) collective-permute-start(bf16[64,1536]{1,0:T(8,128)(2,1)S(1)} %pad_maximum_fusion.1), channel_id=1, source_target_pairs={{0,2},{1,3},{2,0},{3,1},{4,6},{5,7},{6,4},{7,5},{8,10},{9,11},{10,... | collective-permute-start | bytes 589832 | tf_op jit(solution)/shard_map/ppermute | solution.py:265
  19.2 0.0 collective-permute-done.5.refs_7_.refs_4_
  19.2 0.0 collective-permute-done.4.refs_5_.refs_2_
  19.2 2.1 %text.2.refs_0_ = bf16[64,1664]{1,0:T(8,128)(2,1)S(1)} custom-call(s32[1]{0:T(128)S(6)} %copy.7.length_ref, bf16[16,3072]{1,0:T(8,128)(2,1)S(1)} %get-tuple-element.8.refs_0_, bf16[16,3072]{1,0:T(8,128)(2,1)S(1)} %collective-permute-done.refs_1_, bf16[16,3072]{1,0:T(8,128)(2,1)S(1)} %collective-permute-done.1.refs_2_, ...), custom_call_target="tpu_custom_call" | custom-call | flops 113246208 | bytes 3260416 | tf_op jit(solution)/shard_map/text/pallas_call | solution.py:236
  21.3 7.1 %collective-permute-done.3.refs_0_ = bf16[64,1536]{1,0:T(8,128)(2,1)S(1)} collective-permute-done((bf16[64,1536]{1,0:T(8,128)(2,1)S(1)}, bf16[64,1536]{1,0:T(8,128)(2,1)S(1)}, u32[]{:S(2)}, u32[]{:S(2)}) %collective-permute-start.3) | collective-permute-done | bytes 196640 | tf_op jit(solution)/shard_map/ppermute | solution.py:265
  28.5 2.1 %text.3 = bf16[64,1664]{1,0:T(8,128)(2,1)S(1)} custom-call(s32[1]{0:T(128)S(6)} %copy.7.length_ref, bf16[64,1536]{1,0:T(8,128)(2,1)S(1)} %collective-permute-done.3.refs_0_, bf16[3,128,1536]{2,1,0:T(8,128)(2,1)} %bitcast.video_ref.refs_4_.refs_1_, bf16[3,128,1536]{2,1,0:T(8,128)(2,1)S(1)} %collective-permute-done.4.refs_5_.refs_2_, ...), custom_call_target="tpu_custom_call" | custom-call | flops 113246208 | bytes 3063808 | tf_op jit(solution)/shard_map/text/pallas_call | solution.py:236
  30.6 1.3 %collective-permute-start.8 = (bf16[64,1664]{1,0:T(8,128)(2,1)S(1)}, bf16[64,1664]{1,0:T(8,128)(2,1)S(1)}, u32[]{:S(2)}, u32[]{:S(2)}) collective-permute-start(bf16[64,1664]{1,0:T(8,128)(2,1)S(1)} %text.3), channel_id=1, source_target_pairs={{0,2},{1,3},{2,0},{3,1},{4,6},{5,7},{6,4},{7,5},{8,10},{9,11},{10,... | collective-permute-start | bytes 638984 | tf_op jit(solution)/shard_map/ppermute | solution.py:265
  31.9 0.8 %collective-permute-start.6 = (bf16[64,1536]{1,0:T(8,128)(2,1)S(1)}, bf16[64,1536]{1,0:T(8,128)(2,1)S(1)}, u32[]{:S(2)}, u32[]{:S(2)}) collective-permute-start(bf16[64,1536]{1,0:T(8,128)(2,1)S(1)} %pad_maximum_fusion), channel_id=1, source_target_pairs={{0,2},{1,3},{2,0},{3,1},{4,6},{5,7},{6,4},{7,5},{8,10},{9,11},{10,... | collective-permute-start | bytes 589832 | tf_op jit(solution)/shard_map/ppermute | solution.py:265
  32.7 0.0 all-to-all-done
  32.7 1.2 %temporal.1 = bf16[128,768]{1,0:T(8,128)(2,1)} custom-call(bf16[128,2304]{1,0:T(8,128)(2,1)S(1)} %bitcast.6), custom_call_target="tpu_custom_call" | custom-call | flops 50331648 | bytes 786432 | tf_op jit(solution)/shard_map/temporal/pallas_call | solution.py:236
  33.9 0.0 copy-start.1
  33.9 5.6 %all-to-all-start.1 = ((bf16[16,8,768]{2,1,0:T(8,128)(2,1)}), bf16[16,8,768]{2,1,0:T(8,128)(2,1)S(1)}, u32[]{:S(2)}, u32[]{:S(2)}) async-start(bf16[16,8,768]{2,1,0:T(8,128)(2,1)} %bitcast.3), calls=%async_computation.1 | async-start | bytes 393216 | tf_op jit(solution)/shard_map/all_to_all | solution.py:357
  39.5 2.2 %collective-permute-done.6 = bf16[64,1536]{1,0:T(8,128)(2,1)S(1)} collective-permute-done((bf16[64,1536]{1,0:T(8,128)(2,1)S(1)}, bf16[64,1536]{1,0:T(8,128)(2,1)S(1)}, u32[]{:S(2)}, u32[]{:S(2)}) %collective-permute-start.6) | collective-permute-done | bytes 196640 | tf_op jit(solution)/shard_map/ppermute | solution.py:265
  41.7 0.1 collective-permute-start.7
  41.8 0.0 collective-permute-done.8.refs_1_
  41.8 0.5 merge.1
  42.3 2.3 %collective-permute-start.10 = (bf16[16,1664]{1,0:T(8,128)(2,1)S(1)}, bf16[16,1664]{1,0:T(8,128)(2,1)S(1)}, u32[]{:S(2)}, u32[]{:S(2)}) collective-permute-start(bf16[16,1664]{1,0:T(8,128)(2,1)S(1)} %get-tuple-element.15), channel_id=1, source_target_pairs={{0,8},{1,9},{2,10},{3,11},{4,12},{5,13},{6,14},{7,15},{8,0},{9,1},... | collective-permute-start | bytes 159752 | tf_op jit(solution)/shard_map/ppermute | solution.py:265
  44.6 2.0 %collective-permute-start.11 = (bf16[16,1664]{1,0:T(8,128)(2,1)S(1)}, bf16[16,1664]{1,0:T(8,128)(2,1)S(1)}, u32[]{:S(2)}, u32[]{:S(2)}) collective-permute-start(bf16[16,1664]{1,0:T(8,128)(2,1)S(1)} %get-tuple-element.14), channel_id=1, source_target_pairs={{0,12},{1,13},{2,14},{3,15},{4,8},{5,9},{6,10},{7,11},{8,4},{9,5},... | collective-permute-start | bytes 159752 | tf_op jit(solution)/shard_map/ppermute | solution.py:265
  46.6 0.5 collective-permute-start.9
  47.1 0.0 collective-permute-done.7.far_ref
  47.1 0.0 copy-done.1
  47.1 2.0 %spatial.1.spatial_ref = bf16[128,768]{1,0:T(8,128)(2,1)S(1)} custom-call(s32[12]{0:T(128)S(1)} %copy-done.1, s32[1]{0:T(128)S(6)} %copy.7.length_ref, bf16[3,128,1536]{2,1,0:T(8,128)(2,1)} %bitcast.video_ref.refs_4_.refs_1_, bf16[128,1536]{1,0:T(8,128)(2,1)S(1)} %constant_dynamic-update-slice_fusion.near_ref, ...), custom_call_target="tpu_custom_call" | custom-call | flops 150994944 | bytes 2162688 | tf_op jit(solution)/shard_map/spatial/pallas_call | solution.py:236
  49.1 0.0 all-to-all-done.1
  49.1 1.4 %join.1 = bf16[128,1536]{1,0:T(8,128)(2,1)} custom-call(s32[12]{0:T(128)S(1)} %copy-done.1, bf16[128,768]{1,0:T(8,128)(2,1)S(1)} %spatial.1.spatial_ref, bf16[128,768]{1,0:T(8,128)(2,1)S(1)} %bitcast.7), custom_call_target="tpu_custom_call" | custom-call | bytes 786432 | tf_op jit(solution)/shard_map/join/pallas_call | solution.py:236
  50.5 1.1 %collective-permute-done.10.refs_2_ = bf16[16,1664]{1,0:T(8,128)(2,1)S(1)} collective-permute-done((bf16[16,1664]{1,0:T(8,128)(2,1)S(1)}, bf16[16,1664]{1,0:T(8,128)(2,1)S(1)}, u32[]{:S(2)}, u32[]{:S(2)}) %collective-permute-start.10) | collective-permute-done | bytes 53280 | tf_op jit(solution)/shard_map/ppermute | solution.py:265
  51.6 0.0 collective-permute-done.11.refs_3_
  51.6 0.6 %collective-permute-done.9.refs_1_ = bf16[16,1664]{1,0:T(8,128)(2,1)S(1)} collective-permute-done((bf16[16,1664]{1,0:T(8,128)(2,1)S(1)}, bf16[16,1664]{1,0:T(8,128)(2,1)S(1)}, u32[]{:S(2)}, u32[]{:S(2)}) %collective-permute-start.9) | collective-permute-done | bytes 53280 | tf_op jit(solution)/shard_map/ppermute | solution.py:265
  52.2 0.9 %finish.1 = bf16[16,1536]{1,0:T(8,128)(2,1)} custom-call(bf16[16,1664]{1,0:T(8,128)(2,1)S(1)} %get-tuple-element.13.refs_0_, bf16[16,1664]{1,0:T(8,128)(2,1)S(1)} %collective-permute-done.9.refs_1_, bf16[16,1664]{1,0:T(8,128)(2,1)S(1)} %collective-permute-done.10.refs_2_, bf16[16,1664]{1,0:T(8,128)(2,1)S(1)} %collective-permute-done.11.refs_3_), custom_call_target="tpu_custom_call" | custom-call | bytes 262144 | tf_op jit(solution)/shard_map/finish/pallas_call | solution.py:236
  (9 shorter events, 0.1 us)
Async XLA Ops:
  0.6 0.7 %copy-start = (s32[12]{0:T(128)S(1)}, s32[12]{0:T(128)}, u32[]{:S(2)}) copy-start(s32[12]{0:T(128)} %kind_ref.5) | copy-start | bytes 148
  4.0 13.0 %collective-permute-start = (bf16[16,3072]{1,0:T(8,128)(2,1)S(1)}, bf16[16,3072]{1,0:T(8,128)(2,1)S(1)}, u32[]{:S(2)}, u32[]{:S(2)}) collective-permute-start(bf16[16,3072]{1,0:T(8,128)(2,1)S(1)} %get-tuple-element.8.refs_0_), channel_id=1, source_target_pairs={{0,4},{1,5},{2,6},{3,7},{4,0},{5,1},{6,2},{7,3},{8,12},{9,13},{10,... | collective-permute-start | bytes 294920 | tf_op jit(solution)/shard_map/ppermute | solution.py:265
  7.1 10.4 %collective-permute-start.1 = (bf16[16,3072]{1,0:T(8,128)(2,1)S(1)}, bf16[16,3072]{1,0:T(8,128)(2,1)S(1)}, u32[]{:S(2)}, u32[]{:S(2)}) collective-permute-start(bf16[16,3072]{1,0:T(8,128)(2,1)S(1)} %get-tuple-element.8.refs_0_), channel_id=1, source_target_pairs={{0,8},{1,9},{2,10},{3,11},{4,12},{5,13},{6,14},{7,15},{8,0},{9,1},... | collective-permute-start | bytes 294920 | tf_op jit(solution)/shard_map/ppermute | solution.py:265
  9.7 7.8 %collective-permute-start.2 = (bf16[16,3072]{1,0:T(8,128)(2,1)S(1)}, bf16[16,3072]{1,0:T(8,128)(2,1)S(1)}, u32[]{:S(2)}, u32[]{:S(2)}) collective-permute-start(bf16[16,3072]{1,0:T(8,128)(2,1)S(1)} %get-tuple-element.8.refs_0_), channel_id=1, source_target_pairs={{0,12},{1,13},{2,14},{3,15},{4,8},{5,9},{6,10},{7,11},{8,4},{9,5},... | collective-permute-start | bytes 294920 | tf_op jit(solution)/shard_map/ppermute | solution.py:265
  9.7 9.5 %collective-permute-start.4 = (bf16[3,128,1536]{2,1,0:T(8,128)(2,1)}, bf16[3,128,1536]{2,1,0:T(8,128)(2,1)S(1)}, u32[]{:S(2)}, u32[]{:S(2)}) collective-permute-start(bf16[3,128,1536]{2,1,0:T(8,128)(2,1)} %bitcast.video_ref.refs_4_.refs_1_), channel_id=1, source_target_pairs={{0,1},{1,0},{2,3},{3,2},{4,5},{5,4},{6,7},{7,6},{8,9},{9,8},{10,11... | collective-permute-start | bytes 3538952 | tf_op jit(solution)/shard_map/ppermute | solution.py:265
  9.7 9.5 %collective-permute-start.5 = (bf16[3,16,1536]{2,1,0:T(8,128)(2,1)}, bf16[3,16,1536]{2,1,0:T(8,128)(2,1)S(1)}, u32[]{:S(2)}, u32[]{:S(2)}) collective-permute-start(bf16[3,16,1536]{2,1,0:T(8,128)(2,1)} %refs_3_.1), channel_id=1, source_target_pairs={{0,1},{1,0},{2,3},{3,2},{4,5},{5,4},{6,7},{7,6},{8,9},{9,8},{10,11... | collective-permute-start | bytes 442376 | tf_op jit(solution)/shard_map/ppermute | solution.py:265
  10.2 22.4 %all-to-all-start = ((bf16[16,8,2304]{2,1,0:T(8,128)(2,1)}), bf16[16,8,2304]{2,1,0:T(8,128)(2,1)S(1)}, u32[]{:S(2)}, u32[]{:S(2)}) async-start(bf16[16,8,2304]{2,1,0:T(8,128)(2,1)} %bitcast.1), calls=%async_computation | async-start | bytes 1179648 | tf_op jit(solution)/shard_map/all_to_all | solution.py:278
  17.6 10.9 %collective-permute-start.3 = (bf16[64,1536]{1,0:T(8,128)(2,1)S(1)}, bf16[64,1536]{1,0:T(8,128)(2,1)S(1)}, u32[]{:S(2)}, u32[]{:S(2)}) collective-permute-start(bf16[64,1536]{1,0:T(8,128)(2,1)S(1)} %pad_maximum_fusion.1), channel_id=1, source_target_pairs={{0,2},{1,3},{2,0},{3,1},{4,6},{5,7},{6,4},{7,5},{8,10},{9,11},{10,... | collective-permute-start | bytes 589832 | tf_op jit(solution)/shard_map/ppermute | solution.py:265
  30.6 11.2 %collective-permute-start.8 = (bf16[64,1664]{1,0:T(8,128)(2,1)S(1)}, bf16[64,1664]{1,0:T(8,128)(2,1)S(1)}, u32[]{:S(2)}, u32[]{:S(2)}) collective-permute-start(bf16[64,1664]{1,0:T(8,128)(2,1)S(1)} %text.3), channel_id=1, source_target_pairs={{0,2},{1,3},{2,0},{3,1},{4,6},{5,7},{6,4},{7,5},{8,10},{9,11},{10,... | collective-permute-start | bytes 638984 | tf_op jit(solution)/shard_map/ppermute | solution.py:265
  31.9 9.7 %collective-permute-start.6 = (bf16[64,1536]{1,0:T(8,128)(2,1)S(1)}, bf16[64,1536]{1,0:T(8,128)(2,1)S(1)}, u32[]{:S(2)}, u32[]{:S(2)}) collective-permute-start(bf16[64,1536]{1,0:T(8,128)(2,1)S(1)} %pad_maximum_fusion), channel_id=1, source_target_pairs={{0,2},{1,3},{2,0},{3,1},{4,6},{5,7},{6,4},{7,5},{8,10},{9,11},{10,... | collective-permute-start | bytes 589832 | tf_op jit(solution)/shard_map/ppermute | solution.py:265
  33.9 13.2 %copy-start.1 = (s32[12]{0:T(128)S(1)}, s32[12]{0:T(128)}, u32[]{:S(2)}) copy-start(s32[12]{0:T(128)} %kind_ref.5) | copy-start | bytes 148
  33.9 15.2 %all-to-all-start.1 = ((bf16[16,8,768]{2,1,0:T(8,128)(2,1)}), bf16[16,8,768]{2,1,0:T(8,128)(2,1)S(1)}, u32[]{:S(2)}, u32[]{:S(2)}) async-start(bf16[16,8,768]{2,1,0:T(8,128)(2,1)} %bitcast.3), calls=%async_computation.1 | async-start | bytes 393216 | tf_op jit(solution)/shard_map/all_to_all | solution.py:357
  41.7 5.4 %collective-permute-start.7 = (bf16[128,1536]{1,0:T(8,128)(2,1)S(1)}, bf16[128,1536]{1,0:T(8,128)(2,1)S(1)}, u32[]{:S(2)}, u32[]{:S(2)}) collective-permute-start(bf16[128,1536]{1,0:T(8,128)(2,1)S(1)} %constant_dynamic-update-slice_fusion.near_ref), channel_id=1, source_target_pairs={{0,1},{1,0},{2,3},{3,2},{4,5},{5,4},{6,7},{7,6},{8,9},{9,8},{10,11... | collective-permute-start | bytes 1179656 | tf_op jit(solution)/shard_map/ppermute | solution.py:265
  42.3 9.3 %collective-permute-start.10 = (bf16[16,1664]{1,0:T(8,128)(2,1)S(1)}, bf16[16,1664]{1,0:T(8,128)(2,1)S(1)}, u32[]{:S(2)}, u32[]{:S(2)}) collective-permute-start(bf16[16,1664]{1,0:T(8,128)(2,1)S(1)} %get-tuple-element.15), channel_id=1, source_target_pairs={{0,8},{1,9},{2,10},{3,11},{4,12},{5,13},{6,14},{7,15},{8,0},{9,1},... | collective-permute-start | bytes 159752 | tf_op jit(solution)/shard_map/ppermute | solution.py:265
  44.6 7.0 %collective-permute-start.11 = (bf16[16,1664]{1,0:T(8,128)(2,1)S(1)}, bf16[16,1664]{1,0:T(8,128)(2,1)S(1)}, u32[]{:S(2)}, u32[]{:S(2)}) collective-permute-start(bf16[16,1664]{1,0:T(8,128)(2,1)S(1)} %get-tuple-element.14), channel_id=1, source_target_pairs={{0,12},{1,13},{2,14},{3,15},{4,8},{5,9},{6,10},{7,11},{8,4},{9,5},... | collective-permute-start | bytes 159752 | tf_op jit(solution)/shard_map/ppermute | solution.py:265
  46.6 5.6 %collective-permute-start.9 = (bf16[16,1664]{1,0:T(8,128)(2,1)S(1)}, bf16[16,1664]{1,0:T(8,128)(2,1)S(1)}, u32[]{:S(2)}, u32[]{:S(2)}) collective-permute-start(bf16[16,1664]{1,0:T(8,128)(2,1)S(1)} %get-tuple-element.16), channel_id=1, source_target_pairs={{0,4},{1,5},{2,6},{3,7},{4,0},{5,1},{6,2},{7,3},{8,12},{9,13},{10,... | collective-permute-start | bytes 159752 | tf_op jit(solution)/shard_map/ppermute | solution.py:265

commit v3 on v2

--- a/solution.py
+++ b/solution.py
@@ -31,30 +31,67 @@
 
 
 def pack_kernel(
-    head_count, kind_ref, text_ref, video_ref, packed_ref, temporal_ref, list_ref, text_here, video_here, sems
+    head_count,
+    kind_ref,
+    text_ref,
+    video_ref,
+    packed_ref,
+    temporal_ref,
+    list_ref,
+    kind_here,
+    text_here,
+    video_here,
+    packed_here,
+    temporal_here,
+    in_sems,
+    out_sems,
 ):
-    copies = [pltpu.make_async_copy(text_ref, text_here, sems.at[3])]
+    half = head_count // 2
+    width = head_count * lanes
+    copies = [
+        pltpu.make_async_copy(kind_ref, kind_here, in_sems.at[0]),
+        pltpu.make_async_copy(text_ref, text_here, in_sems.at[1]),
+    ]
     for part in range(3):
         copies.append(
-            pltpu.make_async_copy(video_ref.at[part], video_here.at[part], sems.at[part])
+            pltpu.make_async_copy(video_ref.at[part], video_here.at[part], in_sems.at[part + 2])
         )
     for copy in copies:
         copy.start()
-    list_heads(kind_ref, list_ref, head_count)
-    half = head_count // 2
     copies[0].wait()
-    packed_ref[:, : head_count * lanes] = text_here[0]
+    list_heads(kind_here, list_ref, head_count)
+    copies[1].wait()
+    packed_here[:, :width] = text_here[0]
     for slot in range(half):
         for part in range(2):
-            packed_ref[:, head_lanes(head_count + part * half + slot)] = text_here[
+            packed_here[:, head_lanes(head_count + part * half + slot)] = text_here[
                 part + 1, :, head_lanes(list_ref[slot])
             ]
+    sends = [pltpu.make_async_copy(packed_here, packed_ref, out_sems.at[0])]
+    sends[0].start()
     for part in range(3):
-        copies[part + 1].wait()
+        copies[part + 2].wait()
         for slot in range(half):
-            temporal_ref[:, head_lanes(part * half + slot)] = video_here[
+            temporal_here[:, head_lanes(part * half + slot)] = video_here[
                 part, :, head_lanes(list_ref[head_count + slot])
             ]
+        span = pl.ds(part * half * lanes, half * lanes)
+        sends.append(
+            pltpu.make_async_copy(
+                temporal_here.at[:, span], temporal_ref.at[:, span], out_sems.at[part + 1]
+            )
+        )
+        sends[-1].start()
+    for send in sends:
+        send.wait()
+
+
+def stack_kernel(*refs):
+    for half, out_ref in enumerate(refs[-2:]):
+        width = out_ref.shape[1]
+        out_ref[...] = jnp.concatenate(
+            [ref[:, pl.ds(half * width, width)] for ref in refs[:-2]], axis=0
+        )
 
 
 def temporal_kernel(half, stride, scale, block_ref, out_ref, score_ref, weight_ref):
@@ -89,17 +126,14 @@
     kind_ref,
     length_ref,
     video_ref,
-    near_ref,
-    far_ref,
-    out_ref,
-    list_ref,
-    score_ref,
-    weight_ref,
+    *refs,
 ):
+    text_refs = refs[:-4]
+    out_ref, list_ref, score_ref, weight_ref = refs[-4:]
     list_heads(kind_ref, list_ref, head_count)
     half = head_count // 2
     positions = video_ref.shape[1]
-    text_total = near_ref.shape[0] + far_ref.shape[0]
+    text_total = sum(ref.shape[0] for ref in text_refs)
     index = lax.broadcasted_iota(jnp.int32, (8, text_total), 1)
     if relative:
         block = index // shard
@@ -110,11 +144,8 @@
 
     def gathered(part, slot):
         return jnp.concatenate(
-            [
-                video_ref[part + 1, :, head_lanes(list_ref[slot])],
-                near_ref[:, head_lanes(part * half + slot)],
-                far_ref[:, head_lanes(part * half + slot)],
-            ],
+            [video_ref[part + 1, :, head_lanes(list_ref[slot])]]
+            + [ref[:, head_lanes(part * half + slot)] for ref in text_refs],
             axis=0,
         )
 
@@ -230,7 +261,7 @@
     return lax.optimization_barrier((array, *others))[0]
 
 
-def call(kernel, name, out, scalars, arrays, scratch=(), flops=0, space=pltpu.VMEM):
+def call(kernel, name, out, scalars, arrays, scratch=(), flops=0, space=pltpu.VMEM, out_space=pltpu.VMEM, limit=32):
     outs = [jax.ShapeDtypeStruct(shape, jnp.bfloat16) for shape in out]
     moved = sum(a.size * 2 for a in arrays) + sum(o.size * 2 for o in outs)
     return pl.pallas_call(
@@ -238,9 +269,9 @@
         out_shape=outs,
         in_specs=[pl.BlockSpec(memory_space=pltpu.SMEM)] * len(scalars)
         + [pl.BlockSpec(memory_space=space)] * len(arrays),
-        out_specs=[pl.BlockSpec(memory_space=pltpu.VMEM)] * len(outs),
+        out_specs=[pl.BlockSpec(memory_space=out_space)] * len(outs),
         scratch_shapes=scratch,
-        compiler_params=pltpu.CompilerParams(vmem_limit_bytes=32 * 2**20),
+        compiler_params=pltpu.CompilerParams(vmem_limit_bytes=limit * 2**20),
         cost_estimate=pl.CostEstimate(flops=flops, bytes_accessed=moved, transcendentals=0),
         name=name,
     )(*scalars, *arrays)
@@ -268,18 +299,24 @@
         functools.partial(pack_kernel, head_count),
         "pack",
         [(shard, 2 * width), (positions, 3 * half * lanes)],
-        [head_kind],
-        [text_qkv, video],
+        [],
+        [head_kind, text_qkv, video],
         head_list
+        + [pltpu.SMEM(head_kind.shape, jnp.int32)]
         + [pltpu.VMEM(a.shape, a.dtype) for a in (text_qkv, video)]
-        + [pltpu.SemaphoreType.DMA((4,))],
+        + [pltpu.VMEM((shard, 2 * width), jnp.bfloat16)]
+        + [pltpu.VMEM((positions, 3 * half * lanes), jnp.bfloat16)]
+        + [pltpu.SemaphoreType.DMA((5,)), pltpu.SemaphoreType.DMA((4,))],
         space=pl.ANY,
+        out_space=pl.ANY,
+        limit=60,
     )
     block = lax.all_to_all(packed_video, "frame", split_axis=0, concat_axis=0, tiled=True)
 
     text_rows = -(-shard // 16) * 16
     text = jnp.pad(text_qkv, ((0, 0), (0, text_rows - shard), (0, 0)))
-    keys = [video, swap(video, 1), text, swap(text, 1)]
+    other_text = swap(text, 1)
+    keys = [video, swap(video, 1), text, other_text]
 
     def attend(queries):
         rows = sum(q.shape[0] for q in queries)
@@ -294,25 +331,40 @@
             flops=4 * rows * width * key_count,
         )[0]
 
+    def attend_temporal(received):
+        return call(
+            functools.partial(temporal_kernel, half, positions // devices, scale),
+            "temporal",
+            [(positions, half * lanes)],
+            [],
+            [received],
+            score_scratch(half, positions, positions),
+            flops=4 * positions * half * lanes * positions,
+        )
+
     if relative:
         column = [packed_text] + [swap(packed_text, 4 * step) for step in (1, 2, 3)]
-        across = swap(jnp.concatenate([c[:, :width] for c in column], axis=0), 2)
-        kept = attend(column)
+        queries_column, keys_column = call(
+            stack_kernel, "stack", [(4 * shard, width)] * 2, [], column, flops=20000000000
+        )
+        across = swap(queries_column, 2)
+        kept = attend([queries_column])
         across = after(across, kept)
         partial_sums = attend([across])
         sent = swap(partial_sums, 2)
-        block = after(block, partial_sums)
+        (result,) = attend_temporal(after(block, partial_sums))
+        sent = after(sent, result)
         (joined,) = call(
             functools.partial(merge_kernel, head_count), "merge", [kept.shape], [], [kept, sent]
         )
         pieces = [joined[:shard]] + [
             swap(joined[step * shard : (step + 1) * shard], 4 * step) for step in (1, 2, 3)
         ]
-        keys_column = jnp.concatenate([c[:, width:] for c in column], axis=0)
-        keys_column = after(keys_column, partial_sums)
-        near_keys = jnp.concatenate([keys_column, swap(keys_column, 2)], axis=0)
-        far_keys = swap(near_keys, 1)
+        across_keys = swap(after(keys_column, result), 2)
+        across_keys = after(across_keys, joined)
+        text_keys = [keys_column, across_keys, swap(keys_column, 1), swap(across_keys, 1)]
     else:
+        (result,) = attend_temporal(block)
         side = [[2 * chip + core for chip in range(devices // 2)] for core in range(2)]
         gathered = lax.all_gather(
             packed_text[:, :width], "frame", axis=0, tiled=True, axis_index_groups=side
@@ -328,7 +380,7 @@
             [summed / total for _, total, summed in merge(head_count, blocks)], axis=1
         ).astype(jnp.bfloat16)
         all_keys = lax.all_gather(packed_text[:, width:], "frame", axis=0, tiled=True)
-        near_keys, far_keys = jnp.split(all_keys, 2, axis=0)
+        text_keys = [all_keys]
 
     key_count = positions + devices * shard
     (spatial,) = call(
@@ -336,7 +388,7 @@
         "spatial",
         [(positions, half * lanes)],
         [head_kind, text_len],
-        [video, near_keys, far_keys],
+        [video, *text_keys],
         head_list + score_scratch(half, positions, key_count),
         flops=4 * positions * half * lanes * key_count,
     )
@@ -345,15 +397,6 @@
         (text_out,) = call(
             functools.partial(finish_kernel, head_count), "finish", [(shard, width)], [], pieces
         )
-    (result,) = call(
-        functools.partial(temporal_kernel, half, positions // devices, scale),
-        "temporal",
-        [(positions, half * lanes)],
-        [],
-        [block],
-        score_scratch(half, positions, positions),
-        flops=4 * positions * half * lanes * positions,
-    )
     temporal = lax.all_to_all(result, "frame", split_axis=0, concat_axis=0, tiled=True)
     (video_out,) = call(
         functools.partial(join_kernel, head_count),

time: 53.5 us -> 50.9 us (0.951)
  Pallas kernels: 13 us -> 9.15 us
  waiting for transfers between devices: 11.5 us -> 14.4 us
  starting transfers between devices: 26.4 us -> 24.8 us
    pallas_call x8 -> x9, Pallas kernels: 13 us -> 9.15 us  [call(): pl.pallas_call(kernel, out_shape=outs, in_specs=[pl.BlockSpec(memory_spac...]
    all_to_all x1, waiting for transfers between devices: 0.01 us -> 1.65 us  [body(): lax.all_to_all(result, 'frame', split_axis=0, concat_axis=0, tiled=True)]
    all_to_all x1, waiting for transfers between devices: 0.01 us -> 1.38 us  [body(): lax.all_to_all(packed_video, 'frame', split_axis=0, concat_axis=0, tiled=...]
    all_to_all x1, starting transfers between devices: 5.57 us -> 4.58 us  [body(): lax.all_to_all(result, 'frame', split_axis=0, concat_axis=0, tiled=True)]
    ppermute x12 -> x13, starting transfers between devices: 14.7 us -> 14 us  [swap(): return lax.ppermute(array, 'frame', [(i, i ^ bits) for i in range(devices)])]
    ppermute x12 -> x13, waiting for transfers between devices: 11.5 us -> 11.4 us  [swap(): return lax.ppermute(array, 'frame', [(i, i ^ bits) for i in range(devices)])]
  transfers between devices with their start and end apart: 14 -> 15, of which waited for: 5 -> 8; matrix products, arithmetic and copies ran while one was open for 0% -> 0% of each run, Pallas kernels for 18% -> 12%
where the time goes in v3:
time: 50.9 us; the launch traced here: 50.5 us
  starting transfers between devices  24.8 us (49%)
  waiting for transfers between devices  14.4 us (28%)
  Pallas kernels  9.15 us (18%)
  between operations  1.43 us (3%)
  local copies, waits for them, and re-layouts  0.72 us (1%)
    ppermute x13, starting transfers between devices, swap(): return lax.ppermute(array, 'frame', [(i, i ^ bits) for i in range(devices)])  14 us
    ppermute x13, waiting for transfers between devices, swap(): return lax.ppermute(array, 'frame', [(i, i ^ bits) for i in range(devices)])  11.4 us
    pallas_call x9, Pallas kernels, call(): pl.pallas_call(kernel, out_shape=outs, in_specs=[pl.BlockSpec(memory_spac...  9.15 us
    all_to_all x1, starting transfers between devices, body(): lax.all_to_all(packed_video, 'frame', split_axis=0, concat_axis=0, tiled=...  6.27 us
    all_to_all x1, starting transfers between devices, body(): lax.all_to_all(result, 'frame', split_axis=0, concat_axis=0, tiled=True)  4.58 us
    all_to_all x1, waiting for transfers between devices, body(): lax.all_to_all(result, 'frame', split_axis=0, concat_axis=0, tiled=True)  1.65 us
    all_to_all x1, waiting for transfers between devices, body(): lax.all_to_all(packed_video, 'frame', split_axis=0, concat_axis=0, tiled=...  1.38 us
  transfers between devices with their start and end apart: 15, of which 8 were waited for; matrix products, arithmetic and copies ran while one was open for 0% of the time, Pallas kernels for 12%

profile of v3, /device:TPU:0, one launch (start us, length us, event | category | flops | bytes accessed | tf_op | source)
XLA Modules:
  0.0 50.5 jit_solution(6816580694528437378)
XLA Ops:
  0.6 0.0 copy-start
  0.6 2.2 %pack.1 = (bf16[16,3072]{1,0:T(8,128)(2,1)}, bf16[128,2304]{1,0:T(8,128)(2,1)}) custom-call(s32[12]{0:T(128)} %kind_ref.5, bf16[3,16,1536]{2,1,0:T(8,128)(2,1)} %refs_3_.3, bf16[3,128,1536]{2,1,0:T(8,128)(2,1)} %bitcast.6), custom_call_target="tpu_custom_call" | custom-call | bytes 2015256 | tf_op jit(solution)/shard_map/pack/pallas_call | solution.py:267
  2.8 0.0 copy-start.5
  2.9 3.1 %collective-permute-start = (bf16[16,3072]{1,0:T(8,128)(2,1)}, bf16[16,3072]{1,0:T(8,128)(2,1)S(1)}, u32[]{:S(2)}, u32[]{:S(2)}) collective-permute-start(bf16[16,3072]{1,0:T(8,128)(2,1)} %get-tuple-element.12.refs_0_), channel_id=1, source_target_pairs={{0,4},{1,5},{2,6},{3,7},{4,0},{5,1},{6,2},{7,3},{8,12},{9,13},{10,... | collective-permute-start | bytes 294920 | tf_op jit(solution)/shard_map/ppermute | solution.py:296
  5.9 2.6 %collective-permute-start.1 = (bf16[16,3072]{1,0:T(8,128)(2,1)}, bf16[16,3072]{1,0:T(8,128)(2,1)S(1)}, u32[]{:S(2)}, u32[]{:S(2)}) collective-permute-start(bf16[16,3072]{1,0:T(8,128)(2,1)} %get-tuple-element.12.refs_0_), channel_id=1, source_target_pairs={{0,8},{1,9},{2,10},{3,11},{4,12},{5,13},{6,14},{7,15},{8,0},{9,1},... | collective-permute-start | bytes 294920 | tf_op jit(solution)/shard_map/ppermute | solution.py:296
  8.5 0.0 collective-permute-start.2
  8.5 0.0 copy-done
  8.5 0.0 collective-permute-start.4
  8.5 6.3 %all-to-all-start = ((bf16[16,8,2304]{2,1,0:T(8,128)(2,1)}), bf16[16,8,2304]{2,1,0:T(8,128)(2,1)S(1)}, u32[]{:S(2)}, u32[]{:S(2)}) async-start(bf16[16,8,2304]{2,1,0:T(8,128)(2,1)} %bitcast.13), calls=%async_computation | async-start | bytes 1179648 | tf_op jit(solution)/shard_map/all_to_all | solution.py:314
  14.8 0.0 copy-start.1
  14.8 0.0 collective-permute-done.refs_1_
  14.8 1.8 %collective-permute-done.1.refs_2_ = bf16[16,3072]{1,0:T(8,128)(2,1)S(1)} collective-permute-done((bf16[16,3072]{1,0:T(8,128)(2,1)}, bf16[16,3072]{1,0:T(8,128)(2,1)S(1)}, u32[]{:S(2)}, u32[]{:S(2)}) %collective-permute-start.1) | collective-permute-done | bytes 98336 | tf_op jit(solution)/shard_map/ppermute | solution.py:296
  16.6 0.0 collective-permute-done.2.refs_3_
  16.6 0.0 copy-done.5
  16.6 0.0 copy-start.2
  16.6 0.7 %copy-done.2 = bf16[64,1536]{1,0:T(8,128)(2,1)} copy-done((bf16[64,1536]{1,0:T(8,128)(2,1)}, bf16[64,1536]{1,0:T(8,128)(2,1)S(1)}, u32[]{:S(2)}) %copy-start.2) | copy-done | bytes 196632
  17.3 1.5 %collective-permute-start.3 = (bf16[64,1536]{1,0:T(8,128)(2,1)S(1)}, bf16[64,1536]{1,0:T(8,128)(2,1)S(1)}, u32[]{:S(2)}, u32[]{:S(2)}) collective-permute-start(bf16[64,1536]{1,0:T(8,128)(2,1)S(1)} %get-tuple-element.15.refs_0_), channel_id=1, source_target_pairs={{0,2},{1,3},{2,0},{3,1},{4,6},{5,7},{6,4},{7,5},{8,10},{9,11},{10,... | collective-permute-start | bytes 589832 | tf_op jit(solution)/shard_map/ppermute | solution.py:296
  18.8 0.0 copy-done.1
  18.8 0.0 collective-permute-start.5
  19.5 0.7 %collective-permute-done.5.refs_4_ = bf16[3,16,1536]{2,1,0:T(8,128)(2,1)S(1)} collective-permute-done((bf16[3,16,1536]{2,1,0:T(8,128)(2,1)S(1)}, bf16[3,16,1536]{2,1,0:T(8,128)(2,1)S(1)}, u32[]{:S(2)}, u32[]{:S(2)}) %collective-permute-start.5) | collective-permute-done | bytes 147488 | tf_op jit(solution)/shard_map/ppermute | solution.py:296
  20.2 0.0 collective-permute-done.4.refs_2_
  20.2 0.8 %text.2.refs_0_ = bf16[64,1664]{1,0:T(8,128)(2,1)S(1)} custom-call(s32[1]{0:T(128)S(6)} %copy.6.length_ref, bf16[64,1536]{1,0:T(8,128)(2,1)S(1)} %get-tuple-element.15.refs_0_, bf16[3,128,1536]{2,1,0:T(8,128)(2,1)S(1)} %bitcast.8, bf16[3,128,1536]{2,1,0:T(8,128)(2,1)S(1)} %collective-permute-done.4.refs_2_, bf16[3,16,1536]{2,1,0:T(8,128)(2,1)S(1)} %copy-done.1, ...), custom_call_target="tpu_custom_call" | custom-call | flops 113246208 | bytes 3063808 | tf_op jit(solution)/shard_map/text/pallas_call | solution.py:267
  21.0 5.9 %collective-permute-done.3.refs_0_ = bf16[64,1536]{1,0:T(8,128)(2,1)S(1)} collective-permute-done((bf16[64,1536]{1,0:T(8,128)(2,1)S(1)}, bf16[64,1536]{1,0:T(8,128)(2,1)S(1)}, u32[]{:S(2)}, u32[]{:S(2)}) %collective-permute-start.3) | collective-permute-done | bytes 196640 | tf_op jit(solution)/shard_map/ppermute | solution.py:296
  26.9 0.8 %text.3 = bf16[64,1664]{1,0:T(8,128)(2,1)S(1)} custom-call(s32[1]{0:T(128)S(6)} %copy.6.length_ref, bf16[64,1536]{1,0:T(8,128)(2,1)S(1)} %collective-permute-done.3.refs_0_, bf16[3,128,1536]{2,1,0:T(8,128)(2,1)S(1)} %bitcast.9, bf16[3,128,1536]{2,1,0:T(8,128)(2,1)S(1)} %collective-permute-done.4.refs_2_, bf16[3,16,1536]{2,1,0:T(8,128)(2,1)S(1)} %copy-done.1, ...), custom_call_target="tpu_custom_call" | custom-call | flops 113246208 | bytes 3063808 | tf_op jit(solution)/shard_map/text/pallas_call | solution.py:267
  27.7 0.0 copy-start.3
  27.7 0.0 copy-start.4
  27.8 1.3 %collective-permute-start.7 = (bf16[64,1664]{1,0:T(8,128)(2,1)S(1)}, bf16[64,1664]{1,0:T(8,128)(2,1)S(1)}, u32[]{:S(2)}, u32[]{:S(2)}) collective-permute-start(bf16[64,1664]{1,0:T(8,128)(2,1)S(1)} %text.3), channel_id=1, source_target_pairs={{0,2},{1,3},{2,0},{3,1},{4,6},{5,7},{6,4},{7,5},{8,10},{9,11},{10,... | collective-permute-start | bytes 638984 | tf_op jit(solution)/shard_map/ppermute | solution.py:296
  29.0 1.4 %all-to-all-done = bf16[16,8,2304]{2,1,0:T(8,128)(2,1)S(1)} async-done(((bf16[16,8,2304]{2,1,0:T(8,128)(2,1)}), bf16[16,8,2304]{2,1,0:T(8,128)(2,1)S(1)}, u32[]{:S(2)}, u32[]{:S(2)}) %all-to-all-start) | async-done | bytes 589856 | tf_op jit(solution)/shard_map/all_to_all | solution.py:314
  30.4 1.2 %temporal.1 = bf16[128,768]{1,0:T(8,128)(2,1)} custom-call(bf16[128,2304]{1,0:T(8,128)(2,1)S(1)} %bitcast.11), custom_call_target="tpu_custom_call" | custom-call | flops 50331648 | bytes 786432 | tf_op jit(solution)/shard_map/temporal/pallas_call | solution.py:267
  31.6 0.5 %collective-permute-start.6 = (bf16[64,1536]{1,0:T(8,128)(2,1)}, bf16[64,1536]{1,0:T(8,128)(2,1)S(1)}, u32[]{:S(2)}, u32[]{:S(2)}) collective-permute-start(bf16[64,1536]{1,0:T(8,128)(2,1)} %copy-done.2), channel_id=1, source_target_pairs={{0,2},{1,3},{2,0},{3,1},{4,6},{5,7},{6,4},{7,5},{8,10},{9,11},{10,... | collective-permute-start | bytes 589832 | tf_op jit(solution)/shard_map/ppermute | solution.py:296
  32.1 0.5 collective-permute-start.8
  32.6 4.6 %all-to-all-start.1 = ((bf16[16,8,768]{2,1,0:T(8,128)(2,1)}), bf16[16,8,768]{2,1,0:T(8,128)(2,1)S(1)}, u32[]{:S(2)}, u32[]{:S(2)}) async-start(bf16[16,8,768]{2,1,0:T(8,128)(2,1)} %bitcast.3), calls=%async_computation.1 | async-start | bytes 393216 | tf_op jit(solution)/shard_map/all_to_all | solution.py:400
  37.2 0.0 collective-permute-done.7.refs_1_
  37.2 0.5 %merge.1 = bf16[64,1664]{1,0:T(8,128)(2,1)S(1)} custom-call(bf16[64,1664]{1,0:T(8,128)(2,1)S(1)} %text.2.refs_0_, bf16[64,1664]{1,0:T(8,128)(2,1)S(1)} %collective-permute-done.7.refs_1_), custom_call_target="tpu_custom_call" | custom-call | bytes 638976 | tf_op jit(solution)/shard_map/merge/pallas_call | solution.py:267
  37.8 1.5 %collective-permute-done.6.refs_1_ = bf16[64,1536]{1,0:T(8,128)(2,1)S(1)} collective-permute-done((bf16[64,1536]{1,0:T(8,128)(2,1)}, bf16[64,1536]{1,0:T(8,128)(2,1)S(1)}, u32[]{:S(2)}, u32[]{:S(2)}) %collective-permute-start.6) | collective-permute-done | bytes 196640 | tf_op jit(solution)/shard_map/ppermute | solution.py:296
  39.2 0.0 collective-permute-start.9
  39.3 1.6 %collective-permute-start.10 = (bf16[16,1664]{1,0:T(8,128)(2,1)S(1)}, bf16[16,1664]{1,0:T(8,128)(2,1)S(1)}, u32[]{:S(2)}, u32[]{:S(2)}) collective-permute-start(bf16[16,1664]{1,0:T(8,128)(2,1)S(1)} %get-tuple-element.24), channel_id=1, source_target_pairs={{0,4},{1,5},{2,6},{3,7},{4,0},{5,1},{6,2},{7,3},{8,12},{9,13},{10,... | collective-permute-start | bytes 159752 | tf_op jit(solution)/shard_map/ppermute | solution.py:296
  40.8 2.8 %collective-permute-start.11 = (bf16[16,1664]{1,0:T(8,128)(2,1)S(1)}, bf16[16,1664]{1,0:T(8,128)(2,1)S(1)}, u32[]{:S(2)}, u32[]{:S(2)}) collective-permute-start(bf16[16,1664]{1,0:T(8,128)(2,1)S(1)} %get-tuple-element.23), channel_id=1, source_target_pairs={{0,8},{1,9},{2,10},{3,11},{4,12},{5,13},{6,14},{7,15},{8,0},{9,1},... | collective-permute-start | bytes 159752 | tf_op jit(solution)/shard_map/ppermute | solution.py:296
  43.6 0.1 collective-permute-start.12
  43.7 0.0 collective-permute-done.8.refs_2_
  43.7 0.0 collective-permute-done.9.refs_3_
  43.7 1.3 %spatial.1.spatial_ref = bf16[128,768]{1,0:T(8,128)(2,1)S(1)} custom-call(s32[12]{0:T(128)S(1)} %copy-done.4, s32[1]{0:T(128)S(6)} %copy.6.length_ref, bf16[3,128,1536]{2,1,0:T(8,128)(2,1)S(1)} %bitcast.10, bf16[64,1536]{1,0:T(8,128)(2,1)S(1)} %copy-done.3, bf16[64,1536]{1,0:T(8,128)(2,1)S(1)} %collective-permute-done.6.refs_1_, ...), custom_call_target="tpu_custom_call" | custom-call | flops 150994944 | bytes 2162688 | tf_op jit(solution)/shard_map/spatial/pallas_call | solution.py:267
  45.0 1.6 %all-to-all-done.1 = bf16[16,8,768]{2,1,0:T(8,128)(2,1)S(1)} async-done(((bf16[16,8,768]{2,1,0:T(8,128)(2,1)}), bf16[16,8,768]{2,1,0:T(8,128)(2,1)S(1)}, u32[]{:S(2)}, u32[]{:S(2)}) %all-to-all-start.1) | async-done | bytes 196640 | tf_op jit(solution)/shard_map/all_to_all | solution.py:400
  46.7 1.4 %join.1 = bf16[128,1536]{1,0:T(8,128)(2,1)} custom-call(s32[12]{0:T(128)S(1)} %copy-done.4, bf16[128,768]{1,0:T(8,128)(2,1)S(1)} %spatial.1.spatial_ref, bf16[128,768]{1,0:T(8,128)(2,1)S(1)} %bitcast.12), custom_call_target="tpu_custom_call" | custom-call | bytes 786432 | tf_op jit(solution)/shard_map/join/pallas_call | solution.py:267
  48.1 0.0 collective-permute-done.10.refs_1_
  48.1 0.7 %collective-permute-done.11.refs_2_ = bf16[16,1664]{1,0:T(8,128)(2,1)S(1)} collective-permute-done((bf16[16,1664]{1,0:T(8,128)(2,1)S(1)}, bf16[16,1664]{1,0:T(8,128)(2,1)S(1)}, u32[]{:S(2)}, u32[]{:S(2)}) %collective-permute-start.11) | collective-permute-done | bytes 53280 | tf_op jit(solution)/shard_map/ppermute | solution.py:296
  48.8 0.9 %collective-permute-done.12.refs_3_ = bf16[16,1664]{1,0:T(8,128)(2,1)S(1)} collective-permute-done((bf16[16,1664]{1,0:T(8,128)(2,1)S(1)}, bf16[16,1664]{1,0:T(8,128)(2,1)S(1)}, u32[]{:S(2)}, u32[]{:S(2)}) %collective-permute-start.12) | collective-permute-done | bytes 53280 | tf_op jit(solution)/shard_map/ppermute | solution.py:296
  49.6 0.9 %finish.1 = bf16[16,1536]{1,0:T(8,128)(2,1)} custom-call(bf16[16,1664]{1,0:T(8,128)(2,1)S(1)} %get-tuple-element.21.refs_0_, bf16[16,1664]{1,0:T(8,128)(2,1)S(1)} %collective-permute-done.10.refs_1_, bf16[16,1664]{1,0:T(8,128)(2,1)S(1)} %collective-permute-done.11.refs_2_, bf16[16,1664]{1,0:T(8,128)(2,1)S(1)} %collective-permute-done.12.refs_3_), custom_call_target="tpu_custom_call" | custom-call | bytes 262144 | tf_op jit(solution)/shard_map/finish/pallas_call | solution.py:267
  (4 shorter events, 0.0 us)
Async XLA Ops:
  0.6 7.9 %copy-start = (bf16[3,1,128,1536]{3,2,1,0:T(8,128)(2,1)S(1)}, bf16[3,1,128,1536]{3,2,1,0:T(8,128)(2,1)}, u32[]{:S(2)}) copy-start(bf16[3,1,128,1536]{3,2,1,0:T(8,128)(2,1)} %param.4) | copy-start | bytes 3538948
  2.8 13.8 %copy-start.5 = (bf16[16,3072]{1,0:T(8,128)(2,1)S(1)}, bf16[16,3072]{1,0:T(8,128)(2,1)}, u32[]{:S(2)}) copy-start(bf16[16,3072]{1,0:T(8,128)(2,1)} %get-tuple-element.12.refs_0_) | copy-start | bytes 294916
  2.9 12.0 %collective-permute-start = (bf16[16,3072]{1,0:T(8,128)(2,1)}, bf16[16,3072]{1,0:T(8,128)(2,1)S(1)}, u32[]{:S(2)}, u32[]{:S(2)}) collective-permute-start(bf16[16,3072]{1,0:T(8,128)(2,1)} %get-tuple-element.12.refs_0_), channel_id=1, source_target_pairs={{0,4},{1,5},{2,6},{3,7},{4,0},{5,1},{6,2},{7,3},{8,12},{9,13},{10,... | collective-permute-start | bytes 294920 | tf_op jit(solution)/shard_map/ppermute | solution.py:296
  5.9 10.6 %collective-permute-start.1 = (bf16[16,3072]{1,0:T(8,128)(2,1)}, bf16[16,3072]{1,0:T(8,128)(2,1)S(1)}, u32[]{:S(2)}, u32[]{:S(2)}) collective-permute-start(bf16[16,3072]{1,0:T(8,128)(2,1)} %get-tuple-element.12.refs_0_), channel_id=1, source_target_pairs={{0,8},{1,9},{2,10},{3,11},{4,12},{5,13},{6,14},{7,15},{8,0},{9,1},... | collective-permute-start | bytes 294920 | tf_op jit(solution)/shard_map/ppermute | solution.py:296
  8.5 8.1 %collective-permute-start.2 = (bf16[16,3072]{1,0:T(8,128)(2,1)}, bf16[16,3072]{1,0:T(8,128)(2,1)S(1)}, u32[]{:S(2)}, u32[]{:S(2)}) collective-permute-start(bf16[16,3072]{1,0:T(8,128)(2,1)} %get-tuple-element.12.refs_0_), channel_id=1, source_target_pairs={{0,12},{1,13},{2,14},{3,15},{4,8},{5,9},{6,10},{7,11},{8,4},{9,5},... | collective-permute-start | bytes 294920 | tf_op jit(solution)/shard_map/ppermute | solution.py:296
  8.5 11.7 %collective-permute-start.4 = (bf16[3,128,1536]{2,1,0:T(8,128)(2,1)S(1)}, bf16[3,128,1536]{2,1,0:T(8,128)(2,1)S(1)}, u32[]{:S(2)}, u32[]{:S(2)}) collective-permute-start(bf16[3,128,1536]{2,1,0:T(8,128)(2,1)S(1)} %bitcast.7), channel_id=1, source_target_pairs={{0,1},{1,0},{2,3},{3,2},{4,5},{5,4},{6,7},{7,6},{8,9},{9,8},{10,11... | collective-permute-start | bytes 3538952 | tf_op jit(solution)/shard_map/ppermute | solution.py:296
  8.5 21.9 %all-to-all-start = ((bf16[16,8,2304]{2,1,0:T(8,128)(2,1)}), bf16[16,8,2304]{2,1,0:T(8,128)(2,1)S(1)}, u32[]{:S(2)}, u32[]{:S(2)}) async-start(bf16[16,8,2304]{2,1,0:T(8,128)(2,1)} %bitcast.13), calls=%async_computation | async-start | bytes 1179648 | tf_op jit(solution)/shard_map/all_to_all | solution.py:314
  14.8 4.0 %copy-start.1 = (bf16[3,16,1536]{2,1,0:T(8,128)(2,1)S(1)}, bf16[3,16,1536]{2,1,0:T(8,128)(2,1)}, u32[]{:S(2)}) copy-start(bf16[3,16,1536]{2,1,0:T(8,128)(2,1)} %refs_3_.3) | copy-start | bytes 442372
  16.6 0.7 %copy-start.2 = (bf16[64,1536]{1,0:T(8,128)(2,1)}, bf16[64,1536]{1,0:T(8,128)(2,1)S(1)}, u32[]{:S(2)}) copy-start(bf16[64,1536]{1,0:T(8,128)(2,1)S(1)} %get-tuple-element.18.refs_0_) | copy-start | bytes 589828
  17.3 9.6 %collective-permute-start.3 = (bf16[64,1536]{1,0:T(8,128)(2,1)S(1)}, bf16[64,1536]{1,0:T(8,128)(2,1)S(1)}, u32[]{:S(2)}, u32[]{:S(2)}) collective-permute-start(bf16[64,1536]{1,0:T(8,128)(2,1)S(1)} %get-tuple-element.15.refs_0_), channel_id=1, source_target_pairs={{0,2},{1,3},{2,0},{3,1},{4,6},{5,7},{6,4},{7,5},{8,10},{9,11},{10,... | collective-permute-start | bytes 589832 | tf_op jit(solution)/shard_map/ppermute | solution.py:296
  18.8 1.4 %collective-permute-start.5 = (bf16[3,16,1536]{2,1,0:T(8,128)(2,1)S(1)}, bf16[3,16,1536]{2,1,0:T(8,128)(2,1)S(1)}, u32[]{:S(2)}, u32[]{:S(2)}) collective-permute-start(bf16[3,16,1536]{2,1,0:T(8,128)(2,1)S(1)} %copy-done.1), channel_id=1, source_target_pairs={{0,1},{1,0},{2,3},{3,2},{4,5},{5,4},{6,7},{7,6},{8,9},{9,8},{10,11... | collective-permute-start | bytes 442376 | tf_op jit(solution)/shard_map/ppermute | solution.py:296
  27.7 16.0 %copy-start.3 = (bf16[64,1536]{1,0:T(8,128)(2,1)S(1)}, bf16[64,1536]{1,0:T(8,128)(2,1)}, u32[]{:S(2)}) copy-start(bf16[64,1536]{1,0:T(8,128)(2,1)} %copy-done.2) | copy-start | bytes 589828
  27.7 16.0 %copy-start.4 = (s32[12]{0:T(128)S(1)}, s32[12]{0:T(128)}, u32[]{:S(2)}) copy-start(s32[12]{0:T(128)} %kind_ref.5) | copy-start | bytes 148
  27.8 9.5 %collective-permute-start.7 = (bf16[64,1664]{1,0:T(8,128)(2,1)S(1)}, bf16[64,1664]{1,0:T(8,128)(2,1)S(1)}, u32[]{:S(2)}, u32[]{:S(2)}) collective-permute-start(bf16[64,1664]{1,0:T(8,128)(2,1)S(1)} %text.3), channel_id=1, source_target_pairs={{0,2},{1,3},{2,0},{3,1},{4,6},{5,7},{6,4},{7,5},{8,10},{9,11},{10,... | collective-permute-start | bytes 638984 | tf_op jit(solution)/shard_map/ppermute | solution.py:296
  31.6 7.6 %collective-permute-start.6 = (bf16[64,1536]{1,0:T(8,128)(2,1)}, bf16[64,1536]{1,0:T(8,128)(2,1)S(1)}, u32[]{:S(2)}, u32[]{:S(2)}) collective-permute-start(bf16[64,1536]{1,0:T(8,128)(2,1)} %copy-done.2), channel_id=1, source_target_pairs={{0,2},{1,3},{2,0},{3,1},{4,6},{5,7},{6,4},{7,5},{8,10},{9,11},{10,... | collective-permute-start | bytes 589832 | tf_op jit(solution)/shard_map/ppermute | solution.py:296
  32.1 11.6 %collective-permute-start.8 = (bf16[64,1536]{1,0:T(8,128)(2,1)}, bf16[64,1536]{1,0:T(8,128)(2,1)S(1)}, u32[]{:S(2)}, u32[]{:S(2)}) collective-permute-start(bf16[64,1536]{1,0:T(8,128)(2,1)} %copy-done.2), channel_id=1, source_target_pairs={{0,1},{1,0},{2,3},{3,2},{4,5},{5,4},{6,7},{7,6},{8,9},{9,8},{10,11... | collective-permute-start | bytes 589832 | tf_op jit(solution)/shard_map/ppermute | solution.py:296
  32.6 14.1 %all-to-all-start.1 = ((bf16[16,8,768]{2,1,0:T(8,128)(2,1)}), bf16[16,8,768]{2,1,0:T(8,128)(2,1)S(1)}, u32[]{:S(2)}, u32[]{:S(2)}) async-start(bf16[16,8,768]{2,1,0:T(8,128)(2,1)} %bitcast.3), calls=%async_computation.1 | async-start | bytes 393216 | tf_op jit(solution)/shard_map/all_to_all | solution.py:400
  39.2 4.5 %collective-permute-start.9 = (bf16[64,1536]{1,0:T(8,128)(2,1)S(1)}, bf16[64,1536]{1,0:T(8,128)(2,1)S(1)}, u32[]{:S(2)}, u32[]{:S(2)}) collective-permute-start(bf16[64,1536]{1,0:T(8,128)(2,1)S(1)} %collective-permute-done.6.refs_1_), channel_id=1, source_target_pairs={{0,1},{1,0},{2,3},{3,2},{4,5},{5,4},{6,7},{7,6},{8,9},{9,8},{10,11... | collective-permute-start | bytes 589832 | tf_op jit(solution)/shard_map/ppermute | solution.py:296
  39.3 8.8 %collective-permute-start.10 = (bf16[16,1664]{1,0:T(8,128)(2,1)S(1)}, bf16[16,1664]{1,0:T(8,128)(2,1)S(1)}, u32[]{:S(2)}, u32[]{:S(2)}) collective-permute-start(bf16[16,1664]{1,0:T(8,128)(2,1)S(1)} %get-tuple-element.24), channel_id=1, source_target_pairs={{0,4},{1,5},{2,6},{3,7},{4,0},{5,1},{6,2},{7,3},{8,12},{9,13},{10,... | collective-permute-start | bytes 159752 | tf_op jit(solution)/shard_map/ppermute | solution.py:296
  40.8 7.9 %collective-permute-start.11 = (bf16[16,1664]{1,0:T(8,128)(2,1)S(1)}, bf16[16,1664]{1,0:T(8,128)(2,1)S(1)}, u32[]{:S(2)}, u32[]{:S(2)}) collective-permute-start(bf16[16,1664]{1,0:T(8,128)(2,1)S(1)} %get-tuple-element.23), channel_id=1, source_target_pairs={{0,8},{1,9},{2,10},{3,11},{4,12},{5,13},{6,14},{7,15},{8,0},{9,1},... | collective-permute-start | bytes 159752 | tf_op jit(solution)/shard_map/ppermute | solution.py:296
  43.6 6.0 %collective-permute-start.12 = (bf16[16,1664]{1,0:T(8,128)(2,1)S(1)}, bf16[16,1664]{1,0:T(8,128)(2,1)S(1)}, u32[]{:S(2)}, u32[]{:S(2)}) collective-permute-start(bf16[16,1664]{1,0:T(8,128)(2,1)S(1)} %get-tuple-element.22), channel_id=1, source_target_pairs={{0,12},{1,13},{2,14},{3,15},{4,8},{5,9},{6,10},{7,11},{8,4},{9,5},... | collective-permute-start | bytes 159752 | tf_op jit(solution)/shard_map/ppermute | solution.py:296

commit v4 on v3

--- a/solution.py
+++ b/solution.py
@@ -9,6 +9,7 @@
 
 masked_score = -1e30
 lanes = 128
+stat_lanes = 32
 
 
 def contract_last(a, b):
@@ -94,7 +95,7 @@
         )
 
 
-def temporal_kernel(half, stride, scale, block_ref, out_ref, score_ref, weight_ref):
+def temporal_kernel(half, stride, scale, block_ref, out_ref, score_ref, weight_ref, here_ref, sems):
     rows = block_ref.shape[0]
     row = lax.broadcasted_iota(jnp.int32, (rows, rows), 0)
     column = lax.broadcasted_iota(jnp.int32, (rows, rows), 1)
@@ -109,13 +110,22 @@
         exps = jnp.exp(scores - scores.max(-1, keepdims=True))
         totals.append(exps.sum(-1, keepdims=True))
         weight_ref[slot] = exps.astype(jnp.bfloat16)
+    sends = []
     for slot in range(half):
         summed = jnp.dot(
             weight_ref[slot],
             block_ref[:, head_lanes(2 * half + slot)],
             preferred_element_type=jnp.float32,
         )
-        out_ref[:, head_lanes(slot)] = (summed / totals[slot]).astype(jnp.bfloat16)
+        here_ref[:, head_lanes(slot)] = (summed / totals[slot]).astype(jnp.bfloat16)
+        if slot % 2 == 1 or slot == half - 1:
+            span = pl.ds((slot // 2) * 2 * lanes, (slot % 2 + 1) * lanes)
+            sends.append(
+                pltpu.make_async_copy(here_ref.at[:, span], out_ref.at[:, span], sems.at[slot // 2])
+            )
+            sends[-1].start()
+    for send in sends:
+        send.wait()
 
 
 def spatial_kernel(
@@ -123,18 +133,27 @@
     shard,
     relative,
     scale,
+    blocks,
     kind_ref,
     length_ref,
     video_ref,
     *refs,
 ):
-    text_refs = refs[:-4]
-    out_ref, list_ref, score_ref, weight_ref = refs[-4:]
+    text_refs = refs[:blocks]
+    out_ref, list_ref, keys_ref, score_ref, weight_ref, sems = refs[blocks:]
+    width = keys_ref.shape[1]
+    copies = []
+    rows = 0
+    for i, ref in enumerate(text_refs):
+        source = ref.at[:, pl.ds(ref.shape[1] - width, width)]
+        target = keys_ref.at[pl.ds(rows, ref.shape[0])]
+        copies.append(pltpu.make_async_copy(source, target, sems.at[i]))
+        copies[-1].start()
+        rows += ref.shape[0]
     list_heads(kind_ref, list_ref, head_count)
     half = head_count // 2
     positions = video_ref.shape[1]
-    text_total = sum(ref.shape[0] for ref in text_refs)
-    index = lax.broadcasted_iota(jnp.int32, (8, text_total), 1)
+    index = lax.broadcasted_iota(jnp.int32, (8, rows), 1)
     if relative:
         block = index // shard
         differs = (block & 3) * 4 + ((block >> 2) & 1) * 2 + ((block >> 3) & 1)
@@ -144,11 +163,15 @@
 
     def gathered(part, slot):
         return jnp.concatenate(
-            [video_ref[part + 1, :, head_lanes(list_ref[slot])]]
-            + [ref[:, head_lanes(part * half + slot)] for ref in text_refs],
+            [
+                video_ref[part + 1, :, head_lanes(list_ref[slot])],
+                keys_ref[:, head_lanes(part * half + slot)],
+            ],
             axis=0,
         )
 
+    for copy in copies:
+        copy.wait()
     for slot in range(half):
         score_ref[slot] = contract_last(
             video_ref[0, :, head_lanes(list_ref[slot])], gathered(0, slot)
@@ -167,7 +190,7 @@
 
 
 def text_kernel(head_count, shard, scale, length_ref, *refs):
-    query_refs, key_refs = refs[:-7], refs[-7:-3]
+    query_ref, key_refs, rider_refs = refs[0], refs[1:5], refs[5:-3]
     out_ref, score_ref, weight_ref = refs[-3:]
     rows = out_ref.shape[0]
     positions, text_rows = key_refs[0].shape[1], key_refs[2].shape[1]
@@ -184,8 +207,7 @@
         return jnp.concatenate([ref[part, :, head_lanes(head)] for ref in key_refs], axis=0)
 
     for head in range(head_count):
-        query = jnp.concatenate([ref[:, head_lanes(head)] for ref in query_refs], axis=0)
-        score_ref[head] = contract_last(query, gathered(1, head))
+        score_ref[head] = contract_last(query_ref[:, head_lanes(head)], gathered(1, head))
     for head in range(head_count):
         scores = score_ref[head] * scale + bias
         point = scores.max(-1, keepdims=True).astype(jnp.bfloat16).astype(jnp.float32)
@@ -194,53 +216,63 @@
         weight_ref[head] = exps.astype(jnp.bfloat16)
         high = total.astype(jnp.bfloat16).astype(jnp.float32)
         for place, column in enumerate((point, high, total - high)):
-            stats = jnp.where(lane == 3 * head + place, column, stats)
+            stats = jnp.where(lane == place * stat_lanes + head, column, stats)
     for head in range(head_count):
         summed = jnp.dot(
             weight_ref[head], gathered(2, head), preferred_element_type=jnp.float32
         )
         out_ref[:, head_lanes(head)] = summed.astype(jnp.bfloat16)
     out_ref[:, head_lanes(head_count)] = stats.astype(jnp.bfloat16)
+    for ref in rider_refs:
+        out_ref[:, pl.ds((head_count + 1) * lanes, ref.shape[1])] = ref[...]
 
 
 def merge(head_count, blocks):
     stats = [block(head_count).astype(jnp.float32) for block in blocks]
-    merged = []
-    for head in range(head_count):
-        points = [s[:, 3 * head : 3 * head + 1] for s in stats]
-        totals = [s[:, 3 * head + 1 : 3 * head + 2] + s[:, 3 * head + 2 : 3 * head + 3] for s in stats]
-        point = functools.reduce(jnp.maximum, points)
-        factors = [jnp.exp(p - point) for p in points]
-        total = sum(f * t for f, t in zip(factors, totals))
-        summed = sum(f * block(head).astype(jnp.float32) for f, block in zip(factors, blocks))
-        merged.append((point, total, summed))
-    return merged
+    points, highs, lows = (
+        [s[:, part * stat_lanes : (part + 1) * stat_lanes] for s in stats] for part in range(3)
+    )
+    point = functools.reduce(jnp.maximum, points)
+    factors = [jnp.exp(p - point) for p in points]
+    total = sum(f * (high + low) for f, high, low in zip(factors, highs, lows))
+    return point, total, factors
+
+
+def weigh(head, factors, blocks):
+    return sum(
+        f[:, head : head + 1] * block(head).astype(jnp.float32)
+        for f, block in zip(factors, blocks)
+    )
 
 
 def reader(ref):
     return lambda head: ref[:, head_lanes(head)]
 
 
-def merge_kernel(head_count, *refs):
-    out_ref = refs[-1]
-    lane = lax.broadcasted_iota(jnp.int32, (out_ref.shape[0], lanes), 1)
-    stats = jnp.zeros(lane.shape, jnp.float32)
-    for head, (point, total, summed) in enumerate(
-        merge(head_count, [reader(ref) for ref in refs[:-1]])
-    ):
-        out_ref[:, head_lanes(head)] = summed.astype(jnp.bfloat16)
-        high = total.astype(jnp.bfloat16).astype(jnp.float32)
-        for place, column in enumerate((point, high, total - high)):
-            stats = jnp.where(lane == 3 * head + place, column, stats)
-    out_ref[:, head_lanes(head_count)] = stats.astype(jnp.bfloat16)
+def merge_kernel(head_count, parts, first_ref, second_ref, *out_refs):
+    blocks = [reader(first_ref), reader(second_ref)]
+    point, total, factors = merge(head_count, blocks)
+    high = total.astype(jnp.bfloat16).astype(jnp.float32)
+
+    def store(head, merged):
+        for ref, places in zip(out_refs, parts):
+            ref[:, head_lanes(head)] = jnp.concatenate(
+                [merged[i * 16 : (i + 1) * 16] for i in places], axis=0
+            ).astype(jnp.bfloat16)
+
+    for head in range(head_count):
+        store(head, weigh(head, factors, blocks))
+    store(head_count, jnp.concatenate([point, high, total - high, jnp.zeros_like(point)], axis=1))
 
 
 def finish_kernel(head_count, *refs):
     out_ref = refs[-1]
-    for head, (_, total, summed) in enumerate(
-        merge(head_count, [reader(ref) for ref in refs[:-1]])
-    ):
-        out_ref[:, head_lanes(head)] = (summed / total).astype(jnp.bfloat16)
+    blocks = [reader(ref) for ref in refs[:-1]]
+    _, total, factors = merge(head_count, blocks)
+    total = jnp.where(total > 0, total, 1.0)
+    factors = [f / total for f in factors]
+    for head in range(head_count):
+        out_ref[:, head_lanes(head)] = weigh(head, factors, blocks).astype(jnp.bfloat16)
 
 
 def join_kernel(head_count, kind_ref, spatial_ref, temporal_ref, out_ref, list_ref):
@@ -261,14 +293,14 @@
     return lax.optimization_barrier((array, *others))[0]
 
 
-def call(kernel, name, out, scalars, arrays, scratch=(), flops=0, space=pltpu.VMEM, out_space=pltpu.VMEM, limit=32):
+def call(kernel, name, out, scalars, arrays, scratch=(), flops=0, spaces=None, out_space=pltpu.VMEM, limit=32):
     outs = [jax.ShapeDtypeStruct(shape, jnp.bfloat16) for shape in out]
     moved = sum(a.size * 2 for a in arrays) + sum(o.size * 2 for o in outs)
     return pl.pallas_call(
         kernel,
         out_shape=outs,
         in_specs=[pl.BlockSpec(memory_space=pltpu.SMEM)] * len(scalars)
-        + [pl.BlockSpec(memory_space=space)] * len(arrays),
+        + [pl.BlockSpec(memory_space=m) for m in spaces or [pltpu.VMEM] * len(arrays)],
         out_specs=[pl.BlockSpec(memory_space=out_space)] * len(outs),
         scratch_shapes=scratch,
         compiler_params=pltpu.CompilerParams(vmem_limit_bytes=limit * 2**20),
@@ -307,7 +339,7 @@
         + [pltpu.VMEM((shard, 2 * width), jnp.bfloat16)]
         + [pltpu.VMEM((positions, 3 * half * lanes), jnp.bfloat16)]
         + [pltpu.SemaphoreType.DMA((5,)), pltpu.SemaphoreType.DMA((4,))],
-        space=pl.ANY,
+        spaces=[pl.ANY] * 3,
         out_space=pl.ANY,
         limit=60,
     )
@@ -318,15 +350,15 @@
     other_text = swap(text, 1)
     keys = [video, swap(video, 1), text, other_text]
 
-    def attend(queries):
-        rows = sum(q.shape[0] for q in queries)
+    def attend(queries, riders=()):
+        rows = queries.shape[0]
         key_count = 2 * (positions + text_rows)
         return call(
             functools.partial(text_kernel, head_count, shard, scale),
             "text",
-            [(rows, width + lanes)],
+            [(rows, width + lanes + sum(r.shape[1] for r in riders))],
             [text_len],
-            [*queries, *keys],
+            [queries, *keys, *riders],
             score_scratch(head_count, rows, key_count),
             flops=4 * rows * width * key_count,
         )[0]
@@ -338,31 +370,35 @@
             [(positions, half * lanes)],
             [],
             [received],
-            score_scratch(half, positions, positions),
+            score_scratch(half, positions, positions)
+            + [pltpu.VMEM((positions, half * lanes), jnp.bfloat16)]
+            + [pltpu.SemaphoreType.DMA((-(-half // 2),))],
             flops=4 * positions * half * lanes * positions,
+            out_space=pl.ANY,
         )
 
     if relative:
         column = [packed_text] + [swap(packed_text, 4 * step) for step in (1, 2, 3)]
         queries_column, keys_column = call(
-            stack_kernel, "stack", [(4 * shard, width)] * 2, [], column, flops=20000000000
+            stack_kernel, "stack", [(4 * shard, width)] * 2, [], column, flops=8 * 10**9
         )
         across = swap(queries_column, 2)
-        kept = attend([queries_column])
+        kept = attend(queries_column)
         across = after(across, kept)
-        partial_sums = attend([across])
+        partial_sums = attend(across, [keys_column])
         sent = swap(partial_sums, 2)
         (result,) = attend_temporal(after(block, partial_sums))
         sent = after(sent, result)
-        (joined,) = call(
-            functools.partial(merge_kernel, head_count), "merge", [kept.shape], [], [kept, sent]
-        )
-        pieces = [joined[:shard]] + [
-            swap(joined[step * shard : (step + 1) * shard], 4 * step) for step in (1, 2, 3)
-        ]
-        across_keys = swap(after(keys_column, result), 2)
-        across_keys = after(across_keys, joined)
-        text_keys = [keys_column, across_keys, swap(keys_column, 1), swap(across_keys, 1)]
+        joined = call(
+            functools.partial(merge_kernel, head_count, ((0,), (1,), (2,), (3,))),
+            "merge",
+            [(shard, width + lanes)] * 4,
+            [],
+            [kept, sent],
+            flops=20 * 10**9,
+        )
+        pieces = [joined[0]] + [swap(joined[step], 4 * step) for step in (1, 2, 3)]
+        text_keys = [keys_column, sent, swap(keys_column, 1), swap(sent, 1)]
     else:
         (result,) = attend_temporal(block)
         side = [[2 * chip + core for chip in range(devices // 2)] for core in range(2)]
@@ -370,27 +406,36 @@
             packed_text[:, :width], "frame", axis=0, tiled=True, axis_index_groups=side
         )
         partial_sums = lax.all_to_all(
-            attend([gathered]), "frame", 0, 0, tiled=True, axis_index_groups=side
+            attend(gathered), "frame", 0, 0, tiled=True, axis_index_groups=side
         ).reshape(devices // 2, shard, width + lanes)
         blocks = [
             lambda head, i=i: partial_sums[i, :, head * lanes : (head + 1) * lanes]
             for i in range(devices // 2)
         ]
+        _, total, factors = merge(head_count, blocks)
         text_out = jnp.concatenate(
-            [summed / total for _, total, summed in merge(head_count, blocks)], axis=1
+            [
+                weigh(head, factors, blocks) / total[:, head : head + 1]
+                for head in range(head_count)
+            ],
+            axis=1,
         ).astype(jnp.bfloat16)
         all_keys = lax.all_gather(packed_text[:, width:], "frame", axis=0, tiled=True)
         text_keys = [all_keys]
 
     key_count = positions + devices * shard
     (spatial,) = call(
-        functools.partial(spatial_kernel, head_count, shard, relative, scale),
+        functools.partial(spatial_kernel, head_count, shard, relative, scale, len(text_keys)),
         "spatial",
         [(positions, half * lanes)],
         [head_kind, text_len],
         [video, *text_keys],
-        head_list + score_scratch(half, positions, key_count),
+        head_list
+        + [pltpu.VMEM((key_count - positions, 2 * half * lanes), jnp.bfloat16)]
+        + score_scratch(half, positions, key_count)
+        + [pltpu.SemaphoreType.DMA((len(text_keys),))],
         flops=4 * positions * half * lanes * key_count,
+        spaces=[pltpu.VMEM] + [pl.ANY] * len(text_keys),
     )
     if relative:
         pieces[0] = after(pieces[0], spatial)

time: 50.9 us -> 50.3 us (0.988)
  waiting for transfers between devices: 14.4 us -> 13.4 us
  local copies, waits for them, and re-layouts: 0.72 us -> 1.64 us
  starting transfers between devices: 24.8 us -> 23.9 us
    all_to_all x1, waiting for transfers between devices: 1.65 us -> 0.01 us  [body(): lax.all_to_all(result, 'frame', split_axis=0, concat_axis=0, tiled=True)]
    ppermute x13 -> x12, starting transfers between devices: 14 us -> 12.8 us  [swap(): return lax.ppermute(array, 'frame', [(i, i ^ bits) for i in range(devices)])]
    unnamed x12 -> x16, local copies, waits for them, and re-layouts: 0.7 us -> 1.64 us
    ppermute x13 -> x12, waiting for transfers between devices: 11.4 us -> 11.9 us  [swap(): return lax.ppermute(array, 'frame', [(i, i ^ bits) for i in range(devices)])]
  transfers between devices with their start and end apart: 15 -> 14, of which waited for: 8 -> 6; matrix products, arithmetic and copies ran while one was open for 0% -> 0% of each run, Pallas kernels for 12% -> 17%
where the time goes in v4:
time: 50.3 us; the launch traced here: 50 us
  starting transfers between devices  23.9 us (48%)
  waiting for transfers between devices  13.4 us (27%)
  Pallas kernels  9.54 us (19%)
  local copies, waits for them, and re-layouts  1.64 us (3%)
  between operations  1.43 us (3%)
    ppermute x12, starting transfers between devices, swap(): return lax.ppermute(array, 'frame', [(i, i ^ bits) for i in range(devices)])  12.8 us
    ppermute x12, waiting for transfers between devices, swap(): return lax.ppermute(array, 'frame', [(i, i ^ bits) for i in range(devices)])  11.9 us
    pallas_call x9, Pallas kernels, call(): pl.pallas_call(kernel, out_shape=outs, in_specs=[pl.BlockSpec(memory_spac...  9.54 us
    all_to_all x1, starting transfers between devices, body(): lax.all_to_all(packed_video, 'frame', split_axis=0, concat_axis=0, tiled=...  6.16 us
    all_to_all x1, starting transfers between devices, body(): lax.all_to_all(result, 'frame', split_axis=0, concat_axis=0, tiled=True)  4.98 us
    unnamed x16, local copies, waits for them, and re-layouts  1.64 us
    all_to_all x1, waiting for transfers between devices, body(): lax.all_to_all(packed_video, 'frame', split_axis=0, concat_axis=0, tiled=...  1.56 us
  transfers between devices with their start and end apart: 14, of which 6 were waited for; matrix products, arithmetic and copies ran while one was open for 0% of the time, Pallas kernels for 17%

profile of v4, /device:TPU:0, one launch (start us, length us, event | category | flops | bytes accessed | tf_op | source)
XLA Modules:
  0.0 50.0 jit_solution(14740517114309644441)
XLA Ops:
  0.6 0.5 %collective-permute-start.4 = (bf16[3,128,1536]{2,1,0:T(8,128)(2,1)}, bf16[3,128,1536]{2,1,0:T(8,128)(2,1)S(1)}, u32[]{:S(2)}, u32[]{:S(2)}) collective-permute-start(bf16[3,128,1536]{2,1,0:T(8,128)(2,1)} %bitcast.6), channel_id=1, source_target_pairs={{0,1},{1,0},{2,3},{3,2},{4,5},{5,4},{6,7},{7,6},{8,9},{9,8},{10,11... | collective-permute-start | bytes 3538952 | tf_op jit(solution)/shard_map/ppermute | solution.py:328
  1.1 2.1 %pack.1 = (bf16[16,3072]{1,0:T(8,128)(2,1)}, bf16[128,2304]{1,0:T(8,128)(2,1)}) custom-call(s32[12]{0:T(128)} %kind_ref.5, bf16[3,16,1536]{2,1,0:T(8,128)(2,1)} %refs_3_.3, bf16[3,128,1536]{2,1,0:T(8,128)(2,1)} %bitcast.7), custom_call_target="tpu_custom_call" | custom-call | bytes 2015256 | tf_op jit(solution)/shard_map/pack/pallas_call | solution.py:299
  3.3 0.0 copy-start.7
  3.3 2.7 %collective-permute-start = (bf16[16,3072]{1,0:T(8,128)(2,1)}, bf16[16,3072]{1,0:T(8,128)(2,1)S(1)}, u32[]{:S(2)}, u32[]{:S(2)}) collective-permute-start(bf16[16,3072]{1,0:T(8,128)(2,1)} %get-tuple-element.14.refs_0_), channel_id=1, source_target_pairs={{0,4},{1,5},{2,6},{3,7},{4,0},{5,1},{6,2},{7,3},{8,12},{9,13},{10,... | collective-permute-start | bytes 294920 | tf_op jit(solution)/shard_map/ppermute | solution.py:328
  5.9 2.6 %collective-permute-start.1 = (bf16[16,3072]{1,0:T(8,128)(2,1)}, bf16[16,3072]{1,0:T(8,128)(2,1)S(1)}, u32[]{:S(2)}, u32[]{:S(2)}) collective-permute-start(bf16[16,3072]{1,0:T(8,128)(2,1)} %get-tuple-element.14.refs_0_), channel_id=1, source_target_pairs={{0,8},{1,9},{2,10},{3,11},{4,12},{5,13},{6,14},{7,15},{8,0},{9,1},... | collective-permute-start | bytes 294920 | tf_op jit(solution)/shard_map/ppermute | solution.py:328
  8.5 0.0 collective-permute-start.2
  8.5 6.2 %all-to-all-start = ((bf16[16,8,2304]{2,1,0:T(8,128)(2,1)}), bf16[16,8,2304]{2,1,0:T(8,128)(2,1)S(1)}, u32[]{:S(2)}, u32[]{:S(2)}) async-start(bf16[16,8,2304]{2,1,0:T(8,128)(2,1)} %bitcast.13), calls=%async_computation | async-start | bytes 1179648 | tf_op jit(solution)/shard_map/all_to_all | solution.py:346
  14.7 0.0 copy-start.1
  14.7 0.0 copy-start
  14.7 0.0 collective-permute-done.refs_1_
  14.7 2.2 %collective-permute-done.1.refs_2_ = bf16[16,3072]{1,0:T(8,128)(2,1)S(1)} collective-permute-done((bf16[16,3072]{1,0:T(8,128)(2,1)}, bf16[16,3072]{1,0:T(8,128)(2,1)S(1)}, u32[]{:S(2)}, u32[]{:S(2)}) %collective-permute-start.1) | collective-permute-done | bytes 98336 | tf_op jit(solution)/shard_map/ppermute | solution.py:328
  16.9 0.0 collective-permute-done.2.refs_3_
  16.9 0.0 copy-done.7
  16.9 1.6 %collective-permute-start.3 = (bf16[64,1536]{1,0:T(8,128)(2,1)S(1)}, bf16[64,1536]{1,0:T(8,128)(2,1)S(1)}, u32[]{:S(2)}, u32[]{:S(2)}) collective-permute-start(bf16[64,1536]{1,0:T(8,128)(2,1)S(1)} %get-tuple-element.16.refs_0_), channel_id=1, source_target_pairs={{0,2},{1,3},{2,0},{3,1},{4,6},{5,7},{6,4},{7,5},{8,10},{9,11},{10,... | collective-permute-start | bytes 589832 | tf_op jit(solution)/shard_map/ppermute | solution.py:328
  18.5 0.0 copy-done.1
  18.5 0.0 collective-permute-start.5
  19.2 0.7 %collective-permute-done.5.refs_4_ = bf16[3,16,1536]{2,1,0:T(8,128)(2,1)S(1)} collective-permute-done((bf16[3,16,1536]{2,1,0:T(8,128)(2,1)S(1)}, bf16[3,16,1536]{2,1,0:T(8,128)(2,1)S(1)}, u32[]{:S(2)}, u32[]{:S(2)}) %collective-permute-start.5) | collective-permute-done | bytes 147488 | tf_op jit(solution)/shard_map/ppermute | solution.py:328
  19.9 0.0 collective-permute-done.4.refs_2_
  19.9 0.0 copy-done
  19.9 0.8 %text.2.first_ref = bf16[64,1664]{1,0:T(8,128)(2,1)S(1)} custom-call(s32[1]{0:T(128)S(6)} %copy.6.length_ref, bf16[64,1536]{1,0:T(8,128)(2,1)S(1)} %get-tuple-element.16.refs_0_, bf16[3,128,1536]{2,1,0:T(8,128)(2,1)S(1)} %bitcast.8, bf16[3,128,1536]{2,1,0:T(8,128)(2,1)S(1)} %collective-permute-done.4.refs_2_, bf16[3,16,1536]{2,1,0:T(8,128)(2,1)S(1)} %copy-done.1, ...), custom_call_target="tpu_custom_call" | custom-call | flops 113246208 | bytes 3063808 | tf_op jit(solution)/shard_map/text/pallas_call | solution.py:299
  20.7 0.0 copy-start.2
  20.7 6.0 %collective-permute-done.3.refs_0_ = bf16[64,1536]{1,0:T(8,128)(2,1)S(1)} collective-permute-done((bf16[64,1536]{1,0:T(8,128)(2,1)S(1)}, bf16[64,1536]{1,0:T(8,128)(2,1)S(1)}, u32[]{:S(2)}, u32[]{:S(2)}) %collective-permute-start.3) | collective-permute-done | bytes 196640 | tf_op jit(solution)/shard_map/ppermute | solution.py:328
  26.8 0.8 %text.3 = bf16[64,3200]{1,0:T(8,128)(2,1)S(1)} custom-call(s32[1]{0:T(128)S(6)} %copy.6.length_ref, bf16[64,1536]{1,0:T(8,128)(2,1)S(1)} %collective-permute-done.3.refs_0_, bf16[3,128,1536]{2,1,0:T(8,128)(2,1)S(1)} %bitcast.9, bf16[3,128,1536]{2,1,0:T(8,128)(2,1)S(1)} %collective-permute-done.4.refs_2_, bf16[3,16,1536]{2,1,0:T(8,128)(2,1)S(1)} %copy-done.1, ...), custom_call_target="tpu_custom_call" | custom-call | flops 113246208 | bytes 3457024 | tf_op jit(solution)/shard_map/text/pallas_call | solution.py:299
  27.6 0.0 copy-done.2
  27.6 1.1 %collective-permute-start.6 = (bf16[64,3200]{1,0:T(8,128)(2,1)S(1)}, bf16[64,3200]{1,0:T(8,128)(2,1)S(1)}, u32[]{:S(2)}, u32[]{:S(2)}) collective-permute-start(bf16[64,3200]{1,0:T(8,128)(2,1)S(1)} %text.3), channel_id=1, source_target_pairs={{0,2},{1,3},{2,0},{3,1},{4,6},{5,7},{6,4},{7,5},{8,10},{9,11},{10,... | collective-permute-start | bytes 1228808 | tf_op jit(solution)/shard_map/ppermute | solution.py:328
  28.7 0.0 collective-permute-start.7
  28.7 1.6 %all-to-all-done = bf16[16,8,2304]{2,1,0:T(8,128)(2,1)S(1)} async-done(((bf16[16,8,2304]{2,1,0:T(8,128)(2,1)}), bf16[16,8,2304]{2,1,0:T(8,128)(2,1)S(1)}, u32[]{:S(2)}, u32[]{:S(2)}) %all-to-all-start) | async-done | bytes 589856 | tf_op jit(solution)/shard_map/all_to_all | solution.py:346
  30.3 1.2 %temporal.1 = bf16[128,768]{1,0:T(8,128)(2,1)} custom-call(bf16[128,2304]{1,0:T(8,128)(2,1)S(1)} %bitcast.11), custom_call_target="tpu_custom_call" | custom-call | flops 50331648 | bytes 786432 | tf_op jit(solution)/shard_map/temporal/pallas_call | solution.py:299
  31.4 5.0 %all-to-all-start.1 = ((bf16[16,8,768]{2,1,0:T(8,128)(2,1)}), bf16[16,8,768]{2,1,0:T(8,128)(2,1)S(1)}, u32[]{:S(2)}, u32[]{:S(2)}) async-start(bf16[16,8,768]{2,1,0:T(8,128)(2,1)} %bitcast.3), calls=%async_computation.1 | async-start | bytes 393216 | tf_op jit(solution)/shard_map/all_to_all | solution.py:445
  36.4 0.0 copy-start.6
  36.4 2.7 %collective-permute-done.6.refs_1_.second_ref = bf16[64,3200]{1,0:T(8,128)(2,1)S(1)} collective-permute-done((bf16[64,3200]{1,0:T(8,128)(2,1)S(1)}, bf16[64,3200]{1,0:T(8,128)(2,1)S(1)}, u32[]{:S(2)}, u32[]{:S(2)}) %collective-permute-start.6) | collective-permute-done | bytes 409632 | tf_op jit(solution)/shard_map/ppermute | solution.py:328
  39.1 0.0 collective-permute-start.8
  39.1 0.3 merge.1
  39.5 1.7 %collective-permute-start.10 = (bf16[16,1664]{1,0:T(8,128)(2,1)S(1)}, bf16[16,1664]{1,0:T(8,128)(2,1)S(1)}, u32[]{:S(2)}, u32[]{:S(2)}) collective-permute-start(bf16[16,1664]{1,0:T(8,128)(2,1)S(1)} %get-tuple-element.24), channel_id=1, source_target_pairs={{0,8},{1,9},{2,10},{3,11},{4,12},{5,13},{6,14},{7,15},{8,0},{9,1},... | collective-permute-start | bytes 159752 | tf_op jit(solution)/shard_map/ppermute | solution.py:328
  41.1 2.2 %collective-permute-start.11 = (bf16[16,1664]{1,0:T(8,128)(2,1)S(1)}, bf16[16,1664]{1,0:T(8,128)(2,1)S(1)}, u32[]{:S(2)}, u32[]{:S(2)}) collective-permute-start(bf16[16,1664]{1,0:T(8,128)(2,1)S(1)} %get-tuple-element.25), channel_id=1, source_target_pairs={{0,12},{1,13},{2,14},{3,15},{4,8},{5,9},{6,10},{7,11},{8,4},{9,5},... | collective-permute-start | bytes 159752 | tf_op jit(solution)/shard_map/ppermute | solution.py:328
  43.3 0.5 collective-permute-start.9
  43.8 0.0 collective-permute-done.7.refs_2_
  43.8 0.7 %copy-done.4 = bf16[64,1536]{1,0:T(8,128)(2,1)} copy-done((bf16[64,1536]{1,0:T(8,128)(2,1)}, bf16[64,1536]{1,0:T(8,128)(2,1)S(1)}, u32[]{:S(2)}) %copy-start.4) | copy-done | bytes 196632
  44.5 0.0 collective-permute-done.8.refs_3_
  44.5 0.0 copy-done.6
  44.5 0.9 %copy-done.5 = bf16[64,1536]{1,0:T(8,128)(2,1)S(1)} copy-done((bf16[64,1536]{1,0:T(8,128)(2,1)S(1)}, bf16[64,1536]{1,0:T(8,128)(2,1)}, u32[]{:S(2)}) %copy-start.5) | copy-done | bytes 196632
  45.4 1.9 %spatial.1.spatial_ref = bf16[128,768]{1,0:T(8,128)(2,1)S(1)} custom-call(s32[12]{0:T(128)S(1)} %copy-done.6, s32[1]{0:T(128)S(6)} %copy.6.length_ref, bf16[3,128,1536]{2,1,0:T(8,128)(2,1)S(1)} %bitcast.10, bf16[64,1536]{1,0:T(8,128)(2,1)S(1)} %get-tuple-element.15.refs_5_.refs_0_, bf16[64,3200]{1,0:T(8,128)(2,1)S(1)} %collective-permute-done.6.refs_1_.second_ref, ...), custom_call_target="tpu_custom_call" | custom-call | flops 150994944 | bytes 2588672 | tf_op jit(solution)/shard_map/spatial/pallas_call | solution.py:299
  47.3 0.0 all-to-all-done.1
  47.3 1.4 %join.1 = bf16[128,1536]{1,0:T(8,128)(2,1)} custom-call(s32[12]{0:T(128)S(1)} %copy-done.6, bf16[128,768]{1,0:T(8,128)(2,1)S(1)} %spatial.1.spatial_ref, bf16[128,768]{1,0:T(8,128)(2,1)S(1)} %bitcast.12), custom_call_target="tpu_custom_call" | custom-call | bytes 786432 | tf_op jit(solution)/shard_map/join/pallas_call | solution.py:299
  48.7 0.0 collective-permute-done.10.refs_2_
  48.7 0.0 collective-permute-done.11.refs_3_
  48.7 0.3 collective-permute-done.9.refs_1_
  49.0 1.0 %finish.1 = bf16[16,1536]{1,0:T(8,128)(2,1)} custom-call(bf16[16,1664]{1,0:T(8,128)(2,1)S(1)} %get-tuple-element.22.refs_0_, bf16[16,1664]{1,0:T(8,128)(2,1)S(1)} %collective-permute-done.9.refs_1_, bf16[16,1664]{1,0:T(8,128)(2,1)S(1)} %collective-permute-done.10.refs_2_, bf16[16,1664]{1,0:T(8,128)(2,1)S(1)} %collective-permute-done.11.refs_3_), custom_call_target="tpu_custom_call" | custom-call | bytes 262144 | tf_op jit(solution)/shard_map/finish/pallas_call | solution.py:299
  (5 shorter events, 0.0 us)
Async XLA Ops:
  0.6 19.3 %collective-permute-start.4 = (bf16[3,128,1536]{2,1,0:T(8,128)(2,1)}, bf16[3,128,1536]{2,1,0:T(8,128)(2,1)S(1)}, u32[]{:S(2)}, u32[]{:S(2)}) collective-permute-start(bf16[3,128,1536]{2,1,0:T(8,128)(2,1)} %bitcast.6), channel_id=1, source_target_pairs={{0,1},{1,0},{2,3},{3,2},{4,5},{5,4},{6,7},{7,6},{8,9},{9,8},{10,11... | collective-permute-start | bytes 3538952 | tf_op jit(solution)/shard_map/ppermute | solution.py:328
  3.3 13.6 %copy-start.7 = (bf16[16,3072]{1,0:T(8,128)(2,1)S(1)}, bf16[16,3072]{1,0:T(8,128)(2,1)}, u32[]{:S(2)}) copy-start(bf16[16,3072]{1,0:T(8,128)(2,1)} %get-tuple-element.14.refs_0_) | copy-start | bytes 294916
  3.3 11.4 %collective-permute-start = (bf16[16,3072]{1,0:T(8,128)(2,1)}, bf16[16,3072]{1,0:T(8,128)(2,1)S(1)}, u32[]{:S(2)}, u32[]{:S(2)}) collective-permute-start(bf16[16,3072]{1,0:T(8,128)(2,1)} %get-tuple-element.14.refs_0_), channel_id=1, source_target_pairs={{0,4},{1,5},{2,6},{3,7},{4,0},{5,1},{6,2},{7,3},{8,12},{9,13},{10,... | collective-permute-start | bytes 294920 | tf_op jit(solution)/shard_map/ppermute | solution.py:328
  5.9 11.0 %collective-permute-start.1 = (bf16[16,3072]{1,0:T(8,128)(2,1)}, bf16[16,3072]{1,0:T(8,128)(2,1)S(1)}, u32[]{:S(2)}, u32[]{:S(2)}) collective-permute-start(bf16[16,3072]{1,0:T(8,128)(2,1)} %get-tuple-element.14.refs_0_), channel_id=1, source_target_pairs={{0,8},{1,9},{2,10},{3,11},{4,12},{5,13},{6,14},{7,15},{8,0},{9,1},... | collective-permute-start | bytes 294920 | tf_op jit(solution)/shard_map/ppermute | solution.py:328
  8.5 8.4 %collective-permute-start.2 = (bf16[16,3072]{1,0:T(8,128)(2,1)}, bf16[16,3072]{1,0:T(8,128)(2,1)S(1)}, u32[]{:S(2)}, u32[]{:S(2)}) collective-permute-start(bf16[16,3072]{1,0:T(8,128)(2,1)} %get-tuple-element.14.refs_0_), channel_id=1, source_target_pairs={{0,12},{1,13},{2,14},{3,15},{4,8},{5,9},{6,10},{7,11},{8,4},{9,5},... | collective-permute-start | bytes 294920 | tf_op jit(solution)/shard_map/ppermute | solution.py:328
  8.5 21.7 %all-to-all-start = ((bf16[16,8,2304]{2,1,0:T(8,128)(2,1)}), bf16[16,8,2304]{2,1,0:T(8,128)(2,1)S(1)}, u32[]{:S(2)}, u32[]{:S(2)}) async-start(bf16[16,8,2304]{2,1,0:T(8,128)(2,1)} %bitcast.13), calls=%async_computation | async-start | bytes 1179648 | tf_op jit(solution)/shard_map/all_to_all | solution.py:346
  14.7 3.8 %copy-start.1 = (bf16[3,16,1536]{2,1,0:T(8,128)(2,1)S(1)}, bf16[3,16,1536]{2,1,0:T(8,128)(2,1)}, u32[]{:S(2)}) copy-start(bf16[3,16,1536]{2,1,0:T(8,128)(2,1)} %refs_3_.3) | copy-start | bytes 442372
  14.7 5.2 %copy-start = (bf16[3,1,128,1536]{3,2,1,0:T(8,128)(2,1)S(1)}, bf16[3,1,128,1536]{3,2,1,0:T(8,128)(2,1)}, u32[]{:S(2)}) copy-start(bf16[3,1,128,1536]{3,2,1,0:T(8,128)(2,1)} %param.4) | copy-start | bytes 3538948
  16.9 9.8 %collective-permute-start.3 = (bf16[64,1536]{1,0:T(8,128)(2,1)S(1)}, bf16[64,1536]{1,0:T(8,128)(2,1)S(1)}, u32[]{:S(2)}, u32[]{:S(2)}) collective-permute-start(bf16[64,1536]{1,0:T(8,128)(2,1)S(1)} %get-tuple-element.16.refs_0_), channel_id=1, source_target_pairs={{0,2},{1,3},{2,0},{3,1},{4,6},{5,7},{6,4},{7,5},{8,10},{9,11},{10,... | collective-permute-start | bytes 589832 | tf_op jit(solution)/shard_map/ppermute | solution.py:328
  18.5 1.4 %collective-permute-start.5 = (bf16[3,16,1536]{2,1,0:T(8,128)(2,1)S(1)}, bf16[3,16,1536]{2,1,0:T(8,128)(2,1)S(1)}, u32[]{:S(2)}, u32[]{:S(2)}) collective-permute-start(bf16[3,16,1536]{2,1,0:T(8,128)(2,1)S(1)} %copy-done.1), channel_id=1, source_target_pairs={{0,1},{1,0},{2,3},{3,2},{4,5},{5,4},{6,7},{7,6},{8,9},{9,8},{10,11... | collective-permute-start | bytes 442376 | tf_op jit(solution)/shard_map/ppermute | solution.py:328
  20.7 6.9 %copy-start.2 = (bf16[64,1664]{1,0:T(8,128)(2,1)}, bf16[64,1664]{1,0:T(8,128)(2,1)S(1)}, u32[]{:S(2)}) copy-start(bf16[64,1664]{1,0:T(8,128)(2,1)S(1)} %text.2.first_ref) | copy-start | bytes 638980
  27.6 11.5 %collective-permute-start.6 = (bf16[64,3200]{1,0:T(8,128)(2,1)S(1)}, bf16[64,3200]{1,0:T(8,128)(2,1)S(1)}, u32[]{:S(2)}, u32[]{:S(2)}) collective-permute-start(bf16[64,3200]{1,0:T(8,128)(2,1)S(1)} %text.3), channel_id=1, source_target_pairs={{0,2},{1,3},{2,0},{3,1},{4,6},{5,7},{6,4},{7,5},{8,10},{9,11},{10,... | collective-permute-start | bytes 1228808 | tf_op jit(solution)/shard_map/ppermute | solution.py:328
  28.7 10.4 %copy-start.3 = (bf16[64,1664]{1,0:T(8,128)(2,1)S(1)}, bf16[64,1664]{1,0:T(8,128)(2,1)}, u32[]{:S(2)}) copy-start(bf16[64,1664]{1,0:T(8,128)(2,1)} %copy-done.2) | copy-start | bytes 638980
  28.7 15.1 %collective-permute-start.7 = (bf16[64,1536]{1,0:T(8,128)(2,1)S(1)}, bf16[64,1536]{1,0:T(8,128)(2,1)S(1)}, u32[]{:S(2)}, u32[]{:S(2)}) collective-permute-start(bf16[64,1536]{1,0:T(8,128)(2,1)S(1)} %get-tuple-element.15.refs_5_.refs_0_), channel_id=1, source_target_pairs={{0,1},{1,0},{2,3},{3,2},{4,5},{5,4},{6,7},{7,6},{8,9},{9,8},{10,11... | collective-permute-start | bytes 589832 | tf_op jit(solution)/shard_map/ppermute | solution.py:328
  31.4 15.9 %all-to-all-start.1 = ((bf16[16,8,768]{2,1,0:T(8,128)(2,1)}), bf16[16,8,768]{2,1,0:T(8,128)(2,1)S(1)}, u32[]{:S(2)}, u32[]{:S(2)}) async-start(bf16[16,8,768]{2,1,0:T(8,128)(2,1)} %bitcast.3), calls=%async_computation.1 | async-start | bytes 393216 | tf_op jit(solution)/shard_map/all_to_all | solution.py:445
  36.4 8.0 %copy-start.6 = (s32[12]{0:T(128)S(1)}, s32[12]{0:T(128)}, u32[]{:S(2)}) copy-start(s32[12]{0:T(128)} %kind_ref.5) | copy-start | bytes 148
  39.1 5.4 %collective-permute-start.8 = (bf16[64,3200]{1,0:T(8,128)(2,1)S(1)}, bf16[64,3200]{1,0:T(8,128)(2,1)S(1)}, u32[]{:S(2)}, u32[]{:S(2)}) collective-permute-start(bf16[64,3200]{1,0:T(8,128)(2,1)S(1)} %collective-permute-done.6.refs_1_.second_ref), channel_id=1, source_target_pairs={{0,1},{1,0},{2,3},{3,2},{4,5},{5,4},{6,7},{7,6},{8,9},{9,8},{10,11... | collective-permute-start | bytes 1228808 | tf_op jit(solution)/shard_map/ppermute | solution.py:328
  39.5 9.3 %collective-permute-start.10 = (bf16[16,1664]{1,0:T(8,128)(2,1)S(1)}, bf16[16,1664]{1,0:T(8,128)(2,1)S(1)}, u32[]{:S(2)}, u32[]{:S(2)}) collective-permute-start(bf16[16,1664]{1,0:T(8,128)(2,1)S(1)} %get-tuple-element.24), channel_id=1, source_target_pairs={{0,8},{1,9},{2,10},{3,11},{4,12},{5,13},{6,14},{7,15},{8,0},{9,1},... | collective-permute-start | bytes 159752 | tf_op jit(solution)/shard_map/ppermute | solution.py:328
  41.1 7.6 %collective-permute-start.11 = (bf16[16,1664]{1,0:T(8,128)(2,1)S(1)}, bf16[16,1664]{1,0:T(8,128)(2,1)S(1)}, u32[]{:S(2)}, u32[]{:S(2)}) collective-permute-start(bf16[16,1664]{1,0:T(8,128)(2,1)S(1)} %get-tuple-element.25), channel_id=1, source_target_pairs={{0,12},{1,13},{2,14},{3,15},{4,8},{5,9},{6,10},{7,11},{8,4},{9,5},... | collective-permute-start | bytes 159752 | tf_op jit(solution)/shard_map/ppermute | solution.py:328
  43.3 5.7 %collective-permute-start.9 = (bf16[16,1664]{1,0:T(8,128)(2,1)S(1)}, bf16[16,1664]{1,0:T(8,128)(2,1)S(1)}, u32[]{:S(2)}, u32[]{:S(2)}) collective-permute-start(bf16[16,1664]{1,0:T(8,128)(2,1)S(1)} %get-tuple-element.23), channel_id=1, source_target_pairs={{0,4},{1,5},{2,6},{3,7},{4,0},{5,1},{6,2},{7,3},{8,12},{9,13},{10,... | collective-permute-start | bytes 159752 | tf_op jit(solution)/shard_map/ppermute | solution.py:328
  43.8 0.7 %copy-start.4 = (bf16[64,1536]{1,0:T(8,128)(2,1)}, bf16[64,1536]{1,0:T(8,128)(2,1)S(1)}, u32[]{:S(2)}) copy-start(bf16[64,1536]{1,0:T(8,128)(2,1)S(1)} %collective-permute-done.7.refs_2_) | copy-start | bytes 589828
  44.5 0.9 %copy-start.5 = (bf16[64,1536]{1,0:T(8,128)(2,1)S(1)}, bf16[64,1536]{1,0:T(8,128)(2,1)}, u32[]{:S(2)}) copy-start(bf16[64,1536]{1,0:T(8,128)(2,1)} %copy-done.4) | copy-start | bytes 589828

commit v5 on v4

--- a/solution.py
+++ b/solution.py
@@ -133,27 +133,18 @@
     shard,
     relative,
     scale,
-    blocks,
     kind_ref,
     length_ref,
     video_ref,
     *refs,
 ):
-    text_refs = refs[:blocks]
-    out_ref, list_ref, keys_ref, score_ref, weight_ref, sems = refs[blocks:]
-    width = keys_ref.shape[1]
-    copies = []
-    rows = 0
-    for i, ref in enumerate(text_refs):
-        source = ref.at[:, pl.ds(ref.shape[1] - width, width)]
-        target = keys_ref.at[pl.ds(rows, ref.shape[0])]
-        copies.append(pltpu.make_async_copy(source, target, sems.at[i]))
-        copies[-1].start()
-        rows += ref.shape[0]
+    text_refs = refs[:-4]
+    out_ref, list_ref, score_ref, weight_ref = refs[-4:]
     list_heads(kind_ref, list_ref, head_count)
     half = head_count // 2
     positions = video_ref.shape[1]
-    index = lax.broadcasted_iota(jnp.int32, (8, rows), 1)
+    text_total = sum(ref.shape[0] for ref in text_refs)
+    index = lax.broadcasted_iota(jnp.int32, (8, text_total), 1)
     if relative:
         block = index // shard
         differs = (block & 3) * 4 + ((block >> 2) & 1) * 2 + ((block >> 3) & 1)
@@ -163,15 +154,14 @@
 
     def gathered(part, slot):
         return jnp.concatenate(
-            [
-                video_ref[part + 1, :, head_lanes(list_ref[slot])],
-                keys_ref[:, head_lanes(part * half + slot)],
+            [video_ref[part + 1, :, head_lanes(list_ref[slot])]]
+            + [
+                ref[:, head_lanes(ref.shape[1] // lanes + (part - 2) * half + slot)]
+                for ref in text_refs
             ],
             axis=0,
         )
 
-    for copy in copies:
-        copy.wait()
     for slot in range(half):
         score_ref[slot] = contract_last(
             video_ref[0, :, head_lanes(list_ref[slot])], gathered(0, slot)
@@ -266,13 +256,23 @@
 
 
 def finish_kernel(head_count, *refs):
-    out_ref = refs[-1]
-    blocks = [reader(ref) for ref in refs[:-1]]
+    out_ref, here_ref, sems = refs[-3:]
+    blocks = [reader(ref) for ref in refs[:-3]]
     _, total, factors = merge(head_count, blocks)
     total = jnp.where(total > 0, total, 1.0)
     factors = [f / total for f in factors]
-    for head in range(head_count):
-        out_ref[:, head_lanes(head)] = weigh(head, factors, blocks).astype(jnp.bfloat16)
+    half = head_count // 2
+    sends = []
+    for part in range(2):
+        for head in range(part * half, (part + 1) * half):
+            here_ref[:, head_lanes(head)] = weigh(head, factors, blocks).astype(jnp.bfloat16)
+        span = pl.ds(part * half * lanes, half * lanes)
+        sends.append(
+            pltpu.make_async_copy(here_ref.at[:, span], out_ref.at[:, span], sems.at[part])
+        )
+        sends[-1].start()
+    for send in sends:
+        send.wait()
 
 
 def join_kernel(head_count, kind_ref, spatial_ref, temporal_ref, out_ref, list_ref):
@@ -293,14 +293,14 @@
     return lax.optimization_barrier((array, *others))[0]
 
 
-def call(kernel, name, out, scalars, arrays, scratch=(), flops=0, spaces=None, out_space=pltpu.VMEM, limit=32):
+def call(kernel, name, out, scalars, arrays, scratch=(), flops=0, space=pltpu.VMEM, out_space=pltpu.VMEM, limit=32):
     outs = [jax.ShapeDtypeStruct(shape, jnp.bfloat16) for shape in out]
     moved = sum(a.size * 2 for a in arrays) + sum(o.size * 2 for o in outs)
     return pl.pallas_call(
         kernel,
         out_shape=outs,
         in_specs=[pl.BlockSpec(memory_space=pltpu.SMEM)] * len(scalars)
-        + [pl.BlockSpec(memory_space=m) for m in spaces or [pltpu.VMEM] * len(arrays)],
+        + [pl.BlockSpec(memory_space=space)] * len(arrays),
         out_specs=[pl.BlockSpec(memory_space=out_space)] * len(outs),
         scratch_shapes=scratch,
         compiler_params=pltpu.CompilerParams(vmem_limit_bytes=limit * 2**20),
@@ -339,7 +339,7 @@
         + [pltpu.VMEM((shard, 2 * width), jnp.bfloat16)]
         + [pltpu.VMEM((positions, 3 * half * lanes), jnp.bfloat16)]
         + [pltpu.SemaphoreType.DMA((5,)), pltpu.SemaphoreType.DMA((4,))],
-        spaces=[pl.ANY] * 3,
+        space=pl.ANY,
         out_space=pl.ANY,
         limit=60,
     )
@@ -395,7 +395,7 @@
             [(shard, width + lanes)] * 4,
             [],
             [kept, sent],
-            flops=20 * 10**9,
+            flops=7 * 10**9,
         )
         pieces = [joined[0]] + [swap(joined[step], 4 * step) for step in (1, 2, 3)]
         text_keys = [keys_column, sent, swap(keys_column, 1), swap(sent, 1)]
@@ -425,22 +425,23 @@
 
     key_count = positions + devices * shard
     (spatial,) = call(
-        functools.partial(spatial_kernel, head_count, shard, relative, scale, len(text_keys)),
+        functools.partial(spatial_kernel, head_count, shard, relative, scale),
         "spatial",
         [(positions, half * lanes)],
         [head_kind, text_len],
         [video, *text_keys],
-        head_list
-        + [pltpu.VMEM((key_count - positions, 2 * half * lanes), jnp.bfloat16)]
-        + score_scratch(half, positions, key_count)
-        + [pltpu.SemaphoreType.DMA((len(text_keys),))],
+        head_list + score_scratch(half, positions, key_count),
         flops=4 * positions * half * lanes * key_count,
-        spaces=[pltpu.VMEM] + [pl.ANY] * len(text_keys),
     )
     if relative:
         pieces[0] = after(pieces[0], spatial)
         (text_out,) = call(
-            functools.partial(finish_kernel, head_count), "finish", [(shard, width)], [], pieces
+            functools.partial(finish_kernel, head_count), "finish",
+            [(shard, width)],
+            [],
+            pieces,
+            [pltpu.VMEM((shard, width), jnp.bfloat16), pltpu.SemaphoreType.DMA((2,))],
+            out_space=pl.ANY,
         )
     temporal = lax.all_to_all(result, "frame", split_axis=0, concat_axis=0, tiled=True)
     (video_out,) = call(

time: 50.3 us -> 50.3 us (level)
  Pallas kernels: 9.54 us -> 8.93 us
  waiting for transfers between devices: 13.4 us -> 14 us
    ppermute x12, waiting for transfers between devices: 11.9 us -> 12.5 us  [swap(): return lax.ppermute(array, 'frame', [(i, i ^ bits) for i in range(devices)])]
    pallas_call x9, Pallas kernels: 9.54 us -> 8.93 us  [call(): pl.pallas_call(kernel, out_shape=outs, in_specs=[pl.BlockSpec(memory_spac...]
  transfers between devices with their start and end apart: 14 -> 14, of which waited for: 6 -> 7; matrix products, arithmetic and copies ran while one was open for 0% -> 0% of each run, Pallas kernels for 17% -> 16%
where the time goes in v5:
time: 50.3 us; the launch traced here: 50 us
  starting transfers between devices  23.9 us (48%)
  waiting for transfers between devices  14 us (28%)
  Pallas kernels  8.93 us (18%)
  local copies, waits for them, and re-layouts  1.64 us (3%)
  between operations  1.42 us (3%)
    ppermute x12, starting transfers between devices, swap(): return lax.ppermute(array, 'frame', [(i, i ^ bits) for i in range(devices)])  12.8 us
    ppermute x12, waiting for transfers between devices, swap(): return lax.ppermute(array, 'frame', [(i, i ^ bits) for i in range(devices)])  12.5 us
    pallas_call x9, Pallas kernels, call(): pl.pallas_call(kernel, out_shape=outs, in_specs=[pl.BlockSpec(memory_spac...  8.93 us
    all_to_all x1, starting transfers between devices, body(): lax.all_to_all(packed_video, 'frame', split_axis=0, concat_axis=0, tiled=...  6.16 us
    all_to_all x1, starting transfers between devices, body(): lax.all_to_all(result, 'frame', split_axis=0, concat_axis=0, tiled=True)  4.98 us
    unnamed x16, local copies, waits for them, and re-layouts  1.64 us
    all_to_all x1, waiting for transfers between devices, body(): lax.all_to_all(packed_video, 'frame', split_axis=0, concat_axis=0, tiled=...  1.56 us
  transfers between devices with their start and end apart: 14, of which 7 were waited for; matrix products, arithmetic and copies ran while one was open for 0% of the time, Pallas kernels for 16%

profile of v5, /device:TPU:0, one launch (start us, length us, event | category | flops | bytes accessed | tf_op | source)
XLA Modules:
  0.0 50.0 jit_solution(7266833963168011476)
XLA Ops:
  0.6 0.5 %collective-permute-start.4 = (bf16[3,128,1536]{2,1,0:T(8,128)(2,1)}, bf16[3,128,1536]{2,1,0:T(8,128)(2,1)S(1)}, u32[]{:S(2)}, u32[]{:S(2)}) collective-permute-start(bf16[3,128,1536]{2,1,0:T(8,128)(2,1)} %bitcast.6), channel_id=1, source_target_pairs={{0,1},{1,0},{2,3},{3,2},{4,5},{5,4},{6,7},{7,6},{8,9},{9,8},{10,11... | collective-permute-start | bytes 3538952 | tf_op jit(solution)/shard_map/ppermute | solution.py:328
  1.1 2.1 %pack.1 = (bf16[16,3072]{1,0:T(8,128)(2,1)}, bf16[128,2304]{1,0:T(8,128)(2,1)}) custom-call(s32[12]{0:T(128)} %kind_ref.5, bf16[3,16,1536]{2,1,0:T(8,128)(2,1)} %refs_3_.3, bf16[3,128,1536]{2,1,0:T(8,128)(2,1)} %bitcast.7), custom_call_target="tpu_custom_call" | custom-call | bytes 2015256 | tf_op jit(solution)/shard_map/pack/pallas_call | solution.py:299
  3.3 0.0 copy-start.7
  3.3 2.7 %collective-permute-start = (bf16[16,3072]{1,0:T(8,128)(2,1)}, bf16[16,3072]{1,0:T(8,128)(2,1)S(1)}, u32[]{:S(2)}, u32[]{:S(2)}) collective-permute-start(bf16[16,3072]{1,0:T(8,128)(2,1)} %get-tuple-element.14.refs_0_), channel_id=1, source_target_pairs={{0,4},{1,5},{2,6},{3,7},{4,0},{5,1},{6,2},{7,3},{8,12},{9,13},{10,... | collective-permute-start | bytes 294920 | tf_op jit(solution)/shard_map/ppermute | solution.py:328
  5.9 2.6 %collective-permute-start.1 = (bf16[16,3072]{1,0:T(8,128)(2,1)}, bf16[16,3072]{1,0:T(8,128)(2,1)S(1)}, u32[]{:S(2)}, u32[]{:S(2)}) collective-permute-start(bf16[16,3072]{1,0:T(8,128)(2,1)} %get-tuple-element.14.refs_0_), channel_id=1, source_target_pairs={{0,8},{1,9},{2,10},{3,11},{4,12},{5,13},{6,14},{7,15},{8,0},{9,1},... | collective-permute-start | bytes 294920 | tf_op jit(solution)/shard_map/ppermute | solution.py:328
  8.5 0.0 collective-permute-start.2
  8.5 6.2 %all-to-all-start = ((bf16[16,8,2304]{2,1,0:T(8,128)(2,1)}), bf16[16,8,2304]{2,1,0:T(8,128)(2,1)S(1)}, u32[]{:S(2)}, u32[]{:S(2)}) async-start(bf16[16,8,2304]{2,1,0:T(8,128)(2,1)} %bitcast.13), calls=%async_computation | async-start | bytes 1179648 | tf_op jit(solution)/shard_map/all_to_all | solution.py:346
  14.7 0.0 copy-start.1
  14.7 0.0 copy-start
  14.7 0.0 collective-permute-done.refs_1_
  14.7 2.2 %collective-permute-done.1.refs_2_ = bf16[16,3072]{1,0:T(8,128)(2,1)S(1)} collective-permute-done((bf16[16,3072]{1,0:T(8,128)(2,1)}, bf16[16,3072]{1,0:T(8,128)(2,1)S(1)}, u32[]{:S(2)}, u32[]{:S(2)}) %collective-permute-start.1) | collective-permute-done | bytes 98336 | tf_op jit(solution)/shard_map/ppermute | solution.py:328
  16.9 0.0 collective-permute-done.2.refs_3_
  16.9 0.0 copy-done.7
  16.9 1.6 %collective-permute-start.3 = (bf16[64,1536]{1,0:T(8,128)(2,1)S(1)}, bf16[64,1536]{1,0:T(8,128)(2,1)S(1)}, u32[]{:S(2)}, u32[]{:S(2)}) collective-permute-start(bf16[64,1536]{1,0:T(8,128)(2,1)S(1)} %get-tuple-element.16.refs_0_), channel_id=1, source_target_pairs={{0,2},{1,3},{2,0},{3,1},{4,6},{5,7},{6,4},{7,5},{8,10},{9,11},{10,... | collective-permute-start | bytes 589832 | tf_op jit(solution)/shard_map/ppermute | solution.py:328
  18.5 0.0 copy-done.1
  18.5 0.0 collective-permute-start.5
  19.2 0.7 %collective-permute-done.5.refs_4_ = bf16[3,16,1536]{2,1,0:T(8,128)(2,1)S(1)} collective-permute-done((bf16[3,16,1536]{2,1,0:T(8,128)(2,1)S(1)}, bf16[3,16,1536]{2,1,0:T(8,128)(2,1)S(1)}, u32[]{:S(2)}, u32[]{:S(2)}) %collective-permute-start.5) | collective-permute-done | bytes 147488 | tf_op jit(solution)/shard_map/ppermute | solution.py:328
  19.9 0.0 collective-permute-done.4.refs_2_
  19.9 0.0 copy-done
  19.9 0.8 %text.2.first_ref = bf16[64,1664]{1,0:T(8,128)(2,1)S(1)} custom-call(s32[1]{0:T(128)S(6)} %copy.6.length_ref, bf16[64,1536]{1,0:T(8,128)(2,1)S(1)} %get-tuple-element.16.refs_0_, bf16[3,128,1536]{2,1,0:T(8,128)(2,1)S(1)} %bitcast.8, bf16[3,128,1536]{2,1,0:T(8,128)(2,1)S(1)} %collective-permute-done.4.refs_2_, bf16[3,16,1536]{2,1,0:T(8,128)(2,1)S(1)} %copy-done.1, ...), custom_call_target="tpu_custom_call" | custom-call | flops 113246208 | bytes 3063808 | tf_op jit(solution)/shard_map/text/pallas_call | solution.py:299
  20.7 0.0 copy-start.2
  20.7 6.0 %collective-permute-done.3.refs_0_ = bf16[64,1536]{1,0:T(8,128)(2,1)S(1)} collective-permute-done((bf16[64,1536]{1,0:T(8,128)(2,1)S(1)}, bf16[64,1536]{1,0:T(8,128)(2,1)S(1)}, u32[]{:S(2)}, u32[]{:S(2)}) %collective-permute-start.3) | collective-permute-done | bytes 196640 | tf_op jit(solution)/shard_map/ppermute | solution.py:328
  26.8 0.8 %text.3 = bf16[64,3200]{1,0:T(8,128)(2,1)S(1)} custom-call(s32[1]{0:T(128)S(6)} %copy.6.length_ref, bf16[64,1536]{1,0:T(8,128)(2,1)S(1)} %collective-permute-done.3.refs_0_, bf16[3,128,1536]{2,1,0:T(8,128)(2,1)S(1)} %bitcast.9, bf16[3,128,1536]{2,1,0:T(8,128)(2,1)S(1)} %collective-permute-done.4.refs_2_, bf16[3,16,1536]{2,1,0:T(8,128)(2,1)S(1)} %copy-done.1, ...), custom_call_target="tpu_custom_call" | custom-call | flops 113246208 | bytes 3457024 | tf_op jit(solution)/shard_map/text/pallas_call | solution.py:299
  27.6 0.0 copy-done.2
  27.6 1.1 %collective-permute-start.6 = (bf16[64,3200]{1,0:T(8,128)(2,1)S(1)}, bf16[64,3200]{1,0:T(8,128)(2,1)S(1)}, u32[]{:S(2)}, u32[]{:S(2)}) collective-permute-start(bf16[64,3200]{1,0:T(8,128)(2,1)S(1)} %text.3), channel_id=1, source_target_pairs={{0,2},{1,3},{2,0},{3,1},{4,6},{5,7},{6,4},{7,5},{8,10},{9,11},{10,... | collective-permute-start | bytes 1228808 | tf_op jit(solution)/shard_map/ppermute | solution.py:328
  28.7 0.0 collective-permute-start.7
  28.7 1.6 %all-to-all-done = bf16[16,8,2304]{2,1,0:T(8,128)(2,1)S(1)} async-done(((bf16[16,8,2304]{2,1,0:T(8,128)(2,1)}), bf16[16,8,2304]{2,1,0:T(8,128)(2,1)S(1)}, u32[]{:S(2)}, u32[]{:S(2)}) %all-to-all-start) | async-done | bytes 589856 | tf_op jit(solution)/shard_map/all_to_all | solution.py:346
  30.3 1.2 %temporal.1 = bf16[128,768]{1,0:T(8,128)(2,1)} custom-call(bf16[128,2304]{1,0:T(8,128)(2,1)S(1)} %bitcast.11), custom_call_target="tpu_custom_call" | custom-call | flops 50331648 | bytes 786432 | tf_op jit(solution)/shard_map/temporal/pallas_call | solution.py:299
  31.4 5.0 %all-to-all-start.1 = ((bf16[16,8,768]{2,1,0:T(8,128)(2,1)}), bf16[16,8,768]{2,1,0:T(8,128)(2,1)S(1)}, u32[]{:S(2)}, u32[]{:S(2)}) async-start(bf16[16,8,768]{2,1,0:T(8,128)(2,1)} %bitcast.3), calls=%async_computation.1 | async-start | bytes 393216 | tf_op jit(solution)/shard_map/all_to_all | solution.py:446
  36.4 0.0 copy-start.6
  36.4 2.7 %collective-permute-done.6.refs_1_.second_ref = bf16[64,3200]{1,0:T(8,128)(2,1)S(1)} collective-permute-done((bf16[64,3200]{1,0:T(8,128)(2,1)S(1)}, bf16[64,3200]{1,0:T(8,128)(2,1)S(1)}, u32[]{:S(2)}, u32[]{:S(2)}) %collective-permute-start.6) | collective-permute-done | bytes 409632 | tf_op jit(solution)/shard_map/ppermute | solution.py:328
  39.1 0.0 collective-permute-start.8
  39.1 0.0 copy-done.3
  39.1 0.3 merge.1
  39.5 1.7 %collective-permute-start.10 = (bf16[16,1664]{1,0:T(8,128)(2,1)S(1)}, bf16[16,1664]{1,0:T(8,128)(2,1)S(1)}, u32[]{:S(2)}, u32[]{:S(2)}) collective-permute-start(bf16[16,1664]{1,0:T(8,128)(2,1)S(1)} %get-tuple-element.24), channel_id=1, source_target_pairs={{0,8},{1,9},{2,10},{3,11},{4,12},{5,13},{6,14},{7,15},{8,0},{9,1},... | collective-permute-start | bytes 159752 | tf_op jit(solution)/shard_map/ppermute | solution.py:328
  41.1 2.2 %collective-permute-start.11 = (bf16[16,1664]{1,0:T(8,128)(2,1)S(1)}, bf16[16,1664]{1,0:T(8,128)(2,1)S(1)}, u32[]{:S(2)}, u32[]{:S(2)}) collective-permute-start(bf16[16,1664]{1,0:T(8,128)(2,1)S(1)} %get-tuple-element.25), channel_id=1, source_target_pairs={{0,12},{1,13},{2,14},{3,15},{4,8},{5,9},{6,10},{7,11},{8,4},{9,5},... | collective-permute-start | bytes 159752 | tf_op jit(solution)/shard_map/ppermute | solution.py:328
  43.3 0.5 collective-permute-start.9
  43.8 0.0 collective-permute-done.7.refs_2_
  43.8 0.7 %copy-done.4 = bf16[64,1536]{1,0:T(8,128)(2,1)} copy-done((bf16[64,1536]{1,0:T(8,128)(2,1)}, bf16[64,1536]{1,0:T(8,128)(2,1)S(1)}, u32[]{:S(2)}) %copy-start.4) | copy-done | bytes 196632
  44.5 0.0 collective-permute-done.8.refs_3_
  44.5 0.9 %copy-done.5 = bf16[64,1536]{1,0:T(8,128)(2,1)S(1)} copy-done((bf16[64,1536]{1,0:T(8,128)(2,1)S(1)}, bf16[64,1536]{1,0:T(8,128)(2,1)}, u32[]{:S(2)}) %copy-start.5) | copy-done | bytes 196632
  45.4 1.3 %spatial.1.spatial_ref = bf16[128,768]{1,0:T(8,128)(2,1)S(1)} custom-call(s32[12]{0:T(128)S(1)} %copy-done.6, s32[1]{0:T(128)S(6)} %copy.6.length_ref, bf16[3,128,1536]{2,1,0:T(8,128)(2,1)S(1)} %bitcast.10, bf16[64,1536]{1,0:T(8,128)(2,1)S(1)} %get-tuple-element.15.refs_5_.refs_0_, bf16[64,3200]{1,0:T(8,128)(2,1)S(1)} %collective-permute-done.6.refs_1_.second_ref, ...), custom_call_target="tpu_custom_call" | custom-call | flops 150994944 | bytes 2588672 | tf_op jit(solution)/shard_map/spatial/pallas_call | solution.py:299
  46.7 0.0 all-to-all-done.1
  46.7 1.4 %join.1 = bf16[128,1536]{1,0:T(8,128)(2,1)} custom-call(s32[12]{0:T(128)S(1)} %copy-done.6, bf16[128,768]{1,0:T(8,128)(2,1)S(1)} %spatial.1.spatial_ref, bf16[128,768]{1,0:T(8,128)(2,1)S(1)} %bitcast.12), custom_call_target="tpu_custom_call" | custom-call | bytes 786432 | tf_op jit(solution)/shard_map/join/pallas_call | solution.py:299
  48.1 0.5 collective-permute-done.10.refs_2_
  48.6 0.0 collective-permute-done.11.refs_3_
  48.6 0.4 collective-permute-done.9.refs_1_
  49.0 1.0 %finish.1 = bf16[16,1536]{1,0:T(8,128)(2,1)} custom-call(bf16[16,1664]{1,0:T(8,128)(2,1)S(1)} %get-tuple-element.22.refs_0_, bf16[16,1664]{1,0:T(8,128)(2,1)S(1)} %collective-permute-done.9.refs_1_, bf16[16,1664]{1,0:T(8,128)(2,1)S(1)} %collective-permute-done.10.refs_2_, bf16[16,1664]{1,0:T(8,128)(2,1)S(1)} %collective-permute-done.11.refs_3_), custom_call_target="tpu_custom_call" | custom-call | bytes 262144 | tf_op jit(solution)/shard_map/finish/pallas_call | solution.py:299
  (5 shorter events, 0.0 us)
Async XLA Ops:
  0.6 19.3 %collective-permute-start.4 = (bf16[3,128,1536]{2,1,0:T(8,128)(2,1)}, bf16[3,128,1536]{2,1,0:T(8,128)(2,1)S(1)}, u32[]{:S(2)}, u32[]{:S(2)}) collective-permute-start(bf16[3,128,1536]{2,1,0:T(8,128)(2,1)} %bitcast.6), channel_id=1, source_target_pairs={{0,1},{1,0},{2,3},{3,2},{4,5},{5,4},{6,7},{7,6},{8,9},{9,8},{10,11... | collective-permute-start | bytes 3538952 | tf_op jit(solution)/shard_map/ppermute | solution.py:328
  3.3 13.6 %copy-start.7 = (bf16[16,3072]{1,0:T(8,128)(2,1)S(1)}, bf16[16,3072]{1,0:T(8,128)(2,1)}, u32[]{:S(2)}) copy-start(bf16[16,3072]{1,0:T(8,128)(2,1)} %get-tuple-element.14.refs_0_) | copy-start | bytes 294916
  3.3 11.4 %collective-permute-start = (bf16[16,3072]{1,0:T(8,128)(2,1)}, bf16[16,3072]{1,0:T(8,128)(2,1)S(1)}, u32[]{:S(2)}, u32[]{:S(2)}) collective-permute-start(bf16[16,3072]{1,0:T(8,128)(2,1)} %get-tuple-element.14.refs_0_), channel_id=1, source_target_pairs={{0,4},{1,5},{2,6},{3,7},{4,0},{5,1},{6,2},{7,3},{8,12},{9,13},{10,... | collective-permute-start | bytes 294920 | tf_op jit(solution)/shard_map/ppermute | solution.py:328
  5.9 11.0 %collective-permute-start.1 = (bf16[16,3072]{1,0:T(8,128)(2,1)}, bf16[16,3072]{1,0:T(8,128)(2,1)S(1)}, u32[]{:S(2)}, u32[]{:S(2)}) collective-permute-start(bf16[16,3072]{1,0:T(8,128)(2,1)} %get-tuple-element.14.refs_0_), channel_id=1, source_target_pairs={{0,8},{1,9},{2,10},{3,11},{4,12},{5,13},{6,14},{7,15},{8,0},{9,1},... | collective-permute-start | bytes 294920 | tf_op jit(solution)/shard_map/ppermute | solution.py:328
  8.5 8.4 %collective-permute-start.2 = (bf16[16,3072]{1,0:T(8,128)(2,1)}, bf16[16,3072]{1,0:T(8,128)(2,1)S(1)}, u32[]{:S(2)}, u32[]{:S(2)}) collective-permute-start(bf16[16,3072]{1,0:T(8,128)(2,1)} %get-tuple-element.14.refs_0_), channel_id=1, source_target_pairs={{0,12},{1,13},{2,14},{3,15},{4,8},{5,9},{6,10},{7,11},{8,4},{9,5},... | collective-permute-start | bytes 294920 | tf_op jit(solution)/shard_map/ppermute | solution.py:328
  8.5 21.7 %all-to-all-start = ((bf16[16,8,2304]{2,1,0:T(8,128)(2,1)}), bf16[16,8,2304]{2,1,0:T(8,128)(2,1)S(1)}, u32[]{:S(2)}, u32[]{:S(2)}) async-start(bf16[16,8,2304]{2,1,0:T(8,128)(2,1)} %bitcast.13), calls=%async_computation | async-start | bytes 1179648 | tf_op jit(solution)/shard_map/all_to_all | solution.py:346
  14.7 3.8 %copy-start.1 = (bf16[3,16,1536]{2,1,0:T(8,128)(2,1)S(1)}, bf16[3,16,1536]{2,1,0:T(8,128)(2,1)}, u32[]{:S(2)}) copy-start(bf16[3,16,1536]{2,1,0:T(8,128)(2,1)} %refs_3_.3) | copy-start | bytes 442372
  14.7 5.2 %copy-start = (bf16[3,1,128,1536]{3,2,1,0:T(8,128)(2,1)S(1)}, bf16[3,1,128,1536]{3,2,1,0:T(8,128)(2,1)}, u32[]{:S(2)}) copy-start(bf16[3,1,128,1536]{3,2,1,0:T(8,128)(2,1)} %param.4) | copy-start | bytes 3538948
  16.9 9.8 %collective-permute-start.3 = (bf16[64,1536]{1,0:T(8,128)(2,1)S(1)}, bf16[64,1536]{1,0:T(8,128)(2,1)S(1)}, u32[]{:S(2)}, u32[]{:S(2)}) collective-permute-start(bf16[64,1536]{1,0:T(8,128)(2,1)S(1)} %get-tuple-element.16.refs_0_), channel_id=1, source_target_pairs={{0,2},{1,3},{2,0},{3,1},{4,6},{5,7},{6,4},{7,5},{8,10},{9,11},{10,... | collective-permute-start | bytes 589832 | tf_op jit(solution)/shard_map/ppermute | solution.py:328
  18.5 1.4 %collective-permute-start.5 = (bf16[3,16,1536]{2,1,0:T(8,128)(2,1)S(1)}, bf16[3,16,1536]{2,1,0:T(8,128)(2,1)S(1)}, u32[]{:S(2)}, u32[]{:S(2)}) collective-permute-start(bf16[3,16,1536]{2,1,0:T(8,128)(2,1)S(1)} %copy-done.1), channel_id=1, source_target_pairs={{0,1},{1,0},{2,3},{3,2},{4,5},{5,4},{6,7},{7,6},{8,9},{9,8},{10,11... | collective-permute-start | bytes 442376 | tf_op jit(solution)/shard_map/ppermute | solution.py:328
  20.7 6.9 %copy-start.2 = (bf16[64,1664]{1,0:T(8,128)(2,1)}, bf16[64,1664]{1,0:T(8,128)(2,1)S(1)}, u32[]{:S(2)}) copy-start(bf16[64,1664]{1,0:T(8,128)(2,1)S(1)} %text.2.first_ref) | copy-start | bytes 638980
  27.6 11.5 %collective-permute-start.6 = (bf16[64,3200]{1,0:T(8,128)(2,1)S(1)}, bf16[64,3200]{1,0:T(8,128)(2,1)S(1)}, u32[]{:S(2)}, u32[]{:S(2)}) collective-permute-start(bf16[64,3200]{1,0:T(8,128)(2,1)S(1)} %text.3), channel_id=1, source_target_pairs={{0,2},{1,3},{2,0},{3,1},{4,6},{5,7},{6,4},{7,5},{8,10},{9,11},{10,... | collective-permute-start | bytes 1228808 | tf_op jit(solution)/shard_map/ppermute | solution.py:328
  28.7 10.4 %copy-start.3 = (bf16[64,1664]{1,0:T(8,128)(2,1)S(1)}, bf16[64,1664]{1,0:T(8,128)(2,1)}, u32[]{:S(2)}) copy-start(bf16[64,1664]{1,0:T(8,128)(2,1)} %copy-done.2) | copy-start | bytes 638980
  28.7 15.1 %collective-permute-start.7 = (bf16[64,1536]{1,0:T(8,128)(2,1)S(1)}, bf16[64,1536]{1,0:T(8,128)(2,1)S(1)}, u32[]{:S(2)}, u32[]{:S(2)}) collective-permute-start(bf16[64,1536]{1,0:T(8,128)(2,1)S(1)} %get-tuple-element.15.refs_5_.refs_0_), channel_id=1, source_target_pairs={{0,1},{1,0},{2,3},{3,2},{4,5},{5,4},{6,7},{7,6},{8,9},{9,8},{10,11... | collective-permute-start | bytes 589832 | tf_op jit(solution)/shard_map/ppermute | solution.py:328
  31.4 15.2 %all-to-all-start.1 = ((bf16[16,8,768]{2,1,0:T(8,128)(2,1)}), bf16[16,8,768]{2,1,0:T(8,128)(2,1)S(1)}, u32[]{:S(2)}, u32[]{:S(2)}) async-start(bf16[16,8,768]{2,1,0:T(8,128)(2,1)} %bitcast.3), calls=%async_computation.1 | async-start | bytes 393216 | tf_op jit(solution)/shard_map/all_to_all | solution.py:446
  36.4 8.0 %copy-start.6 = (s32[12]{0:T(128)S(1)}, s32[12]{0:T(128)}, u32[]{:S(2)}) copy-start(s32[12]{0:T(128)} %kind_ref.5) | copy-start | bytes 148
  39.1 5.4 %collective-permute-start.8 = (bf16[64,3200]{1,0:T(8,128)(2,1)S(1)}, bf16[64,3200]{1,0:T(8,128)(2,1)S(1)}, u32[]{:S(2)}, u32[]{:S(2)}) collective-permute-start(bf16[64,3200]{1,0:T(8,128)(2,1)S(1)} %collective-permute-done.6.refs_1_.second_ref), channel_id=1, source_target_pairs={{0,1},{1,0},{2,3},{3,2},{4,5},{5,4},{6,7},{7,6},{8,9},{9,8},{10,11... | collective-permute-start | bytes 1228808 | tf_op jit(solution)/shard_map/ppermute | solution.py:328
  39.5 9.1 %collective-permute-start.10 = (bf16[16,1664]{1,0:T(8,128)(2,1)S(1)}, bf16[16,1664]{1,0:T(8,128)(2,1)S(1)}, u32[]{:S(2)}, u32[]{:S(2)}) collective-permute-start(bf16[16,1664]{1,0:T(8,128)(2,1)S(1)} %get-tuple-element.24), channel_id=1, source_target_pairs={{0,8},{1,9},{2,10},{3,11},{4,12},{5,13},{6,14},{7,15},{8,0},{9,1},... | collective-permute-start | bytes 159752 | tf_op jit(solution)/shard_map/ppermute | solution.py:328
  41.1 7.4 %collective-permute-start.11 = (bf16[16,1664]{1,0:T(8,128)(2,1)S(1)}, bf16[16,1664]{1,0:T(8,128)(2,1)S(1)}, u32[]{:S(2)}, u32[]{:S(2)}) collective-permute-start(bf16[16,1664]{1,0:T(8,128)(2,1)S(1)} %get-tuple-element.25), channel_id=1, source_target_pairs={{0,12},{1,13},{2,14},{3,15},{4,8},{5,9},{6,10},{7,11},{8,4},{9,5},... | collective-permute-start | bytes 159752 | tf_op jit(solution)/shard_map/ppermute | solution.py:328
  43.3 5.7 %collective-permute-start.9 = (bf16[16,1664]{1,0:T(8,128)(2,1)S(1)}, bf16[16,1664]{1,0:T(8,128)(2,1)S(1)}, u32[]{:S(2)}, u32[]{:S(2)}) collective-permute-start(bf16[16,1664]{1,0:T(8,128)(2,1)S(1)} %get-tuple-element.23), channel_id=1, source_target_pairs={{0,4},{1,5},{2,6},{3,7},{4,0},{5,1},{6,2},{7,3},{8,12},{9,13},{10,... | collective-permute-start | bytes 159752 | tf_op jit(solution)/shard_map/ppermute | solution.py:328
  43.8 0.7 %copy-start.4 = (bf16[64,1536]{1,0:T(8,128)(2,1)}, bf16[64,1536]{1,0:T(8,128)(2,1)S(1)}, u32[]{:S(2)}) copy-start(bf16[64,1536]{1,0:T(8,128)(2,1)S(1)} %collective-permute-done.7.refs_2_) | copy-start | bytes 589828
  44.5 0.9 %copy-start.5 = (bf16[64,1536]{1,0:T(8,128)(2,1)S(1)}, bf16[64,1536]{1,0:T(8,128)(2,1)}, u32[]{:S(2)}) copy-start(bf16[64,1536]{1,0:T(8,128)(2,1)} %copy-done.4) | copy-start | bytes 589828

commit v6 on v5

--- a/solution.py
+++ b/solution.py
@@ -398,7 +398,7 @@
             flops=7 * 10**9,
         )
         pieces = [joined[0]] + [swap(joined[step], 4 * step) for step in (1, 2, 3)]
-        text_keys = [keys_column, sent, swap(keys_column, 1), swap(sent, 1)]
+        text_keys = [keys_column, sent, swap(keys_column, 1), swap(sent[:, width + lanes :], 1)]
     else:
         (result,) = attend_temporal(block)
         side = [[2 * chip + core for chip in range(devices // 2)] for core in range(2)]

time: 50.3 us -> 50.4 us (level)
  no operation moved by 1% of the time
where the time goes in v6:
time: 50.4 us; the launch traced here: 50 us
  starting transfers between devices  24 us (48%)
  waiting for transfers between devices  14 us (28%)
  Pallas kernels  8.93 us (18%)
  local copies, waits for them, and re-layouts  1.65 us (3%)
  between operations  1.44 us (3%)
    ppermute x12, starting transfers between devices, swap(): return lax.ppermute(array, 'frame', [(i, i ^ bits) for i in range(devices)])  12.8 us
    ppermute x12, waiting for transfers between devices, swap(): return lax.ppermute(array, 'frame', [(i, i ^ bits) for i in range(devices)])  12.4 us
    pallas_call x9, Pallas kernels, call(): pl.pallas_call(kernel, out_shape=outs, in_specs=[pl.BlockSpec(memory_spac...  8.93 us
    all_to_all x1, starting transfers between devices, body(): lax.all_to_all(packed_video, 'frame', split_axis=0, concat_axis=0, tiled=...  6.16 us
    all_to_all x1, starting transfers between devices, body(): lax.all_to_all(result, 'frame', split_axis=0, concat_axis=0, tiled=True)  4.98 us
    unnamed x16, local copies, waits for them, and re-layouts  1.64 us
    all_to_all x1, waiting for transfers between devices, body(): lax.all_to_all(packed_video, 'frame', split_axis=0, concat_axis=0, tiled=...  1.56 us
  transfers between devices with their start and end apart: 14, of which 7 were waited for; matrix products, arithmetic and copies ran while one was open for 0% of the time, Pallas kernels for 16%

profile of v6, /device:TPU:0, one launch (start us, length us, event | category | flops | bytes accessed | tf_op | source)
XLA Modules:
  0.0 50.0 jit_solution(218464327373549479)
XLA Ops:
  0.6 0.5 %collective-permute-start.4 = (bf16[3,128,1536]{2,1,0:T(8,128)(2,1)}, bf16[3,128,1536]{2,1,0:T(8,128)(2,1)S(1)}, u32[]{:S(2)}, u32[]{:S(2)}) collective-permute-start(bf16[3,128,1536]{2,1,0:T(8,128)(2,1)} %bitcast.6), channel_id=1, source_target_pairs={{0,1},{1,0},{2,3},{3,2},{4,5},{5,4},{6,7},{7,6},{8,9},{9,8},{10,11... | collective-permute-start | bytes 3538952 | tf_op jit(solution)/shard_map/ppermute | solution.py:328
  1.1 2.1 %pack.1 = (bf16[16,3072]{1,0:T(8,128)(2,1)}, bf16[128,2304]{1,0:T(8,128)(2,1)}) custom-call(s32[12]{0:T(128)} %kind_ref.5, bf16[3,16,1536]{2,1,0:T(8,128)(2,1)} %refs_3_.3, bf16[3,128,1536]{2,1,0:T(8,128)(2,1)} %bitcast.7), custom_call_target="tpu_custom_call" | custom-call | bytes 2015256 | tf_op jit(solution)/shard_map/pack/pallas_call | solution.py:299
  3.3 0.0 copy-start.7
  3.3 2.7 %collective-permute-start = (bf16[16,3072]{1,0:T(8,128)(2,1)}, bf16[16,3072]{1,0:T(8,128)(2,1)S(1)}, u32[]{:S(2)}, u32[]{:S(2)}) collective-permute-start(bf16[16,3072]{1,0:T(8,128)(2,1)} %get-tuple-element.14.refs_0_), channel_id=1, source_target_pairs={{0,4},{1,5},{2,6},{3,7},{4,0},{5,1},{6,2},{7,3},{8,12},{9,13},{10,... | collective-permute-start | bytes 294920 | tf_op jit(solution)/shard_map/ppermute | solution.py:328
  5.9 2.6 %collective-permute-start.1 = (bf16[16,3072]{1,0:T(8,128)(2,1)}, bf16[16,3072]{1,0:T(8,128)(2,1)S(1)}, u32[]{:S(2)}, u32[]{:S(2)}) collective-permute-start(bf16[16,3072]{1,0:T(8,128)(2,1)} %get-tuple-element.14.refs_0_), channel_id=1, source_target_pairs={{0,8},{1,9},{2,10},{3,11},{4,12},{5,13},{6,14},{7,15},{8,0},{9,1},... | collective-permute-start | bytes 294920 | tf_op jit(solution)/shard_map/ppermute | solution.py:328
  8.5 0.0 collective-permute-start.2
  8.5 6.2 %all-to-all-start = ((bf16[16,8,2304]{2,1,0:T(8,128)(2,1)}), bf16[16,8,2304]{2,1,0:T(8,128)(2,1)S(1)}, u32[]{:S(2)}, u32[]{:S(2)}) async-start(bf16[16,8,2304]{2,1,0:T(8,128)(2,1)} %bitcast.13), calls=%async_computation | async-start | bytes 1179648 | tf_op jit(solution)/shard_map/all_to_all | solution.py:346
  14.7 0.0 copy-start.1
  14.7 0.0 copy-start
  14.7 0.0 collective-permute-done.refs_1_
  14.7 2.2 %collective-permute-done.1.refs_2_ = bf16[16,3072]{1,0:T(8,128)(2,1)S(1)} collective-permute-done((bf16[16,3072]{1,0:T(8,128)(2,1)}, bf16[16,3072]{1,0:T(8,128)(2,1)S(1)}, u32[]{:S(2)}, u32[]{:S(2)}) %collective-permute-start.1) | collective-permute-done | bytes 98336 | tf_op jit(solution)/shard_map/ppermute | solution.py:328
  16.9 0.0 collective-permute-done.2.refs_3_
  16.9 0.0 copy-done.7
  16.9 1.6 %collective-permute-start.3 = (bf16[64,1536]{1,0:T(8,128)(2,1)S(1)}, bf16[64,1536]{1,0:T(8,128)(2,1)S(1)}, u32[]{:S(2)}, u32[]{:S(2)}) collective-permute-start(bf16[64,1536]{1,0:T(8,128)(2,1)S(1)} %get-tuple-element.16.refs_0_), channel_id=1, source_target_pairs={{0,2},{1,3},{2,0},{3,1},{4,6},{5,7},{6,4},{7,5},{8,10},{9,11},{10,... | collective-permute-start | bytes 589832 | tf_op jit(solution)/shard_map/ppermute | solution.py:328
  18.5 0.0 copy-done.1
  18.5 0.0 collective-permute-start.5
  19.2 0.7 %collective-permute-done.5.refs_4_ = bf16[3,16,1536]{2,1,0:T(8,128)(2,1)S(1)} collective-permute-done((bf16[3,16,1536]{2,1,0:T(8,128)(2,1)S(1)}, bf16[3,16,1536]{2,1,0:T(8,128)(2,1)S(1)}, u32[]{:S(2)}, u32[]{:S(2)}) %collective-permute-start.5) | collective-permute-done | bytes 147488 | tf_op jit(solution)/shard_map/ppermute | solution.py:328
  19.9 0.0 collective-permute-done.4.refs_2_
  19.9 0.0 copy-done
  19.9 0.8 %text.2.first_ref = bf16[64,1664]{1,0:T(8,128)(2,1)S(1)} custom-call(s32[1]{0:T(128)S(6)} %copy.6.length_ref, bf16[64,1536]{1,0:T(8,128)(2,1)S(1)} %get-tuple-element.16.refs_0_, bf16[3,128,1536]{2,1,0:T(8,128)(2,1)S(1)} %bitcast.8, bf16[3,128,1536]{2,1,0:T(8,128)(2,1)S(1)} %collective-permute-done.4.refs_2_, bf16[3,16,1536]{2,1,0:T(8,128)(2,1)S(1)} %copy-done.1, ...), custom_call_target="tpu_custom_call" | custom-call | flops 113246208 | bytes 3063808 | tf_op jit(solution)/shard_map/text/pallas_call | solution.py:299
  20.7 0.0 copy-start.2
  20.7 6.0 %collective-permute-done.3.refs_0_ = bf16[64,1536]{1,0:T(8,128)(2,1)S(1)} collective-permute-done((bf16[64,1536]{1,0:T(8,128)(2,1)S(1)}, bf16[64,1536]{1,0:T(8,128)(2,1)S(1)}, u32[]{:S(2)}, u32[]{:S(2)}) %collective-permute-start.3) | collective-permute-done | bytes 196640 | tf_op jit(solution)/shard_map/ppermute | solution.py:328
  26.8 0.8 %text.3 = bf16[64,3200]{1,0:T(8,128)(2,1)S(1)} custom-call(s32[1]{0:T(128)S(6)} %copy.6.length_ref, bf16[64,1536]{1,0:T(8,128)(2,1)S(1)} %collective-permute-done.3.refs_0_, bf16[3,128,1536]{2,1,0:T(8,128)(2,1)S(1)} %bitcast.9, bf16[3,128,1536]{2,1,0:T(8,128)(2,1)S(1)} %collective-permute-done.4.refs_2_, bf16[3,16,1536]{2,1,0:T(8,128)(2,1)S(1)} %copy-done.1, ...), custom_call_target="tpu_custom_call" | custom-call | flops 113246208 | bytes 3457024 | tf_op jit(solution)/shard_map/text/pallas_call | solution.py:299
  27.6 1.1 %collective-permute-start.6 = (bf16[64,3200]{1,0:T(8,128)(2,1)S(1)}, bf16[64,3200]{1,0:T(8,128)(2,1)S(1)}, u32[]{:S(2)}, u32[]{:S(2)}) collective-permute-start(bf16[64,3200]{1,0:T(8,128)(2,1)S(1)} %text.3), channel_id=1, source_target_pairs={{0,2},{1,3},{2,0},{3,1},{4,6},{5,7},{6,4},{7,5},{8,10},{9,11},{10,... | collective-permute-start | bytes 1228808 | tf_op jit(solution)/shard_map/ppermute | solution.py:328
  28.7 0.0 collective-permute-start.7
  28.7 1.6 %all-to-all-done = bf16[16,8,2304]{2,1,0:T(8,128)(2,1)S(1)} async-done(((bf16[16,8,2304]{2,1,0:T(8,128)(2,1)}), bf16[16,8,2304]{2,1,0:T(8,128)(2,1)S(1)}, u32[]{:S(2)}, u32[]{:S(2)}) %all-to-all-start) | async-done | bytes 589856 | tf_op jit(solution)/shard_map/all_to_all | solution.py:346
  30.3 1.2 %temporal.1 = bf16[128,768]{1,0:T(8,128)(2,1)} custom-call(bf16[128,2304]{1,0:T(8,128)(2,1)S(1)} %bitcast.11), custom_call_target="tpu_custom_call" | custom-call | flops 50331648 | bytes 786432 | tf_op jit(solution)/shard_map/temporal/pallas_call | solution.py:299
  31.4 5.0 %all-to-all-start.1 = ((bf16[16,8,768]{2,1,0:T(8,128)(2,1)}), bf16[16,8,768]{2,1,0:T(8,128)(2,1)S(1)}, u32[]{:S(2)}, u32[]{:S(2)}) async-start(bf16[16,8,768]{2,1,0:T(8,128)(2,1)} %bitcast.3), calls=%async_computation.1 | async-start | bytes 393216 | tf_op jit(solution)/shard_map/all_to_all | solution.py:446
  36.4 2.7 %collective-permute-done.6.refs_1_.second_ref = bf16[64,3200]{1,0:T(8,128)(2,1)S(1)} collective-permute-done((bf16[64,3200]{1,0:T(8,128)(2,1)S(1)}, bf16[64,3200]{1,0:T(8,128)(2,1)S(1)}, u32[]{:S(2)}, u32[]{:S(2)}) %collective-permute-start.6) | collective-permute-done | bytes 409632 | tf_op jit(solution)/shard_map/ppermute | solution.py:328
  39.1 0.0 copy-start.6
  39.1 0.1 collective-permute-start.8
  39.2 0.0 copy-done.3
  39.2 0.3 merge.1
  39.6 1.7 %collective-permute-start.10 = (bf16[16,1664]{1,0:T(8,128)(2,1)S(1)}, bf16[16,1664]{1,0:T(8,128)(2,1)S(1)}, u32[]{:S(2)}, u32[]{:S(2)}) collective-permute-start(bf16[16,1664]{1,0:T(8,128)(2,1)S(1)} %get-tuple-element.24), channel_id=1, source_target_pairs={{0,8},{1,9},{2,10},{3,11},{4,12},{5,13},{6,14},{7,15},{8,0},{9,1},... | collective-permute-start | bytes 159752 | tf_op jit(solution)/shard_map/ppermute | solution.py:328
  41.2 2.2 %collective-permute-start.11 = (bf16[16,1664]{1,0:T(8,128)(2,1)S(1)}, bf16[16,1664]{1,0:T(8,128)(2,1)S(1)}, u32[]{:S(2)}, u32[]{:S(2)}) collective-permute-start(bf16[16,1664]{1,0:T(8,128)(2,1)S(1)} %get-tuple-element.25), channel_id=1, source_target_pairs={{0,12},{1,13},{2,14},{3,15},{4,8},{5,9},{6,10},{7,11},{8,4},{9,5},... | collective-permute-start | bytes 159752 | tf_op jit(solution)/shard_map/ppermute | solution.py:328
  43.4 0.5 collective-permute-start.9
  43.9 0.0 collective-permute-done.7.refs_2_
  43.9 0.7 %copy-done.4 = bf16[64,1536]{1,0:T(8,128)(2,1)} copy-done((bf16[64,1536]{1,0:T(8,128)(2,1)}, bf16[64,1536]{1,0:T(8,128)(2,1)S(1)}, u32[]{:S(2)}) %copy-start.4) | copy-done | bytes 196632
  44.6 0.0 collective-permute-done.8.refs_3_
  44.6 0.0 copy-done.6
  44.6 0.9 %copy-done.5 = bf16[64,1536]{1,0:T(8,128)(2,1)S(1)} copy-done((bf16[64,1536]{1,0:T(8,128)(2,1)S(1)}, bf16[64,1536]{1,0:T(8,128)(2,1)}, u32[]{:S(2)}) %copy-start.5) | copy-done | bytes 196632
  45.5 1.3 %spatial.1.spatial_ref = bf16[128,768]{1,0:T(8,128)(2,1)S(1)} custom-call(s32[12]{0:T(128)S(1)} %copy-done.6, s32[1]{0:T(128)S(6)} %copy.6.length_ref, bf16[3,128,1536]{2,1,0:T(8,128)(2,1)S(1)} %bitcast.10, bf16[64,1536]{1,0:T(8,128)(2,1)S(1)} %get-tuple-element.15.refs_5_.refs_0_, bf16[64,3200]{1,0:T(8,128)(2,1)S(1)} %collective-permute-done.6.refs_1_.second_ref, ...), custom_call_target="tpu_custom_call" | custom-call | flops 150994944 | bytes 2375680 | tf_op jit(solution)/shard_map/spatial/pallas_call | solution.py:299
  46.8 0.0 all-to-all-done.1
  46.8 1.4 %join.1 = bf16[128,1536]{1,0:T(8,128)(2,1)} custom-call(s32[12]{0:T(128)S(1)} %copy-done.6, bf16[128,768]{1,0:T(8,128)(2,1)S(1)} %spatial.1.spatial_ref, bf16[128,768]{1,0:T(8,128)(2,1)S(1)} %bitcast.12), custom_call_target="tpu_custom_call" | custom-call | bytes 786432 | tf_op jit(solution)/shard_map/join/pallas_call | solution.py:299
  48.2 0.4 collective-permute-done.10.refs_2_
  48.6 0.0 collective-permute-done.11.refs_3_
  48.6 0.4 collective-permute-done.9.refs_1_
  49.0 1.0 %finish.1 = bf16[16,1536]{1,0:T(8,128)(2,1)} custom-call(bf16[16,1664]{1,0:T(8,128)(2,1)S(1)} %get-tuple-element.22.refs_0_, bf16[16,1664]{1,0:T(8,128)(2,1)S(1)} %collective-permute-done.9.refs_1_, bf16[16,1664]{1,0:T(8,128)(2,1)S(1)} %collective-permute-done.10.refs_2_, bf16[16,1664]{1,0:T(8,128)(2,1)S(1)} %collective-permute-done.11.refs_3_), custom_call_target="tpu_custom_call" | custom-call | bytes 262144 | tf_op jit(solution)/shard_map/finish/pallas_call | solution.py:299
  (6 shorter events, 0.0 us)
Async XLA Ops:
  0.6 19.3 %collective-permute-start.4 = (bf16[3,128,1536]{2,1,0:T(8,128)(2,1)}, bf16[3,128,1536]{2,1,0:T(8,128)(2,1)S(1)}, u32[]{:S(2)}, u32[]{:S(2)}) collective-permute-start(bf16[3,128,1536]{2,1,0:T(8,128)(2,1)} %bitcast.6), channel_id=1, source_target_pairs={{0,1},{1,0},{2,3},{3,2},{4,5},{5,4},{6,7},{7,6},{8,9},{9,8},{10,11... | collective-permute-start | bytes 3538952 | tf_op jit(solution)/shard_map/ppermute | solution.py:328
  3.3 13.6 %copy-start.7 = (bf16[16,3072]{1,0:T(8,128)(2,1)S(1)}, bf16[16,3072]{1,0:T(8,128)(2,1)}, u32[]{:S(2)}) copy-start(bf16[16,3072]{1,0:T(8,128)(2,1)} %get-tuple-element.14.refs_0_) | copy-start | bytes 294916
  3.3 11.4 %collective-permute-start = (bf16[16,3072]{1,0:T(8,128)(2,1)}, bf16[16,3072]{1,0:T(8,128)(2,1)S(1)}, u32[]{:S(2)}, u32[]{:S(2)}) collective-permute-start(bf16[16,3072]{1,0:T(8,128)(2,1)} %get-tuple-element.14.refs_0_), channel_id=1, source_target_pairs={{0,4},{1,5},{2,6},{3,7},{4,0},{5,1},{6,2},{7,3},{8,12},{9,13},{10,... | collective-permute-start | bytes 294920 | tf_op jit(solution)/shard_map/ppermute | solution.py:328
  5.9 11.0 %collective-permute-start.1 = (bf16[16,3072]{1,0:T(8,128)(2,1)}, bf16[16,3072]{1,0:T(8,128)(2,1)S(1)}, u32[]{:S(2)}, u32[]{:S(2)}) collective-permute-start(bf16[16,3072]{1,0:T(8,128)(2,1)} %get-tuple-element.14.refs_0_), channel_id=1, source_target_pairs={{0,8},{1,9},{2,10},{3,11},{4,12},{5,13},{6,14},{7,15},{8,0},{9,1},... | collective-permute-start | bytes 294920 | tf_op jit(solution)/shard_map/ppermute | solution.py:328
  8.5 8.4 %collective-permute-start.2 = (bf16[16,3072]{1,0:T(8,128)(2,1)}, bf16[16,3072]{1,0:T(8,128)(2,1)S(1)}, u32[]{:S(2)}, u32[]{:S(2)}) collective-permute-start(bf16[16,3072]{1,0:T(8,128)(2,1)} %get-tuple-element.14.refs_0_), channel_id=1, source_target_pairs={{0,12},{1,13},{2,14},{3,15},{4,8},{5,9},{6,10},{7,11},{8,4},{9,5},... | collective-permute-start | bytes 294920 | tf_op jit(solution)/shard_map/ppermute | solution.py:328
  8.5 21.7 %all-to-all-start = ((bf16[16,8,2304]{2,1,0:T(8,128)(2,1)}), bf16[16,8,2304]{2,1,0:T(8,128)(2,1)S(1)}, u32[]{:S(2)}, u32[]{:S(2)}) async-start(bf16[16,8,2304]{2,1,0:T(8,128)(2,1)} %bitcast.13), calls=%async_computation | async-start | bytes 1179648 | tf_op jit(solution)/shard_map/all_to_all | solution.py:346
  14.7 3.8 %copy-start.1 = (bf16[3,16,1536]{2,1,0:T(8,128)(2,1)S(1)}, bf16[3,16,1536]{2,1,0:T(8,128)(2,1)}, u32[]{:S(2)}) copy-start(bf16[3,16,1536]{2,1,0:T(8,128)(2,1)} %refs_3_.3) | copy-start | bytes 442372
  14.7 5.2 %copy-start = (bf16[3,1,128,1536]{3,2,1,0:T(8,128)(2,1)S(1)}, bf16[3,1,128,1536]{3,2,1,0:T(8,128)(2,1)}, u32[]{:S(2)}) copy-start(bf16[3,1,128,1536]{3,2,1,0:T(8,128)(2,1)} %param.4) | copy-start | bytes 3538948
  16.9 9.8 %collective-permute-start.3 = (bf16[64,1536]{1,0:T(8,128)(2,1)S(1)}, bf16[64,1536]{1,0:T(8,128)(2,1)S(1)}, u32[]{:S(2)}, u32[]{:S(2)}) collective-permute-start(bf16[64,1536]{1,0:T(8,128)(2,1)S(1)} %get-tuple-element.16.refs_0_), channel_id=1, source_target_pairs={{0,2},{1,3},{2,0},{3,1},{4,6},{5,7},{6,4},{7,5},{8,10},{9,11},{10,... | collective-permute-start | bytes 589832 | tf_op jit(solution)/shard_map/ppermute | solution.py:328
  18.5 1.4 %collective-permute-start.5 = (bf16[3,16,1536]{2,1,0:T(8,128)(2,1)S(1)}, bf16[3,16,1536]{2,1,0:T(8,128)(2,1)S(1)}, u32[]{:S(2)}, u32[]{:S(2)}) collective-permute-start(bf16[3,16,1536]{2,1,0:T(8,128)(2,1)S(1)} %copy-done.1), channel_id=1, source_target_pairs={{0,1},{1,0},{2,3},{3,2},{4,5},{5,4},{6,7},{7,6},{8,9},{9,8},{10,11... | collective-permute-start | bytes 442376 | tf_op jit(solution)/shard_map/ppermute | solution.py:328
  20.7 6.9 %copy-start.2 = (bf16[64,1664]{1,0:T(8,128)(2,1)}, bf16[64,1664]{1,0:T(8,128)(2,1)S(1)}, u32[]{:S(2)}) copy-start(bf16[64,1664]{1,0:T(8,128)(2,1)S(1)} %text.2.first_ref) | copy-start | bytes 638980
  27.6 11.5 %collective-permute-start.6 = (bf16[64,3200]{1,0:T(8,128)(2,1)S(1)}, bf16[64,3200]{1,0:T(8,128)(2,1)S(1)}, u32[]{:S(2)}, u32[]{:S(2)}) collective-permute-start(bf16[64,3200]{1,0:T(8,128)(2,1)S(1)} %text.3), channel_id=1, source_target_pairs={{0,2},{1,3},{2,0},{3,1},{4,6},{5,7},{6,4},{7,5},{8,10},{9,11},{10,... | collective-permute-start | bytes 1228808 | tf_op jit(solution)/shard_map/ppermute | solution.py:328
  28.7 10.5 %copy-start.3 = (bf16[64,1664]{1,0:T(8,128)(2,1)S(1)}, bf16[64,1664]{1,0:T(8,128)(2,1)}, u32[]{:S(2)}) copy-start(bf16[64,1664]{1,0:T(8,128)(2,1)} %copy-done.2) | copy-start | bytes 638980
  28.7 15.2 %collective-permute-start.7 = (bf16[64,1536]{1,0:T(8,128)(2,1)S(1)}, bf16[64,1536]{1,0:T(8,128)(2,1)S(1)}, u32[]{:S(2)}, u32[]{:S(2)}) collective-permute-start(bf16[64,1536]{1,0:T(8,128)(2,1)S(1)} %get-tuple-element.15.refs_5_.refs_0_), channel_id=1, source_target_pairs={{0,1},{1,0},{2,3},{3,2},{4,5},{5,4},{6,7},{7,6},{8,9},{9,8},{10,11... | collective-permute-start | bytes 589832 | tf_op jit(solution)/shard_map/ppermute | solution.py:328
  31.4 15.3 %all-to-all-start.1 = ((bf16[16,8,768]{2,1,0:T(8,128)(2,1)}), bf16[16,8,768]{2,1,0:T(8,128)(2,1)S(1)}, u32[]{:S(2)}, u32[]{:S(2)}) async-start(bf16[16,8,768]{2,1,0:T(8,128)(2,1)} %bitcast.3), calls=%async_computation.1 | async-start | bytes 393216 | tf_op jit(solution)/shard_map/all_to_all | solution.py:446
  39.1 5.5 %copy-start.6 = (s32[12]{0:T(128)S(1)}, s32[12]{0:T(128)}, u32[]{:S(2)}) copy-start(s32[12]{0:T(128)} %kind_ref.5) | copy-start | bytes 148
  39.1 5.4 %collective-permute-start.8 = (bf16[64,1536]{1,0:T(8,128)(2,1)S(1)}, bf16[64,1536]{1,0:T(8,128)(2,1)S(1)}, u32[]{:S(2)}, u32[]{:S(2)}) collective-permute-start(bf16[64,1536]{1,0:T(8,128)(2,1)S(1)} %slice.3), channel_id=1, source_target_pairs={{0,1},{1,0},{2,3},{3,2},{4,5},{5,4},{6,7},{7,6},{8,9},{9,8},{10,11... | collective-permute-start | bytes 589832 | tf_op jit(solution)/shard_map/ppermute | solution.py:328
  39.6 9.0 %collective-permute-start.10 = (bf16[16,1664]{1,0:T(8,128)(2,1)S(1)}, bf16[16,1664]{1,0:T(8,128)(2,1)S(1)}, u32[]{:S(2)}, u32[]{:S(2)}) collective-permute-start(bf16[16,1664]{1,0:T(8,128)(2,1)S(1)} %get-tuple-element.24), channel_id=1, source_target_pairs={{0,8},{1,9},{2,10},{3,11},{4,12},{5,13},{6,14},{7,15},{8,0},{9,1},... | collective-permute-start | bytes 159752 | tf_op jit(solution)/shard_map/ppermute | solution.py:328
  41.2 7.3 %collective-permute-start.11 = (bf16[16,1664]{1,0:T(8,128)(2,1)S(1)}, bf16[16,1664]{1,0:T(8,128)(2,1)S(1)}, u32[]{:S(2)}, u32[]{:S(2)}) collective-permute-start(bf16[16,1664]{1,0:T(8,128)(2,1)S(1)} %get-tuple-element.25), channel_id=1, source_target_pairs={{0,12},{1,13},{2,14},{3,15},{4,8},{5,9},{6,10},{7,11},{8,4},{9,5},... | collective-permute-start | bytes 159752 | tf_op jit(solution)/shard_map/ppermute | solution.py:328
  43.4 5.6 %collective-permute-start.9 = (bf16[16,1664]{1,0:T(8,128)(2,1)S(1)}, bf16[16,1664]{1,0:T(8,128)(2,1)S(1)}, u32[]{:S(2)}, u32[]{:S(2)}) collective-permute-start(bf16[16,1664]{1,0:T(8,128)(2,1)S(1)} %get-tuple-element.23), channel_id=1, source_target_pairs={{0,4},{1,5},{2,6},{3,7},{4,0},{5,1},{6,2},{7,3},{8,12},{9,13},{10,... | collective-permute-start | bytes 159752 | tf_op jit(solution)/shard_map/ppermute | solution.py:328
  43.9 0.7 %copy-start.4 = (bf16[64,1536]{1,0:T(8,128)(2,1)}, bf16[64,1536]{1,0:T(8,128)(2,1)S(1)}, u32[]{:S(2)}) copy-start(bf16[64,1536]{1,0:T(8,128)(2,1)S(1)} %collective-permute-done.7.refs_2_) | copy-start | bytes 589828
  44.6 0.9 %copy-start.5 = (bf16[64,1536]{1,0:T(8,128)(2,1)S(1)}, bf16[64,1536]{1,0:T(8,128)(2,1)}, u32[]{:S(2)}) copy-start(bf16[64,1536]{1,0:T(8,128)(2,1)} %copy-done.4) | copy-start | bytes 589828
